TPU v7x, 32 devices: a whole 2x2x4 slice. The times are simulated.
32 devices in a mesh: section: 2 (over core), dp: 16 (over z, y, x).
Axes of the slice: x: 2, y: 2, z: 4, core: 2. Of those that a mesh axis runs over, the one named last changes fastest.
Arguments:
- endpoints: bfloat16 [2, 16384, 768], P('section', 'dp'), may hold values from -6 to 6
- projection: bfloat16 [2, 768, 2304], P('section'), may hold values from -0.21875 to 0.21875
- projection_bias: bfloat16 [2, 2304], P('section'), may hold values from -3 to 3
- output_weight: bfloat16 [2, 768, 768], P('section'), may hold values from -0.875 to 0.875
- output_bias: bfloat16 [2, 768], P('section'), may hold values from -3 to 3
- first_gain: bfloat16 [2, 768], P('section'), may hold values from 0.099609375 to 1.8984375
- first_shift: bfloat16 [2, 768], P('section'), may hold values from -3 to 3
- up_weight: bfloat16 [2, 768, 3072], P('section'), may hold values from -0.21875 to 0.21875
- up_bias: bfloat16 [2, 3072], P('section'), may hold values from -3 to 3
- down_weight: bfloat16 [2, 3072, 768], P('section'), may hold values from -0.109375 to 0.109375
- down_bias: bfloat16 [2, 768], P('section'), may hold values from -3 to 3
- second_gain: bfloat16 [2, 768], P('section'), may hold values from 0.099609375 to 1.8984375
- second_shift: bfloat16 [2, 768], P('section'), may hold values from -3 to 3
- segment_length: int32 [16], P('dp'), may hold values from 128 to 512, as said below
Outputs:
- results: float32 [2, 16384, 768], P('section', 'dp')
- projection_grad: float32 [2, 768, 2304], P('section')
- projection_bias_grad: float32 [2, 2304], P('section')
- output_weight_grad: float32 [2, 768, 768], P('section')
- output_bias_grad: float32 [2, 768], P('section')
- first_gain_grad: float32 [2, 768], P('section')
- first_shift_grad: float32 [2, 768], P('section')
- up_weight_grad: float32 [2, 768, 3072], P('section')
- up_bias_grad: float32 [2, 3072], P('section')
- down_weight_grad: float32 [2, 3072, 768], P('section')
- down_bias_grad: float32 [2, 768], P('section')
- second_gain_grad: float32 [2, 768], P('section')
- second_shift_grad: float32 [2, 768], P('section')
Inputs may be any that keep to these rules, and one draw needn't show every extreme that they name: `segment_length`: each data group's document length is 128, 256 or 512, each of the three taken by some group; documents tile the group's tokens from its first one.
All inputs are finite; a program needn't handle non-finite values.
Results may differ from a plain program's by a relative error of at most 0.014.
Values may be sent and summed in bfloat16 or wider, within the bound.
A program may use at most 256 MiB of HBM per device.

v0:
```python
from functools import partial
import math

import jax
import jax.numpy as jnp
from jax import lax
from jax.sharding import PartitionSpec as P

HEADS = 12
MICRO = 2


EPSILON = 1e-05


def from_behind(value, axis, steps):
    count = lax.axis_size(axis)
    leading, last = (max(0, -steps), min(count, count - steps))
    return lax.ppermute(value, axis, [(source, source + steps) for source in range(leading, last)])


def rows_product(left_mat, right_mat):
    return lax.dot_general(
        left_mat, right_mat, (((0,), (0,)), ((), ())), preferred_element_type=jnp.float32
    )


def back_product(grad_mat, weight_mat):
    return lax.dot_general(
        grad_mat, weight_mat, (((1,), (1,)), ((), ())), preferred_element_type=jnp.float32
    )


def normalize(summed, gain_vec, shift_vec):
    centre = summed - jnp.mean(summed, axis=-1, keepdims=True)
    spread = jnp.mean(centre * centre, axis=-1, keepdims=True)
    scaling = lax.rsqrt(spread + EPSILON)
    unit_rows = centre * scaling
    return (
        unit_rows * gain_vec.astype(jnp.float32) + shift_vec.astype(jnp.float32),
        unit_rows,
        scaling,
    )


def normalize_back(grad_unit, unit_rows, scaling):
    mean_grad = jnp.mean(grad_unit, axis=-1, keepdims=True)
    mean_cross = jnp.mean(grad_unit * unit_rows, axis=-1, keepdims=True)
    return scaling * (grad_unit - mean_grad - unit_rows * mean_cross)


def geometry(block_rows, length):
    places = jnp.arange(block_rows, dtype=jnp.int32)
    angles = 0.5 * math.pi * (places % length).astype(jnp.float32) / length.astype(jnp.float32)
    same_doc = places[:, None] // length == places[None, :] // length
    earlier = places[:, None] >= places[None, :]
    allowed = jnp.where(same_doc & earlier, 1.0, 0.0).astype(jnp.float32)
    return (jnp.cos(angles), jnp.sin(angles), allowed)


def featured(pre_rows, cosine, sine_rows):
    softened = jax.nn.softplus(pre_rows)
    return jnp.concatenate(
        [softened * cosine[:, None, None], softened * sine_rows[:, None, None]], axis=-1
    ).astype(jnp.bfloat16)


def featured_back(grad_rows, pre_rows, cosine, sine_rows):
    half_dim = pre_rows.shape[-1]
    combined = (
        grad_rows[..., :half_dim] * cosine[:, None, None]
        + grad_rows[..., half_dim:] * sine_rows[:, None, None]
    )
    return combined * jax.nn.sigmoid(pre_rows)


def into_blocks(array_in, blocks):
    return array_in.reshape((blocks, array_in.shape[0] // blocks) + array_in.shape[1:])


def mix_block(operands, allowed):
    queries, keys_in, values = operands
    scores = (
        jnp.einsum("qhe,khe->hqk", queries, keys_in, preferred_element_type=jnp.float32) * allowed
    )
    totals = jnp.sum(scores, axis=-1, keepdims=True)
    weights = (scores / totals).astype(jnp.bfloat16)
    return jnp.einsum("hqk,khd->qhd", weights, values, preferred_element_type=jnp.float32)


def mix_block_back(operands, allowed):
    queries, keys_in, values, grad_out = operands
    scores = (
        jnp.einsum("qhe,khe->hqk", queries, keys_in, preferred_element_type=jnp.float32) * allowed
    )
    totals = jnp.sum(scores, axis=-1, keepdims=True)
    probs = scores / totals
    weights = probs.astype(jnp.bfloat16)
    grad_values = jnp.einsum("hqk,qhd->khd", weights, grad_out, preferred_element_type=jnp.float32)
    grad_weights = jnp.einsum("qhd,khd->hqk", grad_out, values, preferred_element_type=jnp.float32)
    inner = jnp.sum(grad_weights * probs, axis=-1, keepdims=True)
    grad_scores = ((grad_weights - inner) / totals * allowed).astype(jnp.bfloat16)
    grad_queries = jnp.einsum(
        "hqk,khe->qhe", grad_scores, keys_in, preferred_element_type=jnp.float32
    )
    grad_keys = jnp.einsum("hqk,qhe->khe", grad_scores, queries, preferred_element_type=jnp.float32)
    return (grad_queries, grad_keys, grad_values)


def layer_forward(layer_in, params, layout):
    (
        proj_w,
        proj_b,
        out_w,
        out_b,
        gain_one,
        shift_one,
        up_w,
        up_b,
        down_w,
        down_b,
        gain_two,
        shift_two,
    ) = params
    cosine, sine_rows, allowed, block_rows = layout
    tokens, model_width = layer_in.shape
    head_dim = model_width // HEADS
    blocks = tokens // block_rows
    projected = jnp.dot(layer_in, proj_w, preferred_element_type=jnp.float32) + proj_b.astype(
        jnp.float32
    )
    query_pre = projected[:, :model_width].reshape(tokens, HEADS, head_dim)
    key_pre = projected[:, model_width : 2 * model_width].reshape(tokens, HEADS, head_dim)
    values = projected[:, 2 * model_width :].astype(jnp.bfloat16).reshape(tokens, HEADS, head_dim)
    queries = featured(query_pre, cosine, sine_rows)
    keys_in = featured(key_pre, cosine, sine_rows)
    mixed = lax.map(
        partial(mix_block, allowed=allowed),
        (into_blocks(queries, blocks), into_blocks(keys_in, blocks), into_blocks(values, blocks)),
    )
    mixed_out = mixed.reshape(tokens, model_width).astype(jnp.bfloat16)
    first_sum = layer_in.astype(jnp.float32) + (
        jnp.dot(mixed_out, out_w, preferred_element_type=jnp.float32) + out_b.astype(jnp.float32)
    )
    normed, unit_one, scale_one = normalize(first_sum, gain_one, shift_one)
    up_in = normed.astype(jnp.bfloat16)
    hidden = jnp.dot(up_in, up_w, preferred_element_type=jnp.float32) + up_b.astype(jnp.float32)
    active = jax.nn.gelu(hidden, approximate=False).astype(jnp.bfloat16)
    second_sum = normed + (
        jnp.dot(active, down_w, preferred_element_type=jnp.float32) + down_b.astype(jnp.float32)
    )
    layer_out, unit_two, scale_two = normalize(second_sum, gain_two, shift_two)
    kept = (
        layer_in,
        query_pre,
        key_pre,
        queries,
        keys_in,
        values,
        mixed_out,
        unit_one,
        scale_one,
        up_in,
        hidden,
        active,
        unit_two,
        scale_two,
    )
    return (layer_out, kept)


def tail_back(grad_out, params, kept):
    (
        proj_w,
        proj_b,
        out_w,
        out_b,
        gain_one,
        shift_one,
        up_w,
        up_b,
        down_w,
        down_b,
        gain_two,
        shift_two,
    ) = params
    (
        layer_in,
        query_pre,
        key_pre,
        queries,
        keys_in,
        values,
        mixed_out,
        unit_one,
        scale_one,
        up_in,
        hidden,
        active,
        unit_two,
        scale_two,
    ) = kept
    gain_two_grad = jnp.sum(grad_out * unit_two, axis=0)
    shift_two_grad = jnp.sum(grad_out, axis=0)
    second_full = normalize_back(grad_out * gain_two.astype(jnp.float32), unit_two, scale_two)
    second_low = second_full.astype(jnp.bfloat16)
    down_w_grad = rows_product(active, second_low)
    down_b_grad = jnp.sum(second_low.astype(jnp.float32), axis=0)
    grad_active = back_product(second_low, down_w)
    gelu_pull = jax.vjp(partial(jax.nn.gelu, approximate=False), hidden)[1]
    hidden_low = gelu_pull(grad_active)[0].astype(jnp.bfloat16)
    up_w_grad = rows_product(up_in, hidden_low)
    up_b_grad = jnp.sum(hidden_low.astype(jnp.float32), axis=0)
    grad_normed = second_full + back_product(hidden_low, up_w)
    gain_one_grad = jnp.sum(grad_normed * unit_one, axis=0)
    shift_one_grad = jnp.sum(grad_normed, axis=0)
    grad_first = normalize_back(grad_normed * gain_one.astype(jnp.float32), unit_one, scale_one)
    return (
        grad_first,
        (
            gain_one_grad,
            shift_one_grad,
            up_w_grad,
            up_b_grad,
            down_w_grad,
            down_b_grad,
            gain_two_grad,
            shift_two_grad,
        ),
    )


def head_back(grad_first, params, kept, layout):
    (
        proj_w,
        proj_b,
        out_w,
        out_b,
        gain_one,
        shift_one,
        up_w,
        up_b,
        down_w,
        down_b,
        gain_two,
        shift_two,
    ) = params
    (
        layer_in,
        query_pre,
        key_pre,
        queries,
        keys_in,
        values,
        mixed_out,
        unit_one,
        scale_one,
        up_in,
        hidden,
        active,
        unit_two,
        scale_two,
    ) = kept
    cosine, sine_rows, allowed, block_rows = layout
    tokens, model_width = layer_in.shape
    head_dim = model_width // HEADS
    blocks = tokens // block_rows
    first_low = grad_first.astype(jnp.bfloat16)
    out_w_grad = rows_product(mixed_out, first_low)
    out_b_grad = jnp.sum(first_low.astype(jnp.float32), axis=0)
    grad_mixed = (
        back_product(first_low, out_w).astype(jnp.bfloat16).reshape(tokens, HEADS, head_dim)
    )
    grad_queries, grad_keys, grad_values = lax.map(
        partial(mix_block_back, allowed=allowed),
        (
            into_blocks(queries, blocks),
            into_blocks(keys_in, blocks),
            into_blocks(values, blocks),
            into_blocks(grad_mixed, blocks),
        ),
    )
    grad_query_pre = featured_back(
        grad_queries.reshape(tokens, HEADS, 2 * head_dim), query_pre, cosine, sine_rows
    )
    grad_key_pre = featured_back(
        grad_keys.reshape(tokens, HEADS, 2 * head_dim), key_pre, cosine, sine_rows
    )
    grad_projected = jnp.concatenate(
        [
            grad_query_pre.reshape(tokens, model_width),
            grad_key_pre.reshape(tokens, model_width),
            grad_values.reshape(tokens, model_width),
        ],
        axis=1,
    ).astype(jnp.bfloat16)
    proj_w_grad = rows_product(layer_in, grad_projected)
    proj_b_grad = jnp.sum(grad_projected.astype(jnp.float32), axis=0)
    grad_in = grad_first + back_product(grad_projected, proj_w)
    return (grad_in, (proj_w_grad, proj_b_grad, out_w_grad, out_b_grad))


def shards(
    endpoints,
    projection,
    projection_bias,
    output_weight,
    output_bias,
    first_gain,
    first_shift,
    up_weight,
    up_bias,
    down_weight,
    down_bias,
    second_gain,
    second_shift,
    segment_length,
):
    section_index = lax.axis_index("section")
    is_first = section_index == 0
    params = (
        projection[0],
        projection_bias[0],
        output_weight[0],
        output_bias[0],
        first_gain[0],
        first_shift[0],
        up_weight[0],
        up_bias[0],
        down_weight[0],
        down_bias[0],
        second_gain[0],
        second_shift[0],
    )
    local_rows = endpoints[0]
    micro_rows = local_rows.shape[0] // MICRO
    model_width = local_rows.shape[1]
    block_rows = min(512, micro_rows)
    cosine, sine_rows, allowed = geometry(block_rows, segment_length[0])
    repeats = micro_rows // block_rows
    layout = (jnp.tile(cosine, repeats), jnp.tile(sine_rows, repeats), allowed, block_rows)
    pieces = [
        local_rows[micro_idx * micro_rows : (micro_idx + 1) * micro_rows]
        for micro_idx in range(MICRO)
    ]
    empty_rows = jnp.zeros((micro_rows, model_width), jnp.bfloat16)
    received = empty_rows
    inputs_kept = []
    states_kept = []
    outputs_kept = []
    for tick_fwd in range(MICRO + 1):
        own_rows = pieces[tick_fwd] if tick_fwd < MICRO else empty_rows
        layer_in = jnp.where(is_first, own_rows, received)
        layer_out, kept = layer_forward(layer_in, params, layout)
        inputs_kept.append(layer_in)
        outputs_kept.append(layer_out)
        states_kept.append(kept)
        if tick_fwd < MICRO:
            received = from_behind(layer_out.astype(jnp.bfloat16), "section", 1)
    head_total = tuple((jnp.zeros(member.shape, jnp.float32) for member in params[:4]))
    tail_total = tuple((jnp.zeros(member.shape, jnp.float32) for member in params[4:]))
    zero_grad = jnp.zeros((micro_rows, model_width), jnp.float32)
    came_back = zero_grad
    input_grads = [zero_grad for micro_idx in range(MICRO)]
    for back_step in range(MICRO + 1):
        tick_fwd = MICRO - back_step
        own_index = MICRO - 1 - back_step
        own_grad = pieces[own_index].astype(jnp.float32) if own_index >= 0 else zero_grad
        grad_out = jnp.where(is_first, came_back, own_grad)
        kept = states_kept[tick_fwd]
        grad_first, tail_terms = tail_back(grad_out, params, kept)
        tail_total = tuple(jax.tree.map(jnp.add, tail_total, tail_terms))
        grad_in, head_terms = head_back(grad_first, params, kept, layout)
        head_total = tuple(jax.tree.map(jnp.add, head_total, head_terms))
        if tick_fwd < MICRO:
            input_grads[tick_fwd] = grad_in
        if back_step < MICRO:
            came_back = from_behind(grad_in.astype(jnp.bfloat16), "section", -1).astype(jnp.float32)
    summed_all = tuple(
        lax.psum(
            (
                head_total[0],
                head_total[1],
                head_total[2],
                head_total[3],
                tail_total[0],
                tail_total[1],
                tail_total[2],
                tail_total[3],
                tail_total[4],
                tail_total[5],
                tail_total[6],
                tail_total[7],
            ),
            "dp",
        )
    )
    answers = jnp.where(
        is_first, jnp.concatenate(input_grads, axis=0), jnp.concatenate(outputs_kept[1:], axis=0)
    )[None]
    return (answers,) + tuple((member[None] for member in summed_all))


def solution(mesh):
    in_specs = (
        P("section", "dp", None),
        P("section", None, None),
        P("section", None),
        P("section", None, None),
        P("section", None),
        P("section", None),
        P("section", None),
        P("section", None, None),
        P("section", None),
        P("section", None, None),
        P("section", None),
        P("section", None),
        P("section", None),
        P("dp"),
    )
    out_specs = (
        P("section", "dp", None),
        P("section", None, None),
        P("section", None),
        P("section", None, None),
        P("section", None),
        P("section", None),
        P("section", None),
        P("section", None, None),
        P("section", None),
        P("section", None, None),
        P("section", None),
        P("section", None),
        P("section", None),
    )
    return jax.shard_map(shards, mesh=mesh, in_specs=in_specs, out_specs=out_specs, check_vma=False)
```

profile of v0, /device:TPU:0, one launch (start us, length us, event | category | flops | bytes accessed | tf_op | source)
XLA Modules:
  0.0 1209.4 jit_solution(7212822036069908308)
XLA Ops:
  41.8 18.3 %multiply_convert_fusion.5 = (bf16[512,3072]{1,0:T(8,128)(2,1)S(1)}, f32[512,3072]{1,0:T(8,128)}, f32[512,3072]{1,0:T(8,128)}) fusion(f32[3072]{0:T(1024)S(1)} %bitcast.322, bf16[1,768,3072]{2,1,0:T(8,128)(2,1)S(1)} %bitcast.339, f32[512,768]{1,0:T(8,128)S(1)} %get-tuple-element.238, f32[768]{0:T(1024)S(1)} %get-tuple-element.269, ...), kind=kOutput, calls=%fused_computation.59 | convolution fusion | flops 2521694208 | bytes 22042624 | tf_op jit(solution)/shard_map/dot_general | solution.py:147
  94.7 18.3 %multiply_convert_fusion.4 = (bf16[512,3072]{1,0:T(8,128)(2,1)S(1)}, f32[512,3072]{1,0:T(8,128)}, f32[512,3072]{1,0:T(8,128)}) fusion(f32[3072]{0:T(1024)S(1)} %bitcast.323, bf16[1,768,3072]{2,1,0:T(8,128)(2,1)S(1)} %bitcast.341, f32[512,768]{1,0:T(8,128)S(1)} %get-tuple-element.245, f32[512]{0:T(512)S(1)} %add_rsqrt_fusion.3, ...), kind=kOutput, calls=%fused_computation.46 | convolution fusion | flops 2521694208 | bytes 22042624 | tf_op jit(solution)/shard_map/dot_general | solution.py:147
  148.5 18.3 %multiply_convert_fusion.3 = (bf16[512,3072]{1,0:T(8,128)(2,1)S(1)}, f32[512,3072]{1,0:T(8,128)}, f32[512,3072]{1,0:T(8,128)}) fusion(f32[3072]{0:T(1024)S(1)} %bitcast.324, bf16[1,768,3072]{2,1,0:T(8,128)(2,1)S(1)} %bitcast.343, f32[512,768]{1,0:T(8,128)S(1)} %get-tuple-element.252, f32[512]{0:T(512)S(1)} %add_rsqrt_fusion.1, ...), kind=kOutput, calls=%fused_computation.33 | convolution fusion | flops 2521694208 | bytes 22042624 | tf_op jit(solution)/shard_map/dot_general | solution.py:147
  173.6 9.8 convert_reduce_fusion.2
  195.5 8.0 fusion.142
  203.5 12.7 %convolution_bitcast_fusion.5 = f32[512,12,128]{0,2,1:T(8,128)} fusion(bf16[512,12,64]{0,2,1:T(8,128)(2,1)} %copy-done.53, bf16[512,12,64]{0,2,1:T(8,128)(2,1)} %copy-done.52, f32[12,512]{1,0:T(8,128)} %copy-done.98, f32[512,512]{0,1:T(8,128)} %fusion.166, bf16[512,12,64]{0,2,1:T(8,128)(2,1)} %bitcast.310, bf16[512,12,64]{0,2,1:T(8,128)(2,1)} %bitcast.303, ...), kind=kOutput, calls=%fused_computation.142 | convolution fusion | flops 1635785216 | bytes 19947520 | tf_op jit(solution)/shard_map/while/body/eval_jaxpr/hqk,khe->qhe/dot_general | solution.py:103
  216.1 13.8 %convolution_bitcast_fusion.4 = f32[512,12,128]{0,2,1:T(8,128)} fusion(bf16[512,12,64]{0,2,1:T(8,128)(2,1)} %copy-done.50, bf16[512,12,64]{0,2,1:T(8,128)(2,1)} %copy-done.51, f32[12,512]{1,0:T(8,128)} %copy-done.98, f32[512,512]{0,1:T(8,128)} %fusion.166, bf16[512,12,64]{0,2,1:T(8,128)(2,1)} %bitcast.311, bf16[512,12,64]{0,2,1:T(8,128)(2,1)} %bitcast.304, ...), kind=kOutput, calls=%fused_computation.141 | convolution fusion | flops 1635785216 | bytes 19947520 | tf_op jit(solution)/shard_map/while/body/eval_jaxpr/hqk,qhe->khe/dot_general | solution.py:106
  230.0 8.7 fusion.211
  254.7 9.9 convert_reduce_fusion.1
  276.6 8.0 fusion.136
  284.5 12.7 %convolution_bitcast_fusion.3 = f32[512,12,128]{0,2,1:T(8,128)} fusion(bf16[512,12,64]{0,2,1:T(8,128)(2,1)} %copy-done.49, bf16[512,12,64]{0,2,1:T(8,128)(2,1)} %copy-done.48, f32[12,512]{1,0:T(8,128)} %copy-done.97, f32[512,512]{0,1:T(8,128)} %fusion.166, bf16[512,12,64]{0,2,1:T(8,128)(2,1)} %bitcast.313, bf16[512,12,64]{0,2,1:T(8,128)(2,1)} %bitcast.300, ...), kind=kOutput, calls=%fused_computation.140 | convolution fusion | flops 1635785216 | bytes 19947520 | tf_op jit(solution)/shard_map/while/body/eval_jaxpr/hqk,khe->qhe/dot_general | solution.py:103
  297.3 13.4 %convolution_bitcast_fusion.2 = f32[512,12,128]{0,2,1:T(8,128)} fusion(bf16[512,12,64]{0,2,1:T(8,128)(2,1)} %copy-done.46, bf16[512,12,64]{0,2,1:T(8,128)(2,1)} %copy-done.47, f32[12,512]{1,0:T(8,128)} %copy-done.97, f32[512,512]{0,1:T(8,128)} %fusion.166, bf16[512,12,64]{0,2,1:T(8,128)(2,1)} %bitcast.314, bf16[512,12,64]{0,2,1:T(8,128)(2,1)} %bitcast.301, ...), kind=kOutput, calls=%fused_computation.139 | convolution fusion | flops 1635785216 | bytes 19947520 | tf_op jit(solution)/shard_map/while/body/eval_jaxpr/hqk,qhe->khe/dot_general | solution.py:106
  341.4 8.8 convert_reduce_fusion
  350.2 7.2 multiply_reduce_fusion.9
  363.7 8.0 fusion.130
  371.7 12.5 %convolution_bitcast_fusion.1 = f32[512,12,128]{0,2,1:T(8,128)} fusion(bf16[512,12,64]{0,2,1:T(8,128)(2,1)} %copy-done.45, bf16[512,12,64]{0,2,1:T(8,128)(2,1)} %copy-done.44, f32[12,512]{1,0:T(8,128)} %copy-done.96, f32[512,512]{0,1:T(8,128)} %fusion.166, bf16[512,12,64]{0,2,1:T(8,128)(2,1)} %bitcast.307, bf16[512,12,64]{0,2,1:T(8,128)(2,1)} %bitcast.297, ...), kind=kOutput, calls=%fused_computation.138 | convolution fusion | flops 1635785216 | bytes 19947520 | tf_op jit(solution)/shard_map/while/body/eval_jaxpr/hqk,khe->qhe/dot_general | solution.py:103
  384.1 13.2 %convolution_bitcast_fusion = f32[512,12,128]{0,2,1:T(8,128)} fusion(bf16[512,12,64]{0,2,1:T(8,128)(2,1)} %copy-done.42, bf16[512,12,64]{0,2,1:T(8,128)(2,1)} %copy-done.43, f32[12,512]{1,0:T(8,128)} %copy-done.96, f32[512,512]{0,1:T(8,128)} %fusion.166, bf16[512,12,64]{0,2,1:T(8,128)(2,1)} %bitcast.308, bf16[512,12,64]{0,2,1:T(8,128)(2,1)} %bitcast.298, ...), kind=kOutput, calls=%fused_computation.137 | convolution fusion | flops 1635785216 | bytes 19947520 | tf_op jit(solution)/shard_map/while/body/eval_jaxpr/hqk,qhe->khe/dot_general | solution.py:106
  406.3 12.0 add_bitcast_fusion.1
  418.4 12.3 %add_bitcast_fusion = f32[1,3072,768]{2,1,0:T(8,128)} fusion(f32[3072,768]{1,0:T(8,128)S(1)} %bitcast.252, f32[3072,768]{1,0:T(8,128)} %fusion.205, bf16[512,3072]{1,0:T(8,128)(2,1)} %copy-done.18, f32[512,768]{1,0:T(8,128)} %copy-done.26), kind=kOutput, calls=%fused_computation.21 | convolution fusion | flops 2421030912 | bytes 33030144 | tf_op jit(solution)/shard_map/dot_general | solution.py:23
  434.6 7.2 add_bitcast_fusion.2
  450.3 84.3 %all-reduce = (f32[1,2304]{1,0:T(1,128)}, f32[1,768]{1,0:T(1,128)}, f32[1,768]{1,0:T(1,128)}, f32[1,768]{1,0:T(1,128)}, f32[1,3072]{1,0:T(1,128)}, /*index=5*/f3...) all-reduce(f32[1,2304]{1,0:T(1,128)} %broadcast_in_dim.99, ...), channel_id=1, replica_groups=mesh['section'=2,'dp'=16] {'dp'}, use_global_device_ids=true, to_apply=%region_34.35 | all-reduce | flops 9984 | bytes 79872 | tf_op jit(solution)/shard_map/psum | solution.py:380
  541.0 640.0 %all-reduce.4.cloned.1.call-done = (f32[1,768,2304]{2,1,0:T(8,128)}, f32[1,768,768]{2,1,0:T(8,128)}, f32[1,768,3072]{2,1,0:T(8,128)}, f32[1,3072,768]{2,1,0:T(8,128)}) async-done(((f32[1,768,2304]{2,1,0:T(8,128)}, f32[1,768,768]{2,1,0:T(8,128)}, f32[1,768,3072]{2,1,0:T(8,128)}, f32[1,3072,768]{2,1,0:T(8,128)}), (f32[1,768,2304]{2,1,0:T(8,128)}, f32[1,768,768]{2,1,0:T(8,128)}, f32[1,768,3072]{2,1,0:T(8,128)}, ...) | async-done | bytes 28311568 | tf_op jit(solution)/shard_map/psum | solution.py:380
  1181.0 6.6 copy.230
  1189.0 9.3 copy.232
  (541 shorter events, 218.3 us)
Async XLA Ops:
  7.2 1173.8 %all-reduce.4.cloned.1.call-start = ((), (), s32[]{:S(2)}) async-start(), calls=%async_computation | async-start | bytes 56623104 | tf_op jit(solution)/shard_map/psum | solution.py:380
  40.4 19.7 %slice-start.8 = ((s8[4718592]{0:T(1024)(128)(4,1)}), s8[4194304]{0:T(1024)(128)(4,1)S(1)}, s32[]{:S(2)}) async-start(s8[4718592]{0:T(1024)(128)(4,1)} %bitcast.328), calls=%async_computation.9 | async-start | bytes 8388608
  41.3 18.8 %copy-start.8 = (f32[512,768]{1,0:T(8,128)}, f32[512,768]{1,0:T(8,128)S(1)}, u32[]{:S(2)}) copy-start(f32[512,768]{1,0:T(8,128)S(1)} %get-tuple-element.238) | copy-start | bytes 4718596
  41.3 18.7 %copy-start.99 = (f32[512]{0:T(512)}, f32[512]{0:T(512)S(1)}, u32[]{:S(2)}) copy-start(f32[512]{0:T(512)S(1)} %broadcast_multiply_fusion.17) | copy-start | bytes 6148
  41.7 18.4 %copy-start.103 = (f32[512]{0:T(512)}, f32[512]{0:T(512)S(1)}, u32[]{:S(2)}) copy-start(f32[512]{0:T(512)S(1)} %add_rsqrt_fusion.5) | copy-start | bytes 6148
  41.7 18.4 %copy-start.111 = (f32[768]{0:T(1024)}, f32[768]{0:T(1024)S(1)}, u32[]{:S(2)}) copy-start(f32[768]{0:T(1024)S(1)} %get-tuple-element.269) | copy-start | bytes 9220
  63.7 4.3 collective-permute-start
  93.3 19.7 %slice-start.10 = ((s8[4718592]{0:T(1024)(128)(4,1)}), s8[4194304]{0:T(1024)(128)(4,1)S(1)}, s32[]{:S(2)}) async-start(s8[4718592]{0:T(1024)(128)(4,1)} %bitcast.330), calls=%async_computation.11 | async-start | bytes 8388608
  94.3 18.8 %copy-start.33 = (f32[512,768]{1,0:T(8,128)}, f32[512,768]{1,0:T(8,128)S(1)}, u32[]{:S(2)}) copy-start(f32[512,768]{1,0:T(8,128)S(1)} %get-tuple-element.245) | copy-start | bytes 4718596
  94.3 18.7 %copy-start.106 = (f32[512]{0:T(512)}, f32[512]{0:T(512)S(1)}, u32[]{:S(2)}) copy-start(f32[512]{0:T(512)S(1)} %broadcast_multiply_fusion.15) | copy-start | bytes 6148
  94.7 18.4 %copy-start.141 = (f32[512]{0:T(512)}, f32[512]{0:T(512)S(1)}, u32[]{:S(2)}) copy-start(f32[512]{0:T(512)S(1)} %add_rsqrt_fusion.3) | copy-start | bytes 6148
  94.7 18.4 %copy-start.147 = (f32[768]{0:T(1024)S(1)}, f32[768]{0:T(1024)}, u32[]{:S(2)}) copy-start(f32[768]{0:T(1024)} %convert_reduce_fusion.15) | copy-start | bytes 9220
  94.7 18.4 %slice-start.11 = ((s8[4718592]{0:T(1024)(128)(4,1)}), s8[524288]{0:T(1024)(128)(4,1)S(1)}, s32[]{:S(2)}) async-start(s8[4718592]{0:T(1024)(128)(4,1)} %bitcast.330), calls=%async_computation.12 | async-start | bytes 1048576
  117.8 4.2 collective-permute-start.1
  147.1 19.7 %slice-start.12 = ((s8[4718592]{0:T(1024)(128)(4,1)}), s8[4194304]{0:T(1024)(128)(4,1)S(1)}, s32[]{:S(2)}) async-start(s8[4718592]{0:T(1024)(128)(4,1)} %bitcast.332), calls=%async_computation.13 | async-start | bytes 8388608
  148.0 41.2 %copy-start.36 = (f32[512,768]{1,0:T(8,128)}, f32[512,768]{1,0:T(8,128)S(1)}, u32[]{:S(2)}) copy-start(f32[512,768]{1,0:T(8,128)S(1)} %get-tuple-element.252) | copy-start | bytes 4718596
  148.1 41.1 %copy-start.109 = (f32[512]{0:T(512)}, f32[512]{0:T(512)S(1)}, u32[]{:S(2)}) copy-start(f32[512]{0:T(512)S(1)} %broadcast_multiply_fusion.13) | copy-start | bytes 6148
  148.4 40.8 %copy-start.144 = (f32[512]{0:T(512)}, f32[512]{0:T(512)S(1)}, u32[]{:S(2)}) copy-start(f32[512]{0:T(512)S(1)} %add_rsqrt_fusion.1) | copy-start | bytes 6148
  148.5 18.4 %copy-start.148 = (f32[768]{0:T(1024)S(1)}, f32[768]{0:T(1024)}, u32[]{:S(2)}) copy-start(f32[768]{0:T(1024)} %convert_reduce_fusion.15) | copy-start | bytes 9220
  148.5 18.4 %slice-start.13 = ((s8[4718592]{0:T(1024)(128)(4,1)}), s8[524288]{0:T(1024)(128)(4,1)S(1)}, s32[]{:S(2)}) async-start(s8[4718592]{0:T(1024)(128)(4,1)} %bitcast.332), calls=%async_computation.14 | async-start | bytes 1048576
  242.4 9.5 collective-permute-start.2
  329.3 9.5 collective-permute-start.3
  406.3 24.4 %copy-start.60 = (bf16[512,12,64]{0,2,1:T(8,128)(2,1)}, bf16[512,12,64]{0,2,1:T(8,128)(2,1)S(1)}, u32[]{:S(2)}) copy-start(bf16[512,12,64]{0,2,1:T(8,128)(2,1)S(1)} %get-tuple-element.229) | copy-start | bytes 2359300
  406.3 28.2 %slice-start.3 = ((s8[7077888]{0:T(1024)(128)(4,1)}), s8[2883584]{0:T(1024)(128)(4,1)S(1)}, s32[]{:S(2)}) async-start(s8[7077888]{0:T(1024)(128)(4,1)} %bitcast.265), calls=%async_computation.4 | async-start | bytes 5767168
  (177 other events, 948.4 us)
Sparse Core Ops, SparseCore 0:
  441.9 739.0 all-reduce.3
where the time goes:
time: 1220 us; the launch traced here: 1210 us
  waiting for transfers between devices  643 us (53%)
  matrix products  325 us (27%)
  blocking collectives  84.3 us (7%)
  local copies, waits for them, and re-layouts  83.5 us (7%)
  other arithmetic  47.7 us (4%)
  between operations  17.8 us (1%)
    psum x1, waiting for transfers between devices, shards(): lax.psum((head_total[0], head_total[1], head_total[2], head_total[3], tai...  640 us
    psum x1, blocking collectives, shards(): lax.psum((head_total[0], head_total[1], head_total[2], head_total[3], tai...  84.3 us
    dot_general x12, matrix products, rows_product(): lax.dot_general(left_mat, right_mat, (((0,), (0,)), ((), ())), preferred_...  75.3 us
    dot_general x12, matrix products, back_product(): lax.dot_general(grad_mat, weight_mat, (((1,), (1,)), ((), ())), preferred...  61.9 us
    dot_general x3, matrix products, layer_forward(): jnp.dot(up_in, up_w, preferred_element_type=jnp.float32)  54.9 us
    dot_general x3, matrix products, mix_block_back(): jnp.einsum('hqk,qhe->khe', grad_scores, queries, preferred_element_type=j...  40.5 us
    unnamed x396, local copies, waits for them, and re-layouts  39.3 us
    dot_general x3, matrix products, mix_block_back(): jnp.einsum('hqk,khe->qhe', grad_scores, keys_in, preferred_element_type=j...  37.9 us
  transfers between devices with their start and end apart: 5, of which 3 were waited for; matrix products, arithmetic and copies ran while one was open for 2% of the time, Pallas kernels for 0%

commit v1 on v0

--- a/solution.py
+++ b/solution.py
@@ -4,6 +4,8 @@
 import jax
 import jax.numpy as jnp
 from jax import lax
+from jax.experimental import pallas as pl
+from jax.experimental.pallas import tpu as pltpu
 from jax.sharding import PartitionSpec as P
 
 HEADS = 12
@@ -11,6 +13,7 @@
 
 
 EPSILON = 1e-05
+MESH = pl.DeviceIdType.MESH
 
 
 def from_behind(value, axis, steps):
@@ -204,12 +207,10 @@
     shift_two_grad = jnp.sum(grad_out, axis=0)
     second_full = normalize_back(grad_out * gain_two.astype(jnp.float32), unit_two, scale_two)
     second_low = second_full.astype(jnp.bfloat16)
-    down_w_grad = rows_product(active, second_low)
     down_b_grad = jnp.sum(second_low.astype(jnp.float32), axis=0)
     grad_active = back_product(second_low, down_w)
     gelu_pull = jax.vjp(partial(jax.nn.gelu, approximate=False), hidden)[1]
     hidden_low = gelu_pull(grad_active)[0].astype(jnp.bfloat16)
-    up_w_grad = rows_product(up_in, hidden_low)
     up_b_grad = jnp.sum(hidden_low.astype(jnp.float32), axis=0)
     grad_normed = second_full + back_product(hidden_low, up_w)
     gain_one_grad = jnp.sum(grad_normed * unit_one, axis=0)
@@ -220,13 +221,12 @@
         (
             gain_one_grad,
             shift_one_grad,
-            up_w_grad,
             up_b_grad,
-            down_w_grad,
             down_b_grad,
             gain_two_grad,
             shift_two_grad,
         ),
+        (hidden_low, second_low),
     )
 
 
@@ -266,7 +266,6 @@
     head_dim = model_width // HEADS
     blocks = tokens // block_rows
     first_low = grad_first.astype(jnp.bfloat16)
-    out_w_grad = rows_product(mixed_out, first_low)
     out_b_grad = jnp.sum(first_low.astype(jnp.float32), axis=0)
     grad_mixed = (
         back_product(first_low, out_w).astype(jnp.bfloat16).reshape(tokens, HEADS, head_dim)
@@ -294,10 +293,294 @@
         ],
         axis=1,
     ).astype(jnp.bfloat16)
-    proj_w_grad = rows_product(layer_in, grad_projected)
     proj_b_grad = jnp.sum(grad_projected.astype(jnp.float32), axis=0)
     grad_in = grad_first + back_product(grad_projected, proj_w)
-    return (grad_in, (proj_w_grad, proj_b_grad, out_w_grad, out_b_grad))
+    return (grad_in, (proj_b_grad, out_b_grad), (first_low, grad_projected))
+
+
+def factor_dims(count):
+    bits = count.bit_length() - 1
+    return (1 << (bits // 3), 1 << ((bits + 1) // 3), 1 << ((bits + 2) // 3))
+
+
+ORDERS = {"a": (0, 1, 2), "b": (1, 2, 0), "c": (2, 0, 1)}
+PATTERN = "abacabc"
+LAG = 3
+UNIT = 256
+
+
+def stage_list(order, dims, rows):
+    stages, size, landing = [], rows, 0
+    for level, ax in enumerate(order):
+        part = size // dims[ax]
+        for step in range(1, dims[ax]):
+            stages.append(("reduce", level, ax, step, part, landing))
+            landing += part if dims[ax] == 2 else 2 * part
+        size = part
+    for level in reversed(range(3)):
+        ax = order[level]
+        for step in range(1, dims[ax]):
+            stages.append(("gather", level, ax, step, size, 0))
+        size *= dims[ax]
+    return stages, landing
+
+
+def unit_blocks(unit):
+    up, out, proj = unit - 36, unit - 72, unit - 81
+    left = jnp.where(
+        unit < 36,
+        unit // 3,
+        jnp.where(unit < 72, 12 + up // 12, jnp.where(unit < 81, 15 + out // 3, 18 + proj // 9)),
+    )
+    right = jnp.where(
+        unit < 36,
+        unit % 3,
+        jnp.where(unit < 72, 3 + up % 12, jnp.where(unit < 81, 15 + out % 3, 18 + proj % 9)),
+    )
+    return left, right
+
+
+def reduce_kernel(dims, pieces, rows, units, left_hbm, right_hbm, vec_hbm, sum_hbm,
+                  acc, landing, full, vec_buf, left_buf, right_buf, load_sem, vec_sem, out_sem,
+                  send_sem, recv_sem):
+    here = lax.axis_index("dp")
+    strides = (1, dims[0], dims[0] * dims[1])
+    place = [(here // strides[ax]) % dims[ax] for ax in range(3)]
+    slots = send_sem.shape[0]
+    ring = left_buf.shape[0]
+    per_piece = rows // UNIT
+    land_rows = landing.shape[0] // slots
+    plans = {name: stage_list(order, dims, rows)[0] for name, order in ORDERS.items()}
+    n_stages = len(plans["a"])
+    n_shards = dims[0] * dims[1] * dims[2]
+    period = len(PATTERN)
+    rounds = -(-pieces // period)
+    all_rounds = -(-(pieces + n_stages * LAG) // period)
+
+    bases = {}
+    for name, order in ORDERS.items():
+        base, size, found = 0, rows, []
+        for ax in order:
+            found.append(base)
+            size = size // dims[ax]
+            base = base + place[ax] * size
+        bases[name] = found
+
+    def neighbour(ax, sign):
+        return {"dp": here + sign * strides[ax]}
+
+    barrier = pltpu.get_barrier_semaphore()
+    for ax in range(3):
+        for sign, can in ((1, place[ax] < dims[ax] - 1), (-1, place[ax] > 0)):
+            @pl.when(can)
+            def _():
+                pl.semaphore_signal(
+                    barrier, inc=1, device_id=neighbour(ax, sign), device_id_type=MESH
+                )
+    around = sum(
+        (place[ax] < dims[ax] - 1).astype(jnp.int32) + (place[ax] > 0).astype(jnp.int32)
+        for ax in range(3)
+    )
+    pl.semaphore_wait(barrier, around)
+
+    def loads(unit):
+        slot = unit % ring
+        left, right = unit_blocks(unit)
+        return (
+            pltpu.make_async_copy(left_hbm.at[left], left_buf.at[slot], load_sem.at[slot, 0]),
+            pltpu.make_async_copy(right_hbm.at[right], right_buf.at[slot], load_sem.at[slot, 1]),
+        )
+
+    vec_copy = pltpu.make_async_copy(vec_hbm, vec_buf, vec_sem)
+    vec_copy.start()
+    for unit in range(ring):
+        for copy in loads(jnp.int32(unit)):
+            copy.start()
+    vec_copy.wait()
+
+    def form(piece, sub):
+        unit = piece * per_piece + sub
+        start = (piece % slots) * rows + sub * UNIT
+
+        @pl.when(unit < units)
+        def _():
+            for copy in loads(unit):
+                copy.wait()
+            slot = unit % ring
+            acc[pl.ds(pl.multiple_of(start, UNIT), UNIT), :] = lax.dot_general(
+                left_buf[slot], right_buf[slot], (((0,), (0,)), ((), ())),
+                preferred_element_type=jnp.float32,
+            ).astype(jnp.bfloat16)
+
+            @pl.when(unit + ring < units)
+            def _():
+                for copy in loads(unit + ring):
+                    copy.start()
+
+        @pl.when(unit >= units)
+        def _():
+            acc[pl.ds(pl.multiple_of(start, UNIT), UNIT), :] = vec_buf[
+                sub * UNIT : (sub + 1) * UNIT
+            ]
+
+    def copies(name, stage, piece):
+        kind, level, ax, step, part, land = plans[name][stage]
+        count, spot = dims[ax], place[ax]
+        slot = piece % slots
+        held, index = (acc, slot) if kind == "reduce" else (full, piece)
+        start = index * rows + bases[name][level]
+        land_start = pl.multiple_of(slot * land_rows + land, 16)
+
+        def chunk(q):
+            return held.at[pl.ds(pl.multiple_of(start + q * part, 16), part)]
+
+        def landed(way):
+            return landing.at[pl.ds(pl.multiple_of(land_start + way * part, 16), part)]
+
+        def remote(src, dst, way, sign):
+            return lambda: pltpu.make_async_remote_copy(
+                src_ref=src, dst_ref=dst, send_sem=send_sem.at[slot, stage, way],
+                recv_sem=recv_sem.at[slot, stage, way], device_id=neighbour(ax, sign),
+                device_id_type=MESH,
+            )
+
+        sends, receives = [], []
+        if count == 2:
+            sign = 1 - 2 * spot
+            mine, other = spot, 1 - spot
+            if kind == "reduce":
+                sends.append((None, remote(chunk(other), landed(0), 0, sign)))
+                receives.append((None, remote(chunk(mine), landed(0), 0, sign), mine, landed(0)))
+            else:
+                sends.append((None, remote(chunk(mine), chunk(mine), 0, sign)))
+                receives.append((None, remote(chunk(other), chunk(other), 0, sign), other, None))
+            return sends, receives, chunk
+        back = count - 1 - spot
+        if kind == "reduce":
+            for way, sign, can, q in (
+                (0, 1, spot < step, spot + count - step),
+                (1, -1, back < step, step - 1 - back),
+            ):
+                q = jnp.clip(q, 0, count - 1)
+                sends.append((can, remote(chunk(q), landed(way), way, sign)))
+            for way, sign, can, q in (
+                (0, 1, jnp.logical_and(spot >= 1, spot - 1 < step), spot - 1 + count - step),
+                (1, -1, jnp.logical_and(back >= 1, back - 1 < step), step - back),
+            ):
+                q = jnp.clip(q, 0, count - 1)
+                receives.append((can, remote(chunk(q), landed(way), way, sign), q, landed(way)))
+        else:
+            for way, sign, can, q in (
+                (0, 1, jnp.logical_and(back >= 1, spot >= step - 1), spot - step + 1),
+                (1, -1, jnp.logical_and(spot >= 1, back >= step - 1), spot + step - 1),
+            ):
+                q = jnp.clip(q, 0, count - 1)
+                sends.append((can, remote(chunk(q), chunk(q), way, sign)))
+            for way, sign, can, q in (
+                (0, 1, spot >= step, spot - step),
+                (1, -1, back >= step, spot + step),
+            ):
+                q = jnp.clip(q, 0, count - 1)
+                receives.append((can, remote(chunk(q), chunk(q), way, sign), q, None))
+        return sends, receives, chunk
+
+    def guarded(can, action):
+        if can is None:
+            action()
+        else:
+            pl.when(can)(action)
+
+    def out_copy(piece):
+        block = pl.ds(pl.multiple_of(piece * rows, rows), rows)
+        return pltpu.make_async_copy(full.at[block], sum_hbm.at[block], out_sem.at[piece])
+
+    def work(name, stage, piece):
+        if stage > 0:
+            sends, receives, chunk = copies(name, stage - 1, piece)
+            for can, copy, q, landed in receives:
+                def finish():
+                    copy().wait_recv()
+                    if landed is not None:
+                        block = chunk(q)
+                        block[...] = block[...] + landed[...]
+                guarded(can, finish)
+        if stage == n_stages // 2:
+            mine = bases[name][2] + place[ORDERS[name][2]] * (rows // n_shards)
+            kept = acc[pl.ds(pl.multiple_of((piece % slots) * rows + mine, 16), rows // n_shards), :]
+            full[pl.ds(pl.multiple_of(piece * rows + mine, 16), rows // n_shards), :] = kept
+        if stage < n_stages:
+            for can, copy in copies(name, stage, piece)[0]:
+                guarded(can, lambda: copy().start())
+        else:
+            out_copy(piece).start()
+        if stage > 0:
+            for can, copy in sends:
+                guarded(can, lambda: copy().wait_send())
+
+    def one_round(turn, carry):
+        for spot_in in range(period):
+            tick = turn * period + spot_in
+            for stage in reversed(range(1, n_stages + 1)):
+                piece = tick - stage * LAG
+                name = PATTERN[(spot_in - stage * LAG) % period]
+
+                @pl.when(jnp.logical_and(piece >= 0, piece < pieces))
+                def _():
+                    work(name, stage, jnp.clip(piece, 0, pieces - 1))
+
+            @pl.when(tick < pieces)
+            def _():
+                piece = jnp.minimum(tick, pieces - 1)
+                for sub in range(per_piece):
+                    form(piece, sub)
+                work(PATTERN[spot_in], 0, piece)
+        return carry
+
+    lax.fori_loop(0, all_rounds, one_round, 0)
+
+    def drain(piece, carry):
+        out_copy(piece).wait()
+        return carry
+
+    lax.fori_loop(0, pieces, drain, 0)
+
+
+def reduce_gradients(left, right, vec, dp_size):
+    dims = factor_dims(dp_size)
+    rows = 16 * dp_size
+    units = 108
+    pieces = (units * UNIT + vec.shape[0]) // rows
+    slots = 4 * len(PATTERN)
+    ring = 4 if dp_size <= 16 else 2
+    land = max(stage_list(order, dims, rows)[1] for order in ORDERS.values())
+    n_stages = 2 * (sum(dims) - 3)
+    tokens = left.shape[1]
+    total = pieces * rows
+    return pl.pallas_call(
+        partial(reduce_kernel, dims, pieces, rows, units),
+        out_shape=jax.ShapeDtypeStruct((total, UNIT), jnp.bfloat16),
+        in_specs=[pl.BlockSpec(memory_space=pl.ANY)] * 3,
+        out_specs=pl.BlockSpec(memory_space=pl.ANY),
+        scratch_shapes=[
+            pltpu.VMEM((slots * rows, UNIT), jnp.bfloat16),
+            pltpu.VMEM((slots * land, UNIT), jnp.bfloat16),
+            pltpu.VMEM((total, UNIT), jnp.bfloat16),
+            pltpu.VMEM((rows, UNIT), jnp.bfloat16),
+            pltpu.VMEM((ring, tokens, UNIT), jnp.bfloat16),
+            pltpu.VMEM((ring, tokens, UNIT), jnp.bfloat16),
+            pltpu.SemaphoreType.DMA((ring, 2)),
+            pltpu.SemaphoreType.DMA,
+            pltpu.SemaphoreType.DMA((pieces,)),
+            pltpu.SemaphoreType.DMA((slots, n_stages, 2)),
+            pltpu.SemaphoreType.DMA((slots, n_stages, 2)),
+        ],
+        compiler_params=pltpu.CompilerParams(
+            collective_id=1, has_side_effects=True, vmem_limit_bytes=62 << 20
+        ),
+        cost_estimate=pl.CostEstimate(
+            flops=2 * units * UNIT * UNIT * tokens, bytes_accessed=120 << 20, transcendentals=0
+        ),
+    )(left, right, vec)
 
 
 def shards(
@@ -357,43 +640,67 @@
         states_kept.append(kept)
         if tick_fwd < MICRO:
             received = from_behind(layer_out.astype(jnp.bfloat16), "section", 1)
-    head_total = tuple((jnp.zeros(member.shape, jnp.float32) for member in params[:4]))
-    tail_total = tuple((jnp.zeros(member.shape, jnp.float32) for member in params[4:]))
     zero_grad = jnp.zeros((micro_rows, model_width), jnp.float32)
     came_back = zero_grad
     input_grads = [zero_grad for micro_idx in range(MICRO)]
+    vectors = 0.0
+    factors = []
     for back_step in range(MICRO + 1):
         tick_fwd = MICRO - back_step
         own_index = MICRO - 1 - back_step
         own_grad = pieces[own_index].astype(jnp.float32) if own_index >= 0 else zero_grad
         grad_out = jnp.where(is_first, came_back, own_grad)
         kept = states_kept[tick_fwd]
-        grad_first, tail_terms = tail_back(grad_out, params, kept)
-        tail_total = tuple(jax.tree.map(jnp.add, tail_total, tail_terms))
-        grad_in, head_terms = head_back(grad_first, params, kept, layout)
-        head_total = tuple(jax.tree.map(jnp.add, head_total, head_terms))
+        grad_first, tail_terms, tail_factors = tail_back(grad_out, params, kept)
+        grad_in, head_terms, head_factors = head_back(grad_first, params, kept, layout)
+        vectors = vectors + jnp.concatenate(head_terms + tail_terms)
+        factors.append(
+            (
+                (kept[11], kept[9], kept[6], kept[0]),
+                (tail_factors[1], tail_factors[0], head_factors[0], head_factors[1]),
+            )
+        )
         if tick_fwd < MICRO:
             input_grads[tick_fwd] = grad_in
         if back_step < MICRO:
             came_back = from_behind(grad_in.astype(jnp.bfloat16), "section", -1).astype(jnp.float32)
-    summed_all = tuple(
-        lax.psum(
-            (
-                head_total[0],
-                head_total[1],
-                head_total[2],
-                head_total[3],
-                tail_total[0],
-                tail_total[1],
-                tail_total[2],
-                tail_total[3],
-                tail_total[4],
-                tail_total[5],
-                tail_total[6],
-                tail_total[7],
-            ),
-            "dp",
+    factors.reverse()
+
+    def chosen(side):
+        picked = []
+        for member in range(4):
+            ticks = [factors[tick][side][member] for tick in range(MICRO + 1)]
+            early = jnp.concatenate(ticks[:MICRO], axis=0)
+            late = jnp.concatenate(ticks[1:], axis=0)
+            picked.append(jnp.where(is_first, early, late))
+        joined = jnp.concatenate(picked, axis=1)
+        return joined.reshape(joined.shape[0], -1, UNIT).transpose(1, 0, 2)
+
+    dp_size = lax.axis_size("dp")
+    vec_rows = 16 * dp_size
+    vec = jnp.zeros((vec_rows * UNIT,), jnp.float32).at[: vectors.shape[0]].set(vectors)
+    summed = reduce_gradients(
+        chosen(0), chosen(1), vec.astype(jnp.bfloat16).reshape(vec_rows, UNIT), dp_size
+    ).astype(jnp.float32)
+
+    def matrix(start, across, down):
+        blocks = summed[start * UNIT : (start + across * down) * UNIT]
+        return (
+            blocks.reshape(down, across, UNIT, UNIT)
+            .transpose(0, 2, 1, 3)
+            .reshape(down * UNIT, across * UNIT)
         )
+
+    flat = summed[108 * UNIT :].reshape(-1)
+    spots, start = [], 0
+    for size in (3 * model_width, model_width, model_width, model_width, 4 * model_width) + (
+        model_width,
+    ) * 3:
+        spots.append(flat[start : start + size])
+        start += size
+    summed_all = (
+        matrix(81, 9, 3), spots[0], matrix(72, 3, 3), spots[1], spots[2], spots[3],
+        matrix(36, 12, 3), spots[4], matrix(0, 3, 12), spots[5], spots[6], spots[7],
     )
     answers = jnp.where(
         is_first, jnp.concatenate(input_grads, axis=0), jnp.concatenate(outputs_kept[1:], axis=0)

time: 1220 us -> 880 us (0.72)
  waiting for transfers between devices: 643 us -> 4.39 us
  Pallas kernels: 0 us -> 214 us
  local copies, waits for them, and re-layouts: 83.5 us -> 261 us
  blocking collectives: 84.3 us -> 0 us
  other arithmetic: 47.7 us -> 122 us
  matrix products: 325 us -> 255 us
  between operations: 17.8 us -> 4.32 us
    psum x1 -> x0, waiting for transfers between devices: 640 us -> none  [shards(): lax.psum((head_total[0], head_total[1], head_total[2], head_total[3], tai...]
    pallas_call x0 -> x1, Pallas kernels: none -> 214 us  [reduce_gradients(): pl.pallas_call(partial(reduce_kernel, dims, pieces, rows, units), out_sha...]
    reshape x0 -> x16, local copies, waits for them, and re-layouts: none -> 91.4 us  [the longest x4 39.4 us: matrix(): blocks.reshape(down, across, UNIT, UNIT).transpose(0, 2, 1, 3)]
    psum x1 -> x0, blocking collectives: 84.3 us -> none  [shards(): lax.psum((head_total[0], head_total[1], head_total[2], head_total[3], tai...]
    dot_general x12 -> x0, matrix products: 75.3 us -> none  [rows_product(): lax.dot_general(left_mat, right_mat, (((0,), (0,)), ((), ())), preferred_...]
    another operation x0 -> x4, local copies, waits for them, and re-layouts: none -> 40.7 us  [shards(): return (answers,) + tuple((member[None] for member in summed_all))]
    concatenate x0 -> x4, local copies, waits for them, and re-layouts: none -> 33.3 us  [the longest x2 33.3 us: chosen(): joined = jnp.concatenate(picked, axis=1)]
    select_n x0 -> x5, other arithmetic: none -> 30.7 us  [chosen(): picked.append(jnp.where(is_first, early, late))]
  transfers between devices with their start and end apart: 5 -> 4, of which waited for: 3 -> 2; matrix products, arithmetic and copies ran while one was open for 2% -> 1% of each run, Pallas kernels for 0% -> 0%
where the time goes in v1:
time: 880 us; the launch traced here: 870 us
  local copies, waits for them, and re-layouts  261 us (30%)
  matrix products  255 us (29%)
  Pallas kernels  214 us (24%)
  other arithmetic  122 us (14%)
  starting transfers between devices  9.08 us (1%)
    pallas_call x1, Pallas kernels, reduce_gradients(): pl.pallas_call(partial(reduce_kernel, dims, pieces, rows, units), out_sha...  214 us
    dot_general x12, matrix products, back_product(): lax.dot_general(grad_mat, weight_mat, (((1,), (1,)), ((), ())), preferred...  63.9 us
    dot_general x3, matrix products, layer_forward(): jnp.dot(up_in, up_w, preferred_element_type=jnp.float32)  55.6 us
    unnamed x346, local copies, waits for them, and re-layouts  40.7 us
    another operation x4, local copies, waits for them, and re-layouts, shards(): return (answers,) + tuple((member[None] for member in summed_all))  40.7 us
    reshape x4, local copies, waits for them, and re-layouts, matrix(): blocks.reshape(down, across, UNIT, UNIT).transpose(0, 2, 1, 3)  39.4 us
    dot_general x3, matrix products, mix_block_back(): jnp.einsum('hqk,qhe->khe', grad_scores, queries, preferred_element_type=j...  38.7 us
    dot_general x3, matrix products, mix_block_back(): jnp.einsum('hqk,khe->qhe', grad_scores, keys_in, preferred_element_type=j...  36.2 us
  transfers between devices with their start and end apart: 4, of which 2 were waited for; matrix products, arithmetic and copies ran while one was open for 1% of the time, Pallas kernels for 0%

profile of v1, /device:TPU:0, one launch (start us, length us, event | category | flops | bytes accessed | tf_op | source)
XLA Modules:
  0.0 869.7 jit_solution(4447635908656774496)
XLA Ops:
  32.2 18.3 %multiply_convert_fusion.5 = (bf16[512,3072]{1,0:T(8,128)(2,1)S(1)}, f32[512,3072]{1,0:T(8,128)}, f32[512,3072]{1,0:T(8,128)}) fusion(f32[3072]{0:T(1024)S(1)} %bitcast.356, bf16[512,768]{1,0:T(8,128)(2,1)S(1)} %fusion.145, bf16[1,768,3072]{2,1,0:T(8,128)(2,1)S(1)} %bitcast.378), kind=kOutput, calls=%fused_computation.61 | convolution fusion | flops 2519728128 | bytes 21245952 | tf_op jit(solution)/shard_map/dot_general | solution.py:150
  83.0 18.3 %multiply_convert_fusion.4 = (bf16[512,3072]{1,0:T(8,128)(2,1)S(1)}, f32[512,3072]{1,0:T(8,128)}, f32[512,3072]{1,0:T(8,128)}) fusion(f32[3072]{0:T(1024)S(1)} %bitcast.357, bf16[512,768]{1,0:T(8,128)(2,1)S(1)} %fusion.146, bf16[1,768,3072]{2,1,0:T(8,128)(2,1)S(1)} %bitcast.380), kind=kOutput, calls=%fused_computation.48 | convolution fusion | flops 2519728128 | bytes 21245952 | tf_op jit(solution)/shard_map/dot_general | solution.py:150
  143.9 19.0 %multiply_convert_fusion.3 = (bf16[512,3072]{1,0:T(8,128)(2,1)S(1)}, f32[512,3072]{1,0:T(8,128)}, f32[512,3072]{1,0:T(8,128)}) fusion(f32[3072]{0:T(1024)S(1)} %bitcast.358, bf16[512,768]{1,0:T(8,128)(2,1)S(1)} %fusion.149, bf16[1,768,3072]{2,1,0:T(8,128)(2,1)} %param.23), kind=kOutput, calls=%fused_computation.35 | convolution fusion | flops 2519728128 | bytes 21245952 | tf_op jit(solution)/shard_map/dot_general | solution.py:150
  201.0 12.4 %convolution_bitcast_fusion.5 = f32[512,12,128]{0,2,1:T(8,128)} fusion(bf16[512,12,64]{0,2,1:T(8,128)(2,1)} %copy-done.42, bf16[512,12,64]{0,2,1:T(8,128)(2,1)} %copy-done.41, f32[12,512]{1,0:T(8,128)} %copy-done.105, f32[512,512]{0,1:T(8,128)} %copy-done.8, bf16[512,12,64]{0,2,1:T(8,128)(2,1)} %bitcast.346, bf16[512,12,64]{0,2,1:T(8,128)(2,1)} %bitcast.334, ...), kind=kOutput, calls=%fused_computation.145 | convolution fusion | flops 1635785216 | bytes 19947520 | tf_op jit(solution)/shard_map/while/body/eval_jaxpr/hqk,khe->qhe/dot_general | solution.py:106
  213.3 13.6 %convolution_bitcast_fusion.4 = f32[512,12,128]{0,2,1:T(8,128)} fusion(bf16[512,12,64]{0,2,1:T(8,128)(2,1)S(1)} %get-tuple-element.265, bf16[512,12,64]{0,2,1:T(8,128)(2,1)} %copy-done.40, f32[12,512]{1,0:T(8,128)} %copy-done.105, f32[512,512]{0,1:T(8,128)} %copy-done.8, bf16[512,12,64]{0,2,1:T(8,128)(2,1)} %bitcast.347, ...), kind=kOutput, calls=%fused_computation.144 | convolution fusion | flops 1635785216 | bytes 19947520 | tf_op jit(solution)/shard_map/while/body/eval_jaxpr/hqk,qhe->khe/dot_general | solution.py:109
  279.6 12.0 %convolution_bitcast_fusion.3 = f32[512,12,128]{0,2,1:T(8,128)} fusion(bf16[512,12,64]{0,2,1:T(8,128)(2,1)} %copy-done.39, bf16[512,12,64]{0,2,1:T(8,128)(2,1)} %copy-done.38, f32[12,512]{1,0:T(8,128)S(1)} %copy-done.104, f32[512,512]{0,1:T(8,128)S(1)} %copy-done.9, bf16[512,12,64]{0,2,1:T(8,128)(2,1)} %bitcast.350, bf16[512,12,64]{0,2,1:T(8,128)(2,1)} %bitcast.331, ...), kind=kOutput, calls=%fused_computation.143 | convolution fusion | flops 1635785216 | bytes 19947520 | tf_op jit(solution)/shard_map/while/body/eval_jaxpr/hqk,khe->qhe/dot_general | solution.py:106
  291.6 12.6 %convolution_bitcast_fusion.2 = f32[512,12,128]{0,2,1:T(8,128)} fusion(bf16[512,12,64]{0,2,1:T(8,128)(2,1)S(1)} %copy-done.36, bf16[512,12,64]{0,2,1:T(8,128)(2,1)} %copy-done.37, f32[12,512]{1,0:T(8,128)S(1)} %copy-done.104, f32[512,512]{0,1:T(8,128)S(1)} %copy-done.9, bf16[512,12,64]{0,2,1:T(8,128)(2,1)} %bitcast.351, ...), kind=kOutput, calls=%fused_computation.142 | convolution fusion | flops 1635785216 | bytes 19947520 | tf_op jit(solution)/shard_map/while/body/eval_jaxpr/hqk,qhe->khe/dot_general | solution.py:109
  341.1 12.4 %maximum_select_fusion = (bf16[1024,3072]{1,0:T(8,128)(2,1)}, bf16[1024,3072]{1,0:T(8,128)(2,1)}) fusion(bf16[512,3072]{1,0:T(8,128)(2,1)S(1)} %copy-done.46, bf16[512,3072]{1,0:T(8,128)(2,1)S(1)} %copy-done.44, bf16[512,3072]{1,0:T(8,128)(2,1)S(1)} %copy-done.48, pred[]{:T(512)S(6)} %eq.24, bf16[512,3072]{1,0:T(8,128)(2,1)S(1)} %copy-done.50, ...), kind=kLoop, calls=%fused_computation.27 | loop fusion | flops 56623104 | bytes 31457280 | tf_op jit(solution)/shard_map/jit(_where)/select_n | solution.py:675
  376.5 11.8 %convolution_bitcast_fusion.1 = f32[512,12,128]{0,2,1:T(8,128)} fusion(bf16[512,12,64]{0,2,1:T(8,128)(2,1)} %copy-done.34, bf16[512,12,64]{0,2,1:T(8,128)(2,1)} %copy-done.33, f32[12,512]{1,0:T(8,128)S(1)} %copy-done.102, f32[512,512]{0,1:T(8,128)S(1)} %copy-done.9, bf16[512,12,64]{0,2,1:T(8,128)(2,1)} %bitcast.342, bf16[512,12,64]{0,2,1:T(8,128)(2,1)} %bitcast.328, ...), kind=kOutput, calls=%fused_computation.141 | convolution fusion | flops 1635785216 | bytes 19947520 | tf_op jit(solution)/shard_map/while/body/eval_jaxpr/hqk,khe->qhe/dot_general | solution.py:106
  388.3 12.5 %convolution_bitcast_fusion = f32[512,12,128]{0,2,1:T(8,128)} fusion(bf16[512,12,64]{0,2,1:T(8,128)(2,1)S(1)} %copy-done.31, bf16[512,12,64]{0,2,1:T(8,128)(2,1)} %copy-done.32, f32[12,512]{1,0:T(8,128)S(1)} %copy-done.102, f32[512,512]{0,1:T(8,128)S(1)} %copy-done.9, bf16[512,12,64]{0,2,1:T(8,128)(2,1)} %bitcast.343, bf16[512,12,64]{0,2,1:T(8,128)(2,1)} %bitcast.329, ...), kind=kOutput, calls=%fused_computation.140 | convolution fusion | flops 1635785216 | bytes 19947520 | tf_op jit(solution)/shard_map/while/body/eval_jaxpr/hqk,qhe->khe/dot_general | solution.py:109
  412.6 12.1 %maximum_select_fusion.2 = bf16[1024,2304]{1,0:T(8,128)(2,1)} fusion(bf16[512,768]{1,0:T(8,128)(2,1)} %copy-done.18, bf16[512,768]{1,0:T(8,128)(2,1)} %copy.240, bf16[512,768]{1,0:T(8,128)(2,1)} %copy.239, bf16[512,768]{1,0:T(8,128)(2,1)} %copy.248, bf16[512,768]{1,0:T(8,128)(2,1)} %copy.247, bf16[512,768]{1,0:T(8,128)(2,1)} %copy.246, ...), kind=kLoop, calls=%fused_computation.80 | loop fusion | flops 58982400 | bytes 11796481 | tf_op jit(solution)/shard_map/jit(_where)/select_n | solution.py:675
  434.4 14.7 %copy.253 = bf16[1024,5376]{0,1:T(8,128)(2,1)} copy(bf16[1024,5376]{1,0:T(8,128)(2,1)} %pad_maximum_fusion.1) | data formatting | bytes 22020096 | tf_op jit(solution)/shard_map/concatenate | solution.py:676
  449.1 14.7 %copy.254 = bf16[1024,21,256]{2,0,1:T(8,128)(2,1)} copy(bf16[1024,21,256]{0,2,1:T(8,128)(2,1)} %bitcast.298) | data formatting | bytes 22020096 | tf_op jit(solution)/shard_map/reshape | solution.py:677
  463.8 12.9 %pad_maximum_fusion = bf16[1024,6912]{1,0:T(8,128)(2,1)} fusion(bf16[1024,2304]{1,0:T(8,128)(2,1)} %maximum_select_fusion.2, bf16[1024,768]{1,0:T(8,128)(2,1)} %get-tuple-element.310, bf16[1024,3072]{1,0:T(8,128)(2,1)} %get-tuple-element.306, bf16[1024,768]{1,0:T(8,128)(2,1)S(1)} %copy-done.26), kind=kLoop, calls=%fused_computation.3 | loop fusion | flops 56623104 | bytes 28311552 | tf_op jit(solution)/shard_map/concatenate | solution.py:676
  476.7 18.7 %copy.255 = bf16[1024,6912]{0,1:T(8,128)(2,1)} copy(bf16[1024,6912]{1,0:T(8,128)(2,1)} %pad_maximum_fusion) | data formatting | bytes 28311552 | tf_op jit(solution)/shard_map/concatenate | solution.py:676
  495.4 18.7 %copy.256 = bf16[1024,27,256]{2,0,1:T(8,128)(2,1)} copy(bf16[1024,27,256]{0,2,1:T(8,128)(2,1)} %bitcast.295) | data formatting | bytes 28311552 | tf_op jit(solution)/shard_map/reshape | solution.py:677
  514.9 213.8 %shard_map.237 = bf16[27904,256]{1,0:T(8,128)(2,1)} custom-call(bf16[21,1024,256]{2,1,0:T(8,128)(2,1)} %bitcast.319, bf16[27,1024,256]{2,1,0:T(8,128)(2,1)} %bitcast.305, bf16[256,256]{1,0:T(8,128)(2,1)} %reshape.507.vec_hbm), custom_call_target="tpu_custom_call" | custom-call | flops 14495514624 | bytes 125829120 | tf_op jit(solution)/shard_map/pallas_call | solution.py:559
  745.0 11.7 %convert_element_type.315 = f32[27904,256]{1,0:T(8,128)} convert(bf16[27904,256]{1,0:T(8,128)(2,1)S(1)} %copy-done.1) | non-fusion elementwise | flops 7143424 | bytes 42860544 | tf_op jit(solution)/shard_map/convert_element_type | solution.py:684
  770.6 10.7 %copy.257 = f32[3,9,256,256]{2,0,3,1:T(4,128)} copy(f32[3,9,256,256]{3,2,1,0:T(8,128)} %bitcast.302) | data formatting | bytes 14155776 | tf_op jit(solution)/shard_map/reshape | solution.py:689
  781.3 12.0 %broadcast_in_dim_reshape.12 = f32[1,768,2304]{1,2,0:T(8,128)} reshape(f32[3,256,9,256]{1,0,3,2:T(4,128)} %bitcast.299) | data formatting | bytes 14155776 | tf_op jit(solution)/shard_map/broadcast_in_dim;reshape | solution.py:708
  801.3 13.9 %copy.291 = f32[3,12,256,256]{3,1,2,0:T(8,128)} copy(f32[3,12,256,256]{3,2,1,0:T(8,128)} %bitcast.301) | data formatting | bytes 18874368 | tf_op jit(solution)/shard_map/reshape | solution.py:689
  815.2 11.8 %broadcast_in_dim_reshape.14 = f32[1,768,3072]{2,1,0:T(8,128)} reshape(f32[3,256,12,256]{3,2,1,0:T(8,128)} %bitcast.296) | data formatting | bytes 18874368 | tf_op jit(solution)/shard_map/broadcast_in_dim;reshape | solution.py:708
  827.0 11.6 %copy.260 = f32[12,3,256,256]{2,0,3,1:T(8,128)} copy(f32[12,3,256,256]{3,2,1,0:T(8,128)} %bitcast.300) | data formatting | bytes 18874368 | tf_op jit(solution)/shard_map/reshape | solution.py:689
  838.6 11.9 %broadcast_in_dim_reshape.15 = f32[1,3072,768]{1,2,0:T(8,128)} reshape(f32[12,256,3,256]{1,0,3,2:T(8,128)} %bitcast.297) | data formatting | bytes 18874368 | tf_op jit(solution)/shard_map/broadcast_in_dim;reshape | solution.py:708
  (508 shorter events, 333.4 us)
Async XLA Ops:
  0.6 28.1 %copy-start = (bf16[1,768,768]{2,1,0:T(8,128)(2,1)S(1)}, bf16[1,768,768]{2,1,0:T(8,128)(2,1)}, u32[]{:S(2)}) copy-start(bf16[1,768,768]{2,1,0:T(8,128)(2,1)} %param.19) | copy-start | bytes 3538948
  10.1 91.2 %copy-start.88 = (f32[768]{0:T(1024)}, f32[768]{0:T(1024)S(1)}, u32[]{:S(2)}) copy-start(f32[768]{0:T(1024)S(1)} %convert_reduce_fusion.16) | copy-start | bytes 9220
  10.2 71.1 %copy-start.128 = (f32[768]{0:T(1024)}, f32[768]{0:T(1024)S(1)}, u32[]{:S(2)}) copy-start(f32[768]{0:T(1024)S(1)} %convert_reduce_fusion.18) | copy-start | bytes 9220
  10.2 91.1 %copy-start.126 = (f32[768]{0:T(1024)}, f32[768]{0:T(1024)S(1)}, u32[]{:S(2)}) copy-start(f32[768]{0:T(1024)S(1)} %convert_reduce_fusion.15) | copy-start | bytes 9220
  10.3 94.3 %copy-start.90 = (f32[768]{0:T(1024)}, f32[768]{0:T(1024)S(1)}, u32[]{:S(2)}) copy-start(f32[768]{0:T(1024)S(1)} %convert_reduce_fusion.13) | copy-start | bytes 9220
  10.3 72.6 %copy-start.122 = (f32[1,3072]{1,0:T(1,128)}, f32[1,3072]{1,0:T(1,128)S(1)}, u32[]{:S(2)}) copy-start(f32[1,3072]{1,0:T(1,128)S(1)} %add.414) | copy-start | bytes 36868
  10.6 122.9 %copy-start.8 = (f32[512,512]{0,1:T(8,128)}, f32[512,512]{0,1:T(8,128)S(1)}, u32[]{:S(2)}) copy-start(f32[512,512]{0,1:T(8,128)S(1)} %fusion.166) | copy-start | bytes 3145732
  29.7 20.8 %copy-start.10 = (f32[512,768]{1,0:T(8,128)}, f32[512,768]{1,0:T(8,128)S(1)}, u32[]{:S(2)}) copy-start(f32[512,768]{1,0:T(8,128)S(1)} %get-tuple-element.276) | copy-start | bytes 4718596
  29.7 20.8 %copy-start.106 = (f32[512]{0:T(512)}, f32[512]{0:T(512)S(1)}, u32[]{:S(2)}) copy-start(f32[512]{0:T(512)S(1)} %broadcast_multiply_fusion.17) | copy-start | bytes 6148
  29.7 20.8 %slice-start.2 = ((s8[4718592]{0:T(1024)(128)(4,1)}), s8[4194304]{0:T(1024)(128)(4,1)S(1)}, s32[]{:S(2)}) async-start(s8[4718592]{0:T(1024)(128)(4,1)} %bitcast.369), calls=%async_computation.2 | async-start | bytes 8388608
  30.1 20.5 %copy-start.114 = (f32[512]{0:T(512)}, f32[512]{0:T(512)S(1)}, u32[]{:S(2)}) copy-start(f32[512]{0:T(512)S(1)} %add_rsqrt_fusion.5) | copy-start | bytes 6148
  30.4 20.1 %copy-start.52 = (bf16[512,768]{1,0:T(8,128)(2,1)}, bf16[512,768]{1,0:T(8,128)(2,1)S(1)}, u32[]{:S(2)}) copy-start(bf16[512,768]{1,0:T(8,128)(2,1)S(1)} %fusion.145) | copy-start | bytes 2359300
  54.1 4.5 collective-permute-start
  81.3 20.1 %slice-start.4 = ((s8[4718592]{0:T(1024)(128)(4,1)}), s8[4194304]{0:T(1024)(128)(4,1)S(1)}, s32[]{:S(2)}) async-start(s8[4718592]{0:T(1024)(128)(4,1)} %bitcast.371), calls=%async_computation.4 | async-start | bytes 8388608
  82.2 19.1 %copy-start.12 = (f32[512,768]{1,0:T(8,128)}, f32[512,768]{1,0:T(8,128)S(1)}, u32[]{:S(2)}) copy-start(f32[512,768]{1,0:T(8,128)S(1)} %get-tuple-element.283) | copy-start | bytes 4718596
  82.2 19.1 %copy-start.108 = (f32[512]{0:T(512)}, f32[512]{0:T(512)S(1)}, u32[]{:S(2)}) copy-start(f32[512]{0:T(512)S(1)} %broadcast_multiply_fusion.15) | copy-start | bytes 6148
  82.6 18.8 %copy-start.116 = (f32[512]{0:T(512)}, f32[512]{0:T(512)S(1)}, u32[]{:S(2)}) copy-start(f32[512]{0:T(512)S(1)} %add_rsqrt_fusion.3) | copy-start | bytes 6148
  107.2 6.9 collective-permute-start.1
  140.7 22.2 %slice-start.6 = ((s8[4718592]{0:T(1024)(128)(4,1)}), s8[4194304]{0:T(1024)(128)(4,1)S(1)}, s32[]{:S(2)}) async-start(s8[4718592]{0:T(1024)(128)(4,1)} %bitcast.373), calls=%async_computation.6 | async-start | bytes 8388608
  143.8 19.0 %copy-start.56 = (bf16[512,768]{1,0:T(8,128)(2,1)}, bf16[512,768]{1,0:T(8,128)(2,1)S(1)}, u32[]{:S(2)}) copy-start(bf16[512,768]{1,0:T(8,128)(2,1)S(1)} %fusion.149) | copy-start | bytes 2359300
  143.8 19.0 %copy-start.127 = (f32[768]{0:T(1024)S(1)}, f32[768]{0:T(1024)}, u32[]{:S(2)}) copy-start(f32[768]{0:T(1024)} %copy-done.126) | copy-start | bytes 9220
  143.9 19.0 %slice-start.7 = ((s8[4718592]{0:T(1024)(128)(4,1)}), s8[524288]{0:T(1024)(128)(4,1)S(1)}, s32[]{:S(2)}) async-start(s8[4718592]{0:T(1024)(128)(4,1)} %bitcast.373), calls=%async_computation.7 | async-start | bytes 1048576
  246.6 5.9 collective-permute-start.2
  324.7 4.2 collective-permute-start.3
  (136 other events, 860.6 us)

commit v2 on v1

v2 whole, which is shorter than its diff:
```python
from functools import partial
import math

import jax
import jax.numpy as jnp
from jax import lax
from jax.experimental import pallas as pl
from jax.experimental.pallas import tpu as pltpu
from jax.sharding import PartitionSpec as P

HEADS = 12
EPSILON = 1e-05
MESH = pl.DeviceIdType.MESH


def rows_product(left_mat, right_mat):
    return lax.dot_general(
        left_mat, right_mat, (((0,), (0,)), ((), ())), preferred_element_type=jnp.float32
    )


def back_product(grad_mat, weight_mat):
    return lax.dot_general(
        grad_mat, weight_mat, (((1,), (1,)), ((), ())), preferred_element_type=jnp.float32
    )


def factor_dims(count):
    bits = count.bit_length() - 1
    return (1 << (bits // 3), 1 << ((bits + 1) // 3), 1 << ((bits + 2) // 3))


ORDERS = {"a": (0, 1, 2), "b": (1, 2, 0), "c": (2, 0, 1)}
PATTERN = "abacabc"
LAG = 3
UNIT = 256


def stage_list(order, dims, rows):
    stages, size, landing = [], rows, 0
    for level, ax in enumerate(order):
        part = size // dims[ax]
        for step in range(1, dims[ax]):
            stages.append(("reduce", level, ax, step, part, landing))
            landing += part if dims[ax] == 2 else 2 * part
        size = part
    for level in reversed(range(3)):
        ax = order[level]
        for step in range(1, dims[ax]):
            stages.append(("gather", level, ax, step, size, 0))
        size *= dims[ax]
    return stages, landing


def unit_blocks(unit):
    up, out, proj = unit - 36, unit - 72, unit - 81
    left = jnp.where(
        unit < 36,
        unit // 3,
        jnp.where(unit < 72, 12 + up // 12, jnp.where(unit < 81, 15 + out // 3, 18 + proj // 9)),
    )
    right = jnp.where(
        unit < 36,
        unit % 3,
        jnp.where(unit < 72, 3 + up % 12, jnp.where(unit < 81, 15 + out % 3, 18 + proj % 9)),
    )
    return left, right


def reduce_kernel(dims, pieces, rows, units, left_hbm, right_hbm, vec_hbm,
                  proj_hbm, out_hbm, up_hbm, down_hbm, small_hbm, acc, landing, full, vec_buf, left_buf, right_buf, load_sem, vec_sem, out_sem,
                  send_sem, recv_sem):
    here = lax.axis_index("dp")
    strides = (1, dims[0], dims[0] * dims[1])
    place = [(here // strides[ax]) % dims[ax] for ax in range(3)]
    slots = send_sem.shape[0]
    ring = left_buf.shape[0]
    per_piece = rows // UNIT
    land_rows = landing.shape[0] // slots
    plans = {name: stage_list(order, dims, rows)[0] for name, order in ORDERS.items()}
    n_stages = len(plans["a"])
    n_shards = dims[0] * dims[1] * dims[2]
    period = len(PATTERN)
    rounds = -(-pieces // period)
    all_rounds = -(-(pieces + n_stages * LAG) // period)

    bases = {}
    for name, order in ORDERS.items():
        base, size, found = 0, rows, []
        for ax in order:
            found.append(base)
            size = size // dims[ax]
            base = base + place[ax] * size
        bases[name] = found

    def neighbour(ax, sign):
        return {"dp": here + sign * strides[ax]}

    barrier = pltpu.get_barrier_semaphore()
    for ax in range(3):
        for sign, can in ((1, place[ax] < dims[ax] - 1), (-1, place[ax] > 0)):
            @pl.when(can)
            def _():
                pl.semaphore_signal(
                    barrier, inc=1, device_id=neighbour(ax, sign), device_id_type=MESH
                )
    around = sum(
        (place[ax] < dims[ax] - 1).astype(jnp.int32) + (place[ax] > 0).astype(jnp.int32)
        for ax in range(3)
    )
    pl.semaphore_wait(barrier, around)

    def loads(unit):
        slot = unit % ring
        left, right = unit_blocks(unit)
        return (
            pltpu.make_async_copy(left_hbm.at[left], left_buf.at[slot], load_sem.at[slot, 0]),
            pltpu.make_async_copy(right_hbm.at[right], right_buf.at[slot], load_sem.at[slot, 1]),
        )

    vec_copy = pltpu.make_async_copy(vec_hbm, vec_buf, vec_sem)
    vec_copy.start()
    for unit in range(ring):
        for copy in loads(jnp.int32(unit)):
            copy.start()
    vec_copy.wait()

    def form(piece, sub):
        unit = piece * per_piece + sub
        start = (piece % slots) * rows + sub * UNIT

        @pl.when(unit < units)
        def _():
            for copy in loads(unit):
                copy.wait()
            slot = unit % ring
            acc[pl.ds(pl.multiple_of(start, UNIT), UNIT), :] = lax.dot_general(
                left_buf[slot], right_buf[slot], (((0,), (0,)), ((), ())),
                preferred_element_type=jnp.float32,
            ).astype(jnp.bfloat16)

            @pl.when(unit + ring < units)
            def _():
                for copy in loads(unit + ring):
                    copy.start()

        @pl.when(unit >= units)
        def _():
            acc[pl.ds(pl.multiple_of(start, UNIT), UNIT), :] = vec_buf[
                sub * UNIT : (sub + 1) * UNIT
            ].astype(jnp.bfloat16)

    def copies(name, stage, piece):
        kind, level, ax, step, part, land = plans[name][stage]
        count, spot = dims[ax], place[ax]
        slot = piece % slots
        held, index = (acc, slot) if kind == "reduce" else (full, piece)
        start = index * rows + bases[name][level]
        land_start = pl.multiple_of(slot * land_rows + land, 16)

        def chunk(q):
            return held.at[pl.ds(pl.multiple_of(start + q * part, 16), part)]

        def landed(way):
            return landing.at[pl.ds(pl.multiple_of(land_start + way * part, 16), part)]

        def remote(src, dst, way, sign):
            return lambda: pltpu.make_async_remote_copy(
                src_ref=src, dst_ref=dst, send_sem=send_sem.at[slot, stage, way],
                recv_sem=recv_sem.at[slot, stage, way], device_id=neighbour(ax, sign),
                device_id_type=MESH,
            )

        sends, receives = [], []
        if count == 2:
            sign = 1 - 2 * spot
            mine, other = spot, 1 - spot
            if kind == "reduce":
                sends.append((None, remote(chunk(other), landed(0), 0, sign)))
                receives.append((None, remote(chunk(mine), landed(0), 0, sign), mine, landed(0)))
            else:
                sends.append((None, remote(chunk(mine), chunk(mine), 0, sign)))
                receives.append((None, remote(chunk(other), chunk(other), 0, sign), other, None))
            return sends, receives, chunk
        back = count - 1 - spot
        if kind == "reduce":
            for way, sign, can, q in (
                (0, 1, spot < step, spot + count - step),
                (1, -1, back < step, step - 1 - back),
            ):
                q = jnp.clip(q, 0, count - 1)
                sends.append((can, remote(chunk(q), landed(way), way, sign)))
            for way, sign, can, q in (
                (0, 1, jnp.logical_and(spot >= 1, spot - 1 < step), spot - 1 + count - step),
                (1, -1, jnp.logical_and(back >= 1, back - 1 < step), step - back),
            ):
                q = jnp.clip(q, 0, count - 1)
                receives.append((can, remote(chunk(q), landed(way), way, sign), q, landed(way)))
        else:
            for way, sign, can, q in (
                (0, 1, jnp.logical_and(back >= 1, spot >= step - 1), spot - step + 1),
                (1, -1, jnp.logical_and(spot >= 1, back >= step - 1), spot + step - 1),
            ):
                q = jnp.clip(q, 0, count - 1)
                sends.append((can, remote(chunk(q), chunk(q), way, sign)))
            for way, sign, can, q in (
                (0, 1, spot >= step, spot - step),
                (1, -1, back >= step, spot + step),
            ):
                q = jnp.clip(q, 0, count - 1)
                receives.append((can, remote(chunk(q), chunk(q), way, sign), q, None))
        return sends, receives, chunk

    def guarded(can, action):
        if can is None:
            action()
        else:
            pl.when(can)(action)

    def out_copies(piece, action):
        for sub in range(per_piece):
            unit = piece * per_piece + sub
            source = full.at[pl.ds(pl.multiple_of(unit * UNIT, UNIT), UNIT)]
            for begin, end, across, target in (
                (0, 36, 3, down_hbm), (36, 72, 12, up_hbm), (72, 81, 3, out_hbm),
                (81, 108, 9, proj_hbm), (108, 108 + per_piece, 1, small_hbm),
            ):
                @pl.when(jnp.logical_and(unit >= begin, unit < end))
                def _():
                    local = jnp.clip(unit - begin, 0, end - begin - 1)
                    place_in = target.at[
                        pl.ds(pl.multiple_of(local // across * UNIT, UNIT), UNIT),
                        pl.ds(pl.multiple_of(local % across * UNIT, UNIT), UNIT),
                    ]
                    action(pltpu.make_async_copy(source, place_in, out_sem.at[unit]))

    def work(name, stage, piece):
        if stage > 0:
            sends, receives, chunk = copies(name, stage - 1, piece)
            for can, copy, q, landed in receives:
                def finish():
                    copy().wait_recv()
                    if landed is not None:
                        block = chunk(q)
                        block[...] = block[...] + landed[...]
                guarded(can, finish)
        if stage == n_stages // 2:
            mine = bases[name][2] + place[ORDERS[name][2]] * (rows // n_shards)
            kept = acc[pl.ds(pl.multiple_of((piece % slots) * rows + mine, 16), rows // n_shards), :]
            full[pl.ds(pl.multiple_of(piece * rows + mine, 16), rows // n_shards), :] = kept
        if stage < n_stages:
            for can, copy in copies(name, stage, piece)[0]:
                guarded(can, lambda: copy().start())
        else:
            out_copies(piece, lambda copy: copy.start())
        if stage > 0:
            for can, copy in sends:
                guarded(can, lambda: copy().wait_send())

    def one_round(turn, carry):
        for spot_in in range(period):
            tick = turn * period + spot_in
            for stage in reversed(range(1, n_stages + 1)):
                piece = tick - stage * LAG
                name = PATTERN[(spot_in - stage * LAG) % period]

                @pl.when(jnp.logical_and(piece >= 0, piece < pieces))
                def _():
                    work(name, stage, jnp.clip(piece, 0, pieces - 1))

            @pl.when(tick < pieces)
            def _():
                piece = jnp.minimum(tick, pieces - 1)
                for sub in range(per_piece):
                    form(piece, sub)
                work(PATTERN[spot_in], 0, piece)
        return carry

    lax.fori_loop(0, all_rounds, one_round, 0)

    def drain(piece, carry):
        out_copies(piece, lambda copy: copy.wait())
        return carry

    lax.fori_loop(0, pieces, drain, 0)


def reduce_gradients(left, right, vec, dp_size):
    dims = factor_dims(dp_size)
    rows = 16 * dp_size
    units = 108
    pieces = (units * UNIT + vec.shape[0]) // rows
    slots = 4 * len(PATTERN)
    ring = 4 if dp_size <= 16 else 2
    land = max(stage_list(order, dims, rows)[1] for order in ORDERS.values())
    n_stages = 2 * (sum(dims) - 3)
    tokens = left.shape[1]
    total = pieces * rows
    return pl.pallas_call(
        partial(reduce_kernel, dims, pieces, rows, units),
        out_shape=[
            jax.ShapeDtypeStruct(shape, jnp.bfloat16)
            for shape in ((768, 2304), (768, 768), (768, 3072), (3072, 768), (rows, UNIT))
        ],
        in_specs=[pl.BlockSpec(memory_space=pl.ANY)] * 3,
        out_specs=[pl.BlockSpec(memory_space=pl.ANY)] * 5,
        scratch_shapes=[
            pltpu.VMEM((slots * rows, UNIT), jnp.bfloat16),
            pltpu.VMEM((slots * land, UNIT), jnp.bfloat16),
            pltpu.VMEM((total, UNIT), jnp.bfloat16),
            pltpu.VMEM((rows, UNIT), jnp.float32),
            pltpu.VMEM((ring, tokens, UNIT), jnp.bfloat16),
            pltpu.VMEM((ring, tokens, UNIT), jnp.bfloat16),
            pltpu.SemaphoreType.DMA((ring, 2)),
            pltpu.SemaphoreType.DMA,
            pltpu.SemaphoreType.DMA((total // UNIT,)),
            pltpu.SemaphoreType.DMA((slots, n_stages, 2)),
            pltpu.SemaphoreType.DMA((slots, n_stages, 2)),
        ],
        compiler_params=pltpu.CompilerParams(
            collective_id=1, has_side_effects=True, vmem_limit_bytes=62 << 20
        ),
        cost_estimate=pl.CostEstimate(
            flops=2 * units * UNIT * UNIT * tokens, bytes_accessed=120 << 20, transcendentals=0
        ),
        name="reduce",
    )(left, right, vec)


CHUNK = 256
SAVE = {"slope": 0, "u1": 3072, "u2": 3840, "q": 4608, "k": 5376, "sq": 6144, "sk": 6912, "v": 7680}
SAVE_WIDTH = 8448
STAT = {"o": 0, "rden": 768, "s1": 1536, "s2": 1664}
STAT_WIDTH = 1792
TAIL_SCALE = 0.375
TAIL_POLY = (
    0.21141059805705423,
    0.21471795439954675,
    0.17184958530833144,
    0.26915459919947066,
    -0.10973686091480542,
    0.37354383408912983,
    -0.13093832475477368,
)


def dot(left_mat, right_mat):
    return jnp.dot(left_mat, right_mat, preferred_element_type=jnp.float32)


def inverse(value):
    rough = pl.reciprocal(value, approx=True)
    return rough * (2.0 - value * rough)


def gelu_pair(hidden):
    bell = jnp.exp(hidden * hidden * -0.5)
    t = inverse(1.0 + (TAIL_SCALE * math.sqrt(0.5)) * jnp.abs(hidden))
    poly = jnp.full_like(t, 0.5 * TAIL_POLY[-1])
    for coefficient in TAIL_POLY[-2::-1]:
        poly = poly * t + 0.5 * coefficient
    tail = poly * t * bell
    below = jnp.where(hidden >= 0, 1.0 - tail, tail)
    return hidden * below, below + hidden * (bell * (1.0 / math.sqrt(2.0 * math.pi)))


def softplus_pair(value):
    small = jnp.exp(-jnp.abs(value))
    whole = 1.0 + small
    log_whole = jnp.where(
        small < 1e-2, small * (1.0 - small * (0.5 - small * (1.0 / 3.0))), jnp.log(whole)
    )
    return (
        jnp.maximum(value, 0.0) + log_whole,
        jnp.where(value >= 0, 1.0, small) * inverse(whole),
    )


def centred(rows):
    centre = rows - jnp.mean(rows, axis=-1, keepdims=True)
    scaling = lax.rsqrt(jnp.mean(centre * centre, axis=-1, keepdims=True) + EPSILON)
    return centre * scaling, scaling


def wide(column, width=128):
    return jnp.broadcast_to(column, (column.shape[0], width))


def first_half(rows):
    return lax.broadcasted_iota(jnp.int32, (rows, 128), 1) < 64


def row(ref):
    return ref[...].astype(jnp.float32)


def forward_kernel(chunks, x_hbm, wp_hbm, wo_hbm, wu_hbm, wd_hbm, bp, bo, g1, h1, bu, bd, g2, h2, mix,
                   left_hbm, save_hbm, stat_hbm, y_hbm,
                   wp, wo, wu, wd, x_in, h_out, left_buf, save_buf, stat_buf, y_buf, nums, resid,
                   w_sem, x_sem, out_sem, send_sem, recv_sem):
    section = lax.axis_index("section")
    first = section == 0
    partner = {"section": 1 - section}
    width = x_hbm.shape[1]
    pairs = width // 128

    w_copies = [
        pltpu.make_async_copy(src, dst, w_sem.at[n])
        for n, (src, dst) in enumerate(((wp_hbm, wp), (wo_hbm, wo), (wu_hbm, wu), (wd_hbm, wd)))
    ]

    def rows_of(i):
        return pl.ds(pl.multiple_of(i * CHUNK, CHUNK), CHUNK)

    def x_copy(i):
        return pltpu.make_async_copy(x_hbm.at[rows_of(i)], x_in.at[i], x_sem.at[i])

    def hand_over(i):
        return pltpu.make_async_remote_copy(
            src_ref=h_out.at[i], dst_ref=x_in.at[i], send_sem=send_sem.at[i],
            recv_sem=recv_sem.at[i], device_id=partner, device_id_type=MESH,
        )

    def out_copies(i, slot):
        return (
            pltpu.make_async_copy(
                left_buf.at[slot], left_hbm.at[:, rows_of(i), :], out_sem.at[slot, 0]
            ),
            pltpu.make_async_copy(save_buf.at[slot], save_hbm.at[rows_of(i)], out_sem.at[slot, 1]),
            pltpu.make_async_copy(stat_buf.at[slot], stat_hbm.at[rows_of(i)], out_sem.at[slot, 2]),
            pltpu.make_async_copy(y_buf.at[slot], y_hbm.at[rows_of(i)], out_sem.at[slot, 3]),
        )

    w_copies[0].start()

    @pl.when(first)
    def _():
        for i in range(chunks):
            x_copy(i).start()

    for copy in w_copies[1:]:
        copy.start()
    barrier = pltpu.get_barrier_semaphore()
    pl.semaphore_signal(barrier, inc=1, device_id=partner, device_id_type=MESH)
    pl.semaphore_wait(barrier, 1)

    def weights_ready(i, which):
        @pl.when(i == 0)
        def _():
            w_copies[which].wait()

    def body(i, carry):
        slot = lax.rem(i, 2)
        past = 1 - slot

        @pl.when(i >= 2)
        def _():
            for copy in out_copies(i - 2, slot):
                copy.wait()

        weights_ready(i, 0)

        @pl.when(first)
        def _():
            x_copy(i).wait()

        @pl.when(jnp.logical_not(first))
        def _():
            hand_over(i).wait_recv()

        left, save, stat = left_buf.at[slot], save_buf.at[slot], stat_buf.at[slot]
        old = save_buf.at[past]

        def keep(name, start, value):
            save[:, SAVE[name] + start : SAVE[name] + start + value.shape[1]] = value.astype(
                jnp.bfloat16
            )

        def blocks(first_block, value):
            for n in range(value.shape[1] // UNIT):
                left[first_block + n] = value[:, n * UNIT : (n + 1) * UNIT]

        x = x_in[i]
        blocks(18, x)
        for part, (name, slope) in enumerate((("q", "sq"), ("k", "sk"))):
            cols = slice(part * width, (part + 1) * width)
            soft, sigma = softplus_pair(dot(x, wp[:, cols]) + row(bp)[:, cols])
            keep(name, 0, soft)
            keep(slope, 0, sigma)
        cols = slice(2 * width, 3 * width)
        keep("v", 0, dot(x, wp[:, cols]) + row(bp)[:, cols])

        low = first_half(CHUNK)

        def mix_pair(pair, source, table, fresh):
            def cut(ref, name):
                return ref[:, SAVE[name] + pair * 128 : SAVE[name] + (pair + 1) * 128]

            queries, keys_in, values = cut(save, "q"), cut(source, "k"), cut(source, "v")
            zero, one = jnp.zeros_like(keys_in), jnp.ones_like(values)
            for half in range(2):
                own = low if half == 0 else jnp.logical_not(low)
                scores = back_product(queries, jnp.where(own, keys_in, zero)) * table
                num = dot(scores.astype(jnp.bfloat16), jnp.where(own, values, one))
                at = 2 * pair + half
                nums[at] = num if fresh else nums[at] + num

        for pair in range(pairs):
            mix_pair(pair, save, mix[0], True)

        @pl.when(slot == 1)
        def _():
            for pair in range(pairs):
                mix_pair(pair, old, mix[1], False)

        for pair in range(pairs):
            num_a, num_b = nums[2 * pair], nums[2 * pair + 1]
            inv = inverse(
                jnp.where(low, pltpu.roll(num_a, 64, 1), pltpu.roll(num_b, 64, 1))
            )
            mixed = jnp.where(low, num_a, num_b) * inv
            stat[:, STAT["o"] + pair * 128 : STAT["o"] + (pair + 1) * 128] = mixed
            stat[:, STAT["rden"] + pair * 128 : STAT["rden"] + (pair + 1) * 128] = inv
        blocks(15, stat[:, : width].astype(jnp.bfloat16))
        weights_ready(i, 1)
        first_sum = x.astype(jnp.float32) + row(bo)
        for n in range(3):
            first_sum += dot(left[15 + n], wo[n * UNIT : (n + 1) * UNIT, :])
        unit_one, scale_one = centred(first_sum)
        keep("u1", 0, unit_one)
        stat[:, STAT["s1"] : STAT["s1"] + 128] = wide(scale_one)
        normed = unit_one * row(g1) + row(h1)
        resid[...] = normed + row(bd)
        up_in = normed.astype(jnp.bfloat16)
        blocks(12, up_in)
        weights_ready(i, 2)
        for n in range(4):
            cols = slice(n * width, (n + 1) * width)
            active, slope = gelu_pair(dot(up_in, wu[:, cols]) + row(bu)[:, cols])
            active = active.astype(jnp.bfloat16)
            blocks(3 * n, active)
            keep("slope", n * width, slope)
            if n == 0:
                weights_ready(i, 3)
            resid[...] += dot(active, wd[cols, :])
        unit_two, scale_two = centred(resid[...])
        keep("u2", 0, unit_two)
        stat[:, STAT["s2"] : STAT["s2"] + 128] = wide(scale_two)
        result = unit_two * row(g2) + row(h2)
        y_buf[slot] = result

        @pl.when(first)
        def _():
            h_out[i] = result.astype(jnp.bfloat16)
            hand_over(i).start()

        for copy in out_copies(i, slot):
            copy.start()
        return carry

    lax.fori_loop(0, chunks, body, 0)
    for i in (chunks - 2, chunks - 1):
        for copy in out_copies(i, i % 2):
            copy.wait()

    @pl.when(first)
    def _():
        for i in range(chunks):
            hand_over(i).wait_send()


def any_specs(count):
    return [pl.BlockSpec(memory_space=pl.ANY)] * count


def vmem_specs(count):
    return [pl.BlockSpec(memory_space=pltpu.VMEM)] * count


def run_forward(x, mats, rows, mix):
    tokens, width = x.shape
    chunks = tokens // CHUNK
    return pl.pallas_call(
        partial(forward_kernel, chunks),
        out_shape=[
            jax.ShapeDtypeStruct((21, tokens, UNIT), jnp.bfloat16),
            jax.ShapeDtypeStruct((tokens, SAVE_WIDTH), jnp.bfloat16),
            jax.ShapeDtypeStruct((tokens, STAT_WIDTH), jnp.float32),
            jax.ShapeDtypeStruct((tokens, width), jnp.float32),
        ],
        in_specs=any_specs(5) + vmem_specs(9),
        out_specs=any_specs(4),
        scratch_shapes=[pltpu.VMEM(mat.shape, mat.dtype) for mat in mats]
        + [
            pltpu.VMEM((chunks, CHUNK, width), jnp.bfloat16),
            pltpu.VMEM((chunks, CHUNK, width), jnp.bfloat16),
            pltpu.VMEM((2, 21, CHUNK, UNIT), jnp.bfloat16),
            pltpu.VMEM((2, CHUNK, SAVE_WIDTH), jnp.bfloat16),
            pltpu.VMEM((2, CHUNK, STAT_WIDTH), jnp.float32),
            pltpu.VMEM((2, CHUNK, width), jnp.float32),
            pltpu.VMEM((HEADS, CHUNK, 128), jnp.float32),
            pltpu.VMEM((CHUNK, width), jnp.float32),
            pltpu.SemaphoreType.DMA((4,)),
            pltpu.SemaphoreType.DMA((chunks,)),
            pltpu.SemaphoreType.DMA((2, 4)),
            pltpu.SemaphoreType.DMA((chunks,)),
            pltpu.SemaphoreType.DMA((chunks,)),
        ],
        compiler_params=pltpu.CompilerParams(
            collective_id=2, has_side_effects=True, vmem_limit_bytes=62 << 20
        ),
        name="forward",
    )(x, *mats, *rows, mix)


VECTORS = {"bp": (0, 9), "bo": (9, 3), "g1": (12, 3), "h1": (15, 3), "bu": (18, 12), "bd": (30, 3),
           "g2": (33, 3), "h2": (36, 3)}


def backward_kernel(chunks, e_hbm, save_hbm, stat_hbm, y_hbm, wp_hbm, wo_hbm, wu_hbm, wd_hbm, g1, g2, mix,
                    right_hbm, res_hbm, vec,
                    wp, wo, wu, wd, e_in, dh_out, right_buf, save_buf, stat_buf, dx_buf, dn1, dq, dk, dv,
                    w_buf, carry_k, carry_v,
                    w_sem, e_sem, load_sem, out_sem, res_sem, send_sem, recv_sem):
    section = lax.axis_index("section")
    first = section == 0
    partner = {"section": 1 - section}
    width = e_hbm.shape[1]
    pairs = width // 128

    w_copies = [
        pltpu.make_async_copy(src, dst, w_sem.at[n])
        for n, (src, dst) in enumerate(((wd_hbm, wd), (wu_hbm, wu), (wo_hbm, wo), (wp_hbm, wp)))
    ]

    def rows_of(i):
        return pl.ds(pl.multiple_of(i * CHUNK, CHUNK), CHUNK)

    def e_copy(i):
        return pltpu.make_async_copy(e_hbm.at[rows_of(i)], e_in.at[i], e_sem.at[i])

    def hand_over(i):
        return pltpu.make_async_remote_copy(
            src_ref=dh_out.at[i], dst_ref=e_in.at[i], send_sem=send_sem.at[i],
            recv_sem=recv_sem.at[i], device_id=partner, device_id_type=MESH,
        )

    def loads(i, slot):
        return (
            pltpu.make_async_copy(save_hbm.at[rows_of(i)], save_buf.at[slot], load_sem.at[slot, 0]),
            pltpu.make_async_copy(stat_hbm.at[rows_of(i)], stat_buf.at[slot], load_sem.at[slot, 1]),
        )

    def right_copy(i, slot):
        return pltpu.make_async_copy(
            right_buf.at[slot], right_hbm.at[:, rows_of(i), :], out_sem.at[slot]
        )

    def res_copy(i, slot):
        return pltpu.make_async_copy(dx_buf.at[slot], res_hbm.at[rows_of(i)], res_sem.at[slot])

    for i in (chunks - 1, chunks - 2):
        for copy in loads(i, i % 2):
            copy.start()

    @pl.when(jnp.logical_not(first))
    def _():
        for i in reversed(range(chunks)):
            e_copy(i).start()

    for copy in w_copies:
        copy.start()
    barrier = pltpu.get_barrier_semaphore()
    pl.semaphore_signal(barrier, inc=1, device_id=partner, device_id_type=MESH)
    pl.semaphore_wait(barrier, 1)
    vec[...] = jnp.zeros_like(vec)

    def weights_ready(step, which):
        @pl.when(step == 0)
        def _():
            w_copies[which].wait()

    def tally(name, start, values):
        total = jnp.sum(values.astype(jnp.float32), axis=0, keepdims=True)
        at = VECTORS[name][0] + start // UNIT
        for n in range(values.shape[1] // UNIT):
            vec[at + n : at + n + 1, :] += total[:, n * UNIT : (n + 1) * UNIT]

    def body(step, carry):
        i = chunks - 1 - step
        slot = lax.rem(i, 2)
        past = 1 - slot

        @pl.when(step >= 2)
        def _():
            right_copy(i + 2, slot).wait()

            @pl.when(first)
            def _():
                res_copy(i + 2, slot).wait()

        @pl.when(slot == 1)
        def _():
            for copy in loads(i, 1) + loads(i - 1, 0):
                copy.wait()

        @pl.when(first)
        def _():
            hand_over(i).wait_recv()

        @pl.when(jnp.logical_not(first))
        def _():
            e_copy(i).wait()

        right, save, stat = right_buf.at[slot], save_buf.at[slot], stat_buf.at[slot]
        old = save_buf.at[past]

        def kept(name, start=0, size=width):
            return save[:, SAVE[name] + start : SAVE[name] + start + size]

        def blocks(first_block, value):
            for n in range(value.shape[1] // UNIT):
                right[first_block + n] = value[:, n * UNIT : (n + 1) * UNIT]

        def norm_back(grad, unit_rows, scaling):
            mean_grad = jnp.mean(grad, axis=-1, keepdims=True)
            mean_cross = jnp.mean(grad * unit_rows, axis=-1, keepdims=True)
            return scaling * (grad - mean_grad - unit_rows * mean_cross)

        e = e_in[i].astype(jnp.float32)
        unit_two = kept("u2").astype(jnp.float32)
        tally("g2", 0, e * unit_two)
        tally("h2", 0, e)
        second_full = norm_back(
            e * row(g2), unit_two, stat[:, STAT["s2"] : STAT["s2"] + 1]
        )
        second_low = second_full.astype(jnp.bfloat16)
        blocks(0, second_low)
        tally("bd", 0, second_low)
        dn1[...] = second_full
        weights_ready(step, 0)
        for n in range(4):
            cols = slice(n * width, (n + 1) * width)
            hidden_low = (
                back_product(second_low, wd[cols, :])
                * kept("slope", n * width).astype(jnp.float32)
            ).astype(jnp.bfloat16)
            blocks(3 + 3 * n, hidden_low)
            tally("bu", n * width, hidden_low)
            if n == 0:
                weights_ready(step, 1)
            dn1[...] += back_product(hidden_low, wu[:, cols])
        grad_normed = dn1[...]
        unit_one = kept("u1").astype(jnp.float32)
        tally("g1", 0, grad_normed * unit_one)
        tally("h1", 0, grad_normed)
        grad_first = norm_back(
            grad_normed * row(g1), unit_one, stat[:, STAT["s1"] : STAT["s1"] + 1]
        )
        dn1[...] = grad_first
        first_low = grad_first.astype(jnp.bfloat16)
        blocks(15, first_low)
        tally("bo", 0, first_low)
        weights_ready(step, 2)
        grad_mixed = back_product(first_low, wo[...]).astype(jnp.bfloat16).astype(jnp.float32)
        w_buf[...] = (grad_mixed * stat[:, STAT["rden"] : STAT["rden"] + width]).astype(
            jnp.bfloat16
        )

        lanes = lax.broadcasted_iota(jnp.int32, (CHUNK, 128), 1)
        low = lanes < 64

        def pair_back(pair, source, table, target_k, target_v, fresh):
            span = slice(pair * 128, (pair + 1) * 128)

            def cut(ref, name):
                return ref[:, SAVE[name] + pair * 128 : SAVE[name] + (pair + 1) * 128]

            queries, keys_in, values = cut(save, "q"), cut(source, "k"), cut(source, "v")
            weighed = w_buf[:, span]
            cross = weighed.astype(jnp.float32) * stat[:, span]
            zero, one = jnp.zeros_like(keys_in), jnp.ones_like(values)
            total_q, total_k, total_v = 0.0, 0.0, 0.0
            for half in range(2):
                own = low if half == 0 else jnp.logical_not(low)
                spare = 64 * (1 - half)
                inner = jnp.sum(jnp.where(own, cross, 0.0), axis=-1, keepdims=True)
                rough = inner.astype(jnp.bfloat16).astype(jnp.float32)
                extra = jnp.where(
                    lanes == spare, -rough, jnp.where(lanes == spare + 1, rough - inner, 0.0)
                ).astype(jnp.bfloat16)
                own_keys = jnp.where(own, keys_in, zero)
                scores = (back_product(queries, own_keys) * table).astype(jnp.bfloat16)
                grads = (
                    back_product(
                        jnp.where(own, weighed, extra), jnp.where(own, values, one)
                    )
                    * table
                ).astype(jnp.bfloat16)
                total_q += dot(grads, own_keys)
                total_k += rows_product(grads, jnp.where(own, queries, zero))
                total_v += rows_product(scores, jnp.where(own, weighed, zero))
            if fresh:
                dq[:, span] = total_q
            else:
                dq[:, span] += total_q
            target_k[:, span] = total_k
            target_v[:, span] = total_v

        for pair in range(pairs):
            pair_back(pair, save, mix[0], dk, dv, True)

        @pl.when(slot == 0)
        def _():
            dk[...] += carry_k[...]
            dv[...] += carry_v[...]

        @pl.when(slot == 1)
        def _():
            for pair in range(pairs):
                pair_back(pair, old, mix[1], carry_k, carry_v, False)

        weights_ready(step, 3)
        grad_in = dn1[...]
        for n, values in enumerate(
            (
                dq[...] * kept("sq").astype(jnp.float32),
                dk[...] * kept("sk").astype(jnp.float32),
                dv[...],
            )
        ):
            values = values.astype(jnp.bfloat16)
            blocks(18 + 3 * n, values)
            tally("bp", n * width, values)
            grad_in += back_product(values, wp[:, n * width : (n + 1) * width])

        @pl.when(first)
        def _():
            dx_buf[slot] = grad_in
            res_copy(i, slot).start()

        @pl.when(jnp.logical_not(first))
        def _():
            dh_out[i] = grad_in.astype(jnp.bfloat16)
            hand_over(i).start()

        right_copy(i, slot).start()

        @pl.when(jnp.logical_and(slot == 0, i >= 2))
        def _():
            for copy in loads(i - 1, 1) + loads(i - 2, 0):
                copy.start()

        return carry

    lax.fori_loop(0, chunks, body, 0)
    for i in (1, 0):
        right_copy(i, i).wait()

    @pl.when(first)
    def _():
        for i in (1, 0):
            res_copy(i, i).wait()

    @pl.when(jnp.logical_not(first))
    def _():
        for i in range(chunks):
            hand_over(i).wait_send()


def run_backward(e, save, stat, y, mats, gains, mix, vec_rows):
    tokens, width = e.shape
    chunks = tokens // CHUNK
    wp, wo, wu, wd = mats
    return pl.pallas_call(
        partial(backward_kernel, chunks),
        out_shape=[
            jax.ShapeDtypeStruct((27, tokens, UNIT), jnp.bfloat16),
            jax.ShapeDtypeStruct((tokens, width), jnp.float32),
            jax.ShapeDtypeStruct((vec_rows, UNIT), jnp.float32),
        ],
        in_specs=any_specs(8) + vmem_specs(3),
        out_specs=any_specs(2) + vmem_specs(1),
        input_output_aliases={3: 1},
        scratch_shapes=[pltpu.VMEM(mat.shape, mat.dtype) for mat in (wp, wo, wu, wd)]
        + [
            pltpu.VMEM((chunks, CHUNK, width), jnp.bfloat16),
            pltpu.VMEM((chunks, CHUNK, width), jnp.bfloat16),
            pltpu.VMEM((2, 27, CHUNK, UNIT), jnp.bfloat16),
            pltpu.VMEM((2, CHUNK, SAVE_WIDTH), jnp.bfloat16),
            pltpu.VMEM((2, CHUNK, STAT_WIDTH), jnp.float32),
            pltpu.VMEM((2, CHUNK, width), jnp.float32),
            pltpu.VMEM((CHUNK, width), jnp.float32),
            pltpu.VMEM((CHUNK, width), jnp.float32),
            pltpu.VMEM((CHUNK, width), jnp.float32),
            pltpu.VMEM((CHUNK, width), jnp.float32),
            pltpu.VMEM((CHUNK, width), jnp.bfloat16),
            pltpu.VMEM((CHUNK, width), jnp.float32),
            pltpu.VMEM((CHUNK, width), jnp.float32),
            pltpu.SemaphoreType.DMA((4,)),
            pltpu.SemaphoreType.DMA((chunks,)),
            pltpu.SemaphoreType.DMA((2, 2)),
            pltpu.SemaphoreType.DMA((2,)),
            pltpu.SemaphoreType.DMA((2,)),
            pltpu.SemaphoreType.DMA((chunks,)),
            pltpu.SemaphoreType.DMA((chunks,)),
        ],
        compiler_params=pltpu.CompilerParams(
            collective_id=3, has_side_effects=True, vmem_limit_bytes=62 << 20
        ),
        name="backward",
    )(e, save, stat, y, wp, wo, wu, wd, *gains, mix)


def mix_tables(length):
    later = lax.broadcasted_iota(jnp.int32, (CHUNK, CHUNK), 0)
    earlier = lax.broadcasted_iota(jnp.int32, (CHUNK, CHUNK), 1)
    unit = (0.5 * math.pi) / length.astype(jnp.float32)
    seen = jnp.logical_and(later // length == earlier // length, later >= earlier)
    near = jnp.where(seen, jnp.cos((later - earlier).astype(jnp.float32) * unit), 0.0)
    far = jnp.where(
        length > CHUNK, jnp.cos((later + CHUNK - earlier).astype(jnp.float32) * unit), 0.0
    )
    return jnp.stack([near, far])


def shards(
    endpoints,
    projection,
    projection_bias,
    output_weight,
    output_bias,
    first_gain,
    first_shift,
    up_weight,
    up_bias,
    down_weight,
    down_bias,
    second_gain,
    second_shift,
    segment_length,
):
    dp_size = lax.axis_size("dp")
    mats = (projection[0], output_weight[0], up_weight[0], down_weight[0])
    rows = (
        projection_bias, output_bias, first_gain, first_shift, up_bias, down_bias, second_gain,
        second_shift,
    )
    mix = mix_tables(segment_length[0])
    left, save, stat, y = run_forward(endpoints[0], mats, rows, mix)
    right, results, vec = run_backward(
        endpoints[0], save, stat, y, mats, (first_gain, second_gain), mix, 16 * dp_size
    )
    proj, out, up, down, small = reduce_gradients(left, right, vec, dp_size)
    small = small[:39].astype(jnp.float32)

    def vector(name):
        start, count = VECTORS[name]
        return small[start : start + count].reshape(1, count * UNIT)

    def whole(mat):
        return mat.astype(jnp.float32)[None]

    return (
        results[None], whole(proj), vector("bp"), whole(out), vector("bo"), vector("g1"),
        vector("h1"), whole(up), vector("bu"), whole(down), vector("bd"), vector("g2"),
        vector("h2"),
    )


def solution(mesh):
    in_specs = (
        P("section", "dp", None),
        P("section", None, None),
        P("section", None),
        P("section", None, None),
        P("section", None),
        P("section", None),
        P("section", None),
        P("section", None, None),
        P("section", None),
        P("section", None, None),
        P("section", None),
        P("section", None),
        P("section", None),
        P("dp"),
    )
    out_specs = (
        P("section", "dp", None),
        P("section", None, None),
        P("section", None),
        P("section", None, None),
        P("section", None),
        P("section", None),
        P("section", None),
        P("section", None, None),
        P("section", None),
        P("section", None, None),
        P("section", None),
        P("section", None),
        P("section", None),
    )
    return jax.shard_map(shards, mesh=mesh, in_specs=in_specs, out_specs=out_specs, check_vma=False)
```

time: 880 us -> 373 us (0.42); the launches traced: 870 us -> 373 us
  matrix products: 255 us -> 0 us
  local copies, waits for them, and re-layouts: 261 us -> 6.83 us
  Pallas kernels: 214 us -> 344 us
  other arithmetic: 122 us -> 20.1 us
  starting transfers between devices: 9.08 us -> 0 us
    dot_general x39 -> x0, matrix products: 255 us -> none  [the longest x12 63.9 us: back_product(): lax.dot_general(grad_mat, weight_mat, (((1,), (1,)), ((), ())), preferred...]
    pallas_call x0 -> x2, Pallas kernels: none -> 132 us  [the longest x1 81.9 us: run_backward(): pl.pallas_call(partial(backward_kernel, chunks), out_shape=[jax.ShapeDtyp...]
    reshape x16 -> x0, local copies, waits for them, and re-layouts: 91.4 us -> none  [the longest x4 39.4 us: matrix(): blocks.reshape(down, across, UNIT, UNIT).transpose(0, 2, 1, 3)]
    slice x18 -> x0, local copies, waits for them, and re-layouts: 43.4 us -> none  [the longest x3 15.3 us: matrix(): blocks = summed[start * UNIT:(start + across * down) * UNIT]]
    another operation x4 -> x0, local copies, waits for them, and re-layouts: 40.7 us -> none  [shards(): return (answers,) + tuple((member[None] for member in summed_all))]
    select_n x11 -> x2, other arithmetic: 36.8 us -> 1.65 us  [the longest x1 0.94 us: mix_tables(): jnp.where(length > CHUNK, jnp.cos((later + CHUNK - earlier).astype(jnp.fl...]
    unnamed x346 -> x22, local copies, waits for them, and re-layouts: 40.7 us -> 6.83 us
    concatenate x4 -> x0, local copies, waits for them, and re-layouts: 33.3 us -> none  [the longest x2 33.3 us: chosen(): joined = jnp.concatenate(picked, axis=1)]
  transfers between devices with their start and end apart: 4 -> 0, of which waited for: 2 -> 0; matrix products, arithmetic and copies ran while one was open for 1% -> 0% of each run, Pallas kernels for 0% -> 0%
where the time goes in v2:
time: 373 us
  Pallas kernels  344 us (92%)
  other arithmetic  20.1 us (5%)
  local copies, waits for them, and re-layouts  6.83 us (2%)
    pallas_call x1, Pallas kernels, reduce_gradients(): pl.pallas_call(partial(reduce_kernel, dims, pieces, rows, units), out_sha...  212 us
    pallas_call x1, Pallas kernels, run_backward(): pl.pallas_call(partial(backward_kernel, chunks), out_shape=[jax.ShapeDtyp...  81.9 us
    pallas_call x1, Pallas kernels, run_forward(): pl.pallas_call(partial(forward_kernel, chunks), out_shape=[jax.ShapeDtype...  49.9 us
    broadcast_in_dim x4, other arithmetic, whole(): return mat.astype(jnp.float32)[None]  16.5 us

profile of v2, /device:TPU:0, one launch (start us, length us, event | category | flops | bytes accessed | tf_op | source)
XLA Modules:
  0.0 372.6 jit_solution(7145260564343859122)
XLA Ops:
  1.3 0.1 compare_and_fusion
  1.5 0.1 iota_divide_fusion
  1.6 0.7 cosine_select_fusion.1
  2.3 0.9 cosine_select_fusion
  3.3 0.8 pad_maximum_fusion.mix
  4.1 49.9 %forward.1 = (bf16[21,1024,256]{2,1,0:T(8,128)(2,1)}, bf16[1024,8448]{1,0:T(8,128)(2,1)}, f32[1024,1792]{1,0:T(8,128)}, f32[1024,768]{1,0:T(8,128)}) custom-call(bf16[1024,768]{1,0:T(8,128)(2,1)} %bitcast.63, bf16[768,2304]{1,0:T(8,128)(2,1)} %bitcast.60, bf16[768,768]{1,0:T(8,128)(2,1)} %bitcast.65, bf16[768,3072]{1,0:T(8,128)(2,1)} %bitcast.56, ...), custom_call_target="tpu_custom_call" | custom-call | tf_op jit(solution)/shard_map/forward/pallas_call | solution.py:583
  54.0 81.9 %backward.1 = (bf16[27,1024,256]{2,1,0:T(8,128)(2,1)}, f32[1024,768]{1,0:T(8,128)}, f32[256,256]{1,0:T(8,128)}) custom-call(bf16[1024,768]{1,0:T(8,128)(2,1)} %bitcast.64, bf16[1024,8448]{1,0:T(8,128)(2,1)} %get-tuple-element.25.save_hbm, f32[1024,1792]{1,0:T(8,128)} %get-tuple-element.26.stat_hbm, ...), custom_call_target="tpu_custom_call", output_to_operand_aliasing={{1}: (3, {})} | custom-call | tf_op jit(solution)/shard_map/backward/pallas_call | solution.py:875
  135.9 212.5 %reduce.1 = (bf16[768,2304]{1,0:T(8,128)(2,1)}, bf16[768,768]{1,0:T(8,128)(2,1)}, bf16[768,3072]{1,0:T(8,128)(2,1)}, bf16[3072,768]{1,0:T(8,128)(2,1)}, bf16[256,256]{1,0:T(8,128)(2,1)}) custom-call(bf16[21,1024,256]{2,1,0:T(8,128)(2,1)} %get-tuple-element.29.left_hbm, bf16[27,1024,256]{2,1,0:T(8,128)(2,1)} %get-tuple-element.30.right_hbm, ...), custom_call_target="tpu_custom_call" | custom-call | flops 14495514624 | bytes 125829120 | tf_op jit(solution)/shard_map/reduce/pallas_call | solution.py:299
  348.4 0.9 slice_convert_fusion
  349.3 0.6 copy.32
  349.9 0.6 copy.28
  350.5 0.6 copy.35
  351.1 0.6 copy.34
  351.7 0.6 copy.33
  352.2 0.6 copy.31
  352.8 0.6 copy.30
  353.4 0.6 copy.29
  354.0 2.8 bitcast_convert_fusion.3
  356.8 4.1 %bitcast_convert_fusion.2 = f32[1,768,2304]{2,1,0:T(8,128)} fusion(bf16[768,2304]{1,0:T(8,128)(2,1)S(1)} %copy-done.2), kind=kLoop, calls=%fused_computation.2 | loop fusion | flops 1769472 | bytes 10616832 | tf_op jit(solution)/shard_map/broadcast_in_dim | solution.py:962
  360.9 0.4 copy-done.1
  361.4 5.0 %bitcast_convert_fusion.1 = f32[1,768,3072]{2,1,0:T(8,128)} fusion(bf16[768,3072]{1,0:T(8,128)(2,1)S(1)} %copy-done.1), kind=kLoop, calls=%fused_computation.1 | loop fusion | flops 2359296 | bytes 14155776 | tf_op jit(solution)/shard_map/broadcast_in_dim | solution.py:962
  366.4 0.0 slice-done
  366.4 4.5 %bitcast_convert_fusion = f32[1,3072,768]{2,1,0:T(8,128)} fusion(bf16[3072,768]{1,0:T(8,128)(2,1)S(1)} %bitcast.68), kind=kLoop, calls=%fused_computation | loop fusion | flops 2359296 | bytes 14155776 | tf_op jit(solution)/shard_map/broadcast_in_dim | solution.py:962
  370.9 1.7 copy.39
  (13 shorter events, 0.0 us)
Async XLA Ops:
  348.4 8.5 %copy-start.2 = (bf16[768,2304]{1,0:T(8,128)(2,1)S(1)}, bf16[768,2304]{1,0:T(8,128)(2,1)}, u32[]{:S(2)}) copy-start(bf16[768,2304]{1,0:T(8,128)(2,1)} %get-tuple-element.32) | copy-start | bytes 10616836
  356.8 4.5 %copy-start.1 = (bf16[768,3072]{1,0:T(8,128)(2,1)S(1)}, bf16[768,3072]{1,0:T(8,128)(2,1)}, u32[]{:S(2)}) copy-start(bf16[768,3072]{1,0:T(8,128)(2,1)} %get-tuple-element.35) | copy-start | bytes 14155780
  356.8 9.6 %slice-start = ((s8[4718592]{0:T(1024)(128)(4,1)}), s8[4194304]{0:T(1024)(128)(4,1)S(1)}, s32[]{:S(2)}) async-start(s8[4718592]{0:T(1024)(128)(4,1)} %bitcast.67), calls=%async_computation | async-start | bytes 8388608
  361.4 5.1 %slice-start.1 = ((s8[4718592]{0:T(1024)(128)(4,1)}), s8[524288]{0:T(1024)(128)(4,1)S(1)}, s32[]{:S(2)}) async-start(s8[4718592]{0:T(1024)(128)(4,1)} %bitcast.67), calls=%async_computation.1 | async-start | bytes 1048576
  366.4 4.5 %copy-start = (f32[1024,768]{1,0:T(8,128)S(1)}, f32[1024,768]{1,0:T(8,128)}, u32[]{:S(2)}) copy-start(f32[1024,768]{1,0:T(8,128)} %get-tuple-element.28) | copy-start | bytes 9437188

commit v3 on v2

v3 whole, which is shorter than its diff:
```python
from functools import partial
import math

import jax
import jax.numpy as jnp
from jax import lax
from jax.experimental import pallas as pl
from jax.experimental.pallas import tpu as pltpu
from jax.sharding import PartitionSpec as P

HEADS = 12
EPSILON = 1e-05
MESH = pl.DeviceIdType.MESH


def rows_product(left_mat, right_mat):
    return lax.dot_general(
        left_mat, right_mat, (((0,), (0,)), ((), ())), preferred_element_type=jnp.float32
    )


def back_product(grad_mat, weight_mat):
    return lax.dot_general(
        grad_mat, weight_mat, (((1,), (1,)), ((), ())), preferred_element_type=jnp.float32
    )


def factor_dims(count):
    bits = count.bit_length() - 1
    return (1 << (bits // 3), 1 << ((bits + 1) // 3), 1 << ((bits + 2) // 3))


ORDERS = {"a": (0, 1, 2), "b": (1, 2, 0), "c": (2, 0, 1)}
PATTERN = "abacabc"
LAG = 3
OUT_LAG = 4
UNIT = 256
UNITS = 108
PIECE_ROWS = 512
SEM_SLOTS = 35


def stage_list(order, dims, rows):
    stages, size, landing = [], rows, 0
    for level, ax in enumerate(order):
        part = size // dims[ax]
        for step in range(1, dims[ax]):
            stages.append(("reduce", level, ax, step, part, landing))
            landing += part if dims[ax] == 2 else 2 * part
        size = part
    for level in reversed(range(3)):
        ax = order[level]
        for step in range(1, dims[ax]):
            stages.append(("gather", level, ax, step, size, 0))
        size *= dims[ax]
    return stages, landing


def unit_blocks(unit):
    up, out, proj = unit - 36, unit - 72, unit - 81
    left = jnp.where(
        unit < 36,
        unit // 3,
        jnp.where(unit < 72, 12 + up // 12, jnp.where(unit < 81, 15 + out // 3, 18 + proj // 9)),
    )
    right = jnp.where(
        unit < 36,
        unit % 3,
        jnp.where(unit < 72, 3 + up % 12, jnp.where(unit < 81, 15 + out % 3, 18 + proj % 9)),
    )
    return left, right


def axis_places(dims):
    here = lax.axis_index("dp")
    strides = (1, dims[0], dims[0] * dims[1])
    return here, strides, [(here // strides[ax]) % dims[ax] for ax in range(3)]


def greet_axes(dims, semaphore):
    here, strides, place = axis_places(dims)
    around = 0
    for ax in range(3):
        for sign, can in ((1, place[ax] < dims[ax] - 1), (-1, place[ax] > 0)):
            @pl.when(can)
            def _():
                pl.semaphore_signal(
                    semaphore, inc=1, device_id={"dp": here + sign * strides[ax]},
                    device_id_type=MESH,
                )
            around = around + can.astype(jnp.int32)
    return around


def gather_sends(spot, count):
    found = {}
    for at in range(count):
        sent = (at + 1 if at < count - 1 else 0) + (count - at if at > 0 else 0)
        found.setdefault(sent, []).append(spot == at)
    options = []
    for sent, spots in found.items():
        can = spots[0]
        for other in spots[1:]:
            can = jnp.logical_or(can, other)
        options.append((can, sent))
    return options


def guarded(can, action):
    if can is None:
        action()
    else:
        pl.when(can)(action)


def summing(dims, pieces, rows, acc, acc_slots, full, full_slots, landing, land_slots, left_hbm,
            right_hbm, vec, outs, left_ring, right_ring, load_sem, out_sem, send_sem, recv_sem):
    here, strides, place = axis_places(dims)
    proj_hbm, out_hbm, up_hbm, down_hbm, small_hbm = outs
    ring, chunks = left_ring.shape[0], left_ring.shape[1]
    per_piece = rows // UNIT
    land_rows = landing.shape[0] // land_slots
    plans = {name: stage_list(order, dims, rows)[0] for name, order in ORDERS.items()}
    n_stages = len(plans["a"])
    shard = rows // (dims[0] * dims[1] * dims[2])
    period = len(PATTERN)

    bases = {}
    for name, order in ORDERS.items():
        base, size, found = 0, rows, []
        for ax in order:
            found.append(base)
            size = size // dims[ax]
            base = base + place[ax] * size
        bases[name] = found + [base]

    sent_rows = {}
    for name, plan in plans.items():
        sure, options = 0, [(None, 0)]
        for kind, _, ax, step, part, _ in plan:
            if dims[ax] == 2 or kind == "reduce":
                sure += part
            elif step == 1:
                options = [
                    (can if other is None else jnp.logical_and(can, other), more + part * count)
                    for other, more in options
                    for can, count in gather_sends(place[ax], dims[ax])
                ]
        sent_rows[name] = [(can, sure + more) for can, more in options]

    def view(ref, slot, start, size):
        across = ref.shape[1] // UNIT
        first = pl.multiple_of(slot // across * rows + start, 16)
        if across == 1:
            return ref.at[pl.ds(first, size)]
        return ref.at[pl.ds(first, size), pl.ds(pl.multiple_of(slot % across * UNIT, UNIT), UNIT)]

    def loads(unit):
        slot = unit % ring
        left, right = unit_blocks(unit)
        return (
            pltpu.make_async_copy(left_hbm.at[left], left_ring.at[slot], load_sem.at[slot, 0]),
            pltpu.make_async_copy(right_hbm.at[right], right_ring.at[slot], load_sem.at[slot, 1]),
        )

    def prime():
        for unit in range(ring):
            for copy in loads(jnp.int32(unit)):
                copy.start()

    def form(piece, sub):
        unit = piece * per_piece + sub
        target = view(acc, piece % acc_slots, sub * UNIT, UNIT)

        @pl.when(unit < UNITS)
        def _():
            for copy in loads(unit):
                copy.wait()
            slot = unit % ring
            tokens = chunks * left_ring.shape[2]
            target[...] = rows_product(
                left_ring[slot].reshape(tokens, UNIT), right_ring[slot].reshape(tokens, UNIT)
            ).astype(jnp.bfloat16)

            @pl.when(unit + ring < UNITS)
            def _():
                for copy in loads(unit + ring):
                    copy.start()

        @pl.when(unit >= UNITS)
        def _():
            target[...] = vec[sub * UNIT : (sub + 1) * UNIT, :].astype(jnp.bfloat16)

    def copies(name, stage, piece):
        kind, level, ax, step, part, land = plans[name][stage]
        count, spot = dims[ax], place[ax]
        slot = piece % SEM_SLOTS
        held, index = (acc, piece % acc_slots) if kind == "reduce" else (full, piece % full_slots)
        land_start = piece % land_slots * land_rows + land

        def chunk(q):
            return view(held, index, bases[name][level] + q * part, part)

        def landed(way):
            return landing.at[pl.ds(pl.multiple_of(land_start + way * part, 16), part)]

        def remote(src, dst, way, sign):
            return lambda: pltpu.make_async_remote_copy(
                src_ref=src, dst_ref=dst, send_sem=send_sem.at[slot],
                recv_sem=recv_sem.at[slot, stage, way],
                device_id={"dp": here + sign * strides[ax]}, device_id_type=MESH,
            )

        sends, receives = [], []
        if count == 2:
            sign = 1 - 2 * spot
            mine, other = spot, 1 - spot
            if kind == "reduce":
                sends.append((None, remote(chunk(other), landed(0), 0, sign)))
                receives.append((None, remote(chunk(mine), landed(0), 0, sign), mine, landed(0)))
            else:
                sends.append((None, remote(chunk(mine), chunk(mine), 0, sign)))
                receives.append((None, remote(chunk(other), chunk(other), 0, sign), other, None))
            return sends, receives, chunk
        back = count - 1 - spot
        if kind == "reduce":
            for way, sign, can, q in (
                (0, 1, spot < step, spot + count - step),
                (1, -1, back < step, step - 1 - back),
            ):
                q = jnp.clip(q, 0, count - 1)
                sends.append((can, remote(chunk(q), landed(way), way, sign)))
            for way, sign, can, q in (
                (0, 1, jnp.logical_and(spot >= 1, spot - 1 < step), spot - 1 + count - step),
                (1, -1, jnp.logical_and(back >= 1, back - 1 < step), step - back),
            ):
                q = jnp.clip(q, 0, count - 1)
                receives.append((can, remote(chunk(q), landed(way), way, sign), q, landed(way)))
        else:
            for way, sign, can, q in (
                (0, 1, jnp.logical_and(back >= 1, spot >= step - 1), spot - step + 1),
                (1, -1, jnp.logical_and(spot >= 1, back >= step - 1), spot + step - 1),
            ):
                q = jnp.clip(q, 0, count - 1)
                sends.append((can, remote(chunk(q), chunk(q), way, sign)))
            for way, sign, can, q in (
                (0, 1, spot >= step, spot - step),
                (1, -1, back >= step, spot + step),
            ):
                q = jnp.clip(q, 0, count - 1)
                receives.append((can, remote(chunk(q), chunk(q), way, sign), q, None))
        return sends, receives, chunk

    def out_copies(piece, action):
        for sub in range(per_piece):
            unit = piece * per_piece + sub
            source = view(full, piece % full_slots, sub * UNIT, UNIT)
            for begin, end, across, target in (
                (0, 36, 3, down_hbm), (36, 72, 12, up_hbm), (72, 81, 3, out_hbm),
                (81, 108, 9, proj_hbm), (108, 108 + per_piece, 1, small_hbm),
            ):
                @pl.when(jnp.logical_and(unit >= begin, unit < end))
                def _():
                    local = jnp.clip(unit - begin, 0, end - begin - 1)
                    place_in = target.at[
                        pl.ds(pl.multiple_of(local // across * UNIT, UNIT), UNIT),
                        pl.ds(pl.multiple_of(local % across * UNIT, UNIT), UNIT),
                    ]
                    action(pltpu.make_async_copy(source, place_in, out_sem.at[unit]))

    def work(name, stage, piece):
        if stage > 0:
            sends, receives, chunk = copies(name, stage - 1, piece)
            for can, copy, q, landed in receives:
                def finish():
                    copy().wait_recv()
                    if landed is not None:
                        block = chunk(q)
                        block[...] = block[...] + landed[...]
                guarded(can, finish)
        if stage == n_stages // 2:
            mine = bases[name][3]
            own = view(full, piece % full_slots, mine, shard)
            own[...] = view(acc, piece % acc_slots, mine, shard)[...]
        if stage < n_stages:
            for can, copy in copies(name, stage, piece)[0]:
                guarded(can, lambda: copy().start())
        else:
            out_copies(piece, lambda copy: copy.start())
        if stage == n_stages:
            for can, amount in sent_rows[name]:
                sent = landing.at[pl.ds(0, amount)]
                guarded(
                    can,
                    lambda: pltpu.make_async_copy(
                        sent, sent, send_sem.at[piece % SEM_SLOTS]
                    ).wait(),
                )

    def tick(now):
        oldest = now - n_stages * LAG - OUT_LAG

        @pl.when(jnp.logical_and(oldest >= 0, oldest < pieces))
        def _():
            out_copies(jnp.clip(oldest, 0, pieces - 1), lambda copy: copy.wait())

        for stage in reversed(range(n_stages + 1)):
            piece = now - stage * LAG
            alive = jnp.logical_and(piece >= 0, piece < pieces)
            piece = jnp.clip(piece, 0, pieces - 1)
            spot_in = piece % period

            def on(name):
                found = False
                for n in range(period):
                    if PATTERN[n] == name:
                        found = jnp.logical_or(found, spot_in == n)
                return found

            if stage == 0:
                @pl.when(alive)
                def _():
                    for sub in range(per_piece):
                        form(piece, sub)

            for name in ORDERS:
                @pl.when(jnp.logical_and(alive, on(name)))
                def _():
                    work(name, stage, piece)

    return prime, tick, pieces + n_stages * LAG + OUT_LAG


def sum_sizes(dp_size):
    dims = factor_dims(dp_size)
    rows = max(PIECE_ROWS, 16 * dp_size)
    land = max(stage_list(order, dims, rows)[1] for order in ORDERS.values())
    return dims, rows, -(-(UNITS + 1) * UNIT // rows), land, 2 * (sum(dims) - 3)


def sum_out_shapes(rows):
    return [
        jax.ShapeDtypeStruct(shape, jnp.bfloat16)
        for shape in ((768, 2304), (768, 768), (768, 3072), (3072, 768), (rows, UNIT))
    ]


def sum_semaphores(ring, rows, pieces, stages):
    return [
        pltpu.SemaphoreType.DMA((ring, 2)),
        pltpu.SemaphoreType.DMA((pieces * rows // UNIT,)),
        pltpu.SemaphoreType.DMA((SEM_SLOTS,)),
        pltpu.SemaphoreType.DMA((SEM_SLOTS, stages, 2)),
    ]


def reduce_kernel(dims, pieces, rows, left_hbm, right_hbm, vec, proj_hbm, out_hbm, up_hbm, down_hbm,
                  small_hbm, acc, full, landing, left_ring, right_ring, load_sem, out_sem, send_sem,
                  recv_sem):
    barrier = pltpu.get_barrier_semaphore()
    around = greet_axes(dims, barrier)
    pl.semaphore_wait(barrier, around)
    slots = acc.shape[0] // rows
    prime, tick, ticks = summing(
        dims, pieces, rows, acc, slots, full, pieces, landing, slots, left_hbm, right_hbm,
        vec, (proj_hbm, out_hbm, up_hbm, down_hbm, small_hbm), left_ring, right_ring, load_sem,
        out_sem, send_sem, recv_sem,
    )
    prime()

    def body(now, carry):
        tick(now)
        return carry

    lax.fori_loop(0, ticks, body, 0)


def reduce_gradients(left, right, vec, dp_size):
    dims, rows, pieces, land, stages = sum_sizes(dp_size)
    ring = 4 if dp_size <= 16 else 2
    slots = min(SEM_SLOTS, pieces)
    return pl.pallas_call(
        partial(reduce_kernel, dims, pieces, rows),
        out_shape=sum_out_shapes(rows),
        in_specs=any_specs(2) + vmem_specs(1),
        out_specs=any_specs(5),
        scratch_shapes=[
            pltpu.VMEM((slots * rows, UNIT), jnp.bfloat16),
            pltpu.VMEM((pieces * rows, UNIT), jnp.bfloat16),
            pltpu.VMEM((slots * land, UNIT), jnp.bfloat16),
            pltpu.VMEM((ring,) + left.shape[1:], jnp.bfloat16),
            pltpu.VMEM((ring,) + left.shape[1:], jnp.bfloat16),
        ]
        + sum_semaphores(ring, rows, pieces, stages),
        compiler_params=pltpu.CompilerParams(
            collective_id=1, has_side_effects=True, vmem_limit_bytes=62 << 20
        ),
        name="reduce",
    )(left, right, vec)


CHUNK = 256
KEEP_A = {"slope": 0, "u1": 3072, "u2": 3840}
KEEP_A_WIDTH = 4608
STAT_A = {"rden": 0, "s1": 768, "s2": 896}
STAT_A_WIDTH = 1024
KEEP_B = {"q": 0, "k": 768, "sq": 1536, "sk": 2304, "v": 3072}
KEEP_B_WIDTH = 3840
VECTORS = {
    "bp": (0, 9), "bo": (9, 3), "g1": (12, 3), "h1": (15, 3), "bu": (18, 12), "bd": (30, 3), "g2": (33, 3),
    "h2": (36, 3),
}
TAIL_SCALE = 0.375
TAIL_POLY = (
    0.21141059805705423,
    0.21471795439954675,
    0.17184958530833144,
    0.26915459919947066,
    -0.10973686091480542,
    0.37354383408912983,
    -0.13093832475477368,
)


def dot(left_mat, right_mat):
    return jnp.dot(left_mat, right_mat, preferred_element_type=jnp.float32)


def inverse(value):
    rough = pl.reciprocal(value, approx=True)
    return rough * (2.0 - value * rough)


def gelu_pair(hidden):
    bell = jnp.exp(hidden * hidden * -0.5)
    t = inverse(1.0 + (TAIL_SCALE * math.sqrt(0.5)) * jnp.abs(hidden))
    poly = jnp.full_like(t, 0.5 * TAIL_POLY[-1])
    for coefficient in TAIL_POLY[-2::-1]:
        poly = poly * t + 0.5 * coefficient
    tail = poly * t * bell
    below = jnp.where(hidden >= 0, 1.0 - tail, tail)
    return hidden * below, below + hidden * (bell * (1.0 / math.sqrt(2.0 * math.pi)))


def softplus_pair(value):
    small = jnp.exp(-jnp.abs(value))
    whole = 1.0 + small
    log_whole = jnp.where(
        small < 1e-2, small * (1.0 - small * (0.5 - small * (1.0 / 3.0))), jnp.log(whole)
    )
    return (
        jnp.maximum(value, 0.0) + log_whole,
        jnp.where(value >= 0, 1.0, small) * inverse(whole),
    )


def centred(rows):
    centre = rows - jnp.mean(rows, axis=-1, keepdims=True)
    scaling = lax.rsqrt(jnp.mean(centre * centre, axis=-1, keepdims=True) + EPSILON)
    return centre * scaling, scaling


def wide(column, width=128):
    return jnp.broadcast_to(column, (column.shape[0], width))


def first_half(rows):
    return lax.broadcasted_iota(jnp.int32, (rows, 128), 1) < 64


def row(ref):
    return ref[...].astype(jnp.float32)


def any_specs(count):
    return [pl.BlockSpec(memory_space=pl.ANY)] * count


def vmem_specs(count):
    return [pl.BlockSpec(memory_space=pltpu.VMEM)] * count


def norm_back(grad, unit_rows, scaling):
    mean_grad = jnp.mean(grad, axis=-1, keepdims=True)
    mean_cross = jnp.mean(grad * unit_rows, axis=-1, keepdims=True)
    return scaling * (grad - mean_grad - unit_rows * mean_cross)


def layers_kernel(chunks, *refs):
    (ends_hbm, wp_hbm, wo_hbm, wu_hbm, wd_hbm, bp, bo, g1, h1, bu, bd, g2, h2, mix) = refs[:14]
    left_hbm, right_hbm = refs[14:16]
    own_hbm, peer_hbm, peer_w_hbm = refs[16:20], refs[20:24], refs[24:28]
    res_hbm, vec_out = refs[28:30]
    (wp, wo, wu, wd, x_in, e_in, handed, left, right, keep_a, stat_a, keep_b, stat_b, rows_out, nums, dq,
     dk, dv, carry_k, carry_v, dn1, weighed, vec, vec_sent, vec_peer, gains, gains_peer, w_sem, x_sem, xo_sem, e_sem, left_sem,
     right_sem, load_sem, res_sem, send_f, recv_f, send_b, recv_b, send_w, recv_w, send_e, recv_e,
     send_k, recv_k, send_r, recv_r, send_v, recv_v, send_g, recv_g) = refs[30:]

    section = lax.axis_index("section")
    first = section == 0
    second = jnp.logical_not(first)
    partner = {"section": 1 - section}
    width = ends_hbm.shape[1]
    pairs = width // 128
    half = chunks // 2
    mats_hbm, mats = (wp_hbm, wo_hbm, wu_hbm, wd_hbm), (wp, wo, wu, wd)
    kept_bufs = (keep_a, stat_a, keep_b, stat_b)

    def w_copy(which, sources=mats_hbm):
        return pltpu.make_async_copy(sources[which], mats[which], w_sem.at[which])

    def remote(src, dst, send, recv):
        return pltpu.make_async_remote_copy(
            src_ref=src, dst_ref=dst, send_sem=send, recv_sem=recv, device_id=partner,
            device_id_type=MESH,
        )

    def w_push(which):
        return remote(mats_hbm[which], peer_w_hbm[which], send_w.at[which], recv_w.at[which])

    def rows_of(i):
        return pl.ds(pl.multiple_of(i * CHUNK, CHUNK), CHUNK)

    def x_copy(i):
        return pltpu.make_async_copy(ends_hbm.at[rows_of(i)], x_in.at[i], x_sem.at[i])

    def x_out_copies(i):
        return [
            pltpu.make_async_copy(
                x_in.at[i, :, n * UNIT : (n + 1) * UNIT], left_hbm.at[18 + n, i], xo_sem.at[i, n]
            )
            for n in range(3)
        ]

    def e_copy(i):
        return pltpu.make_async_copy(ends_hbm.at[rows_of(i)], e_in.at[i], e_sem.at[i])

    def e_push(i):
        return remote(ends_hbm.at[rows_of(i)], e_in.at[i], send_e.at[i], recv_e.at[i])

    def hand_on(i):
        return remote(handed.at[i], x_in.at[i], send_f.at[i], recv_f.at[i])

    def hand_back(i):
        return remote(handed.at[i], e_in.at[i], send_b.at[i], recv_b.at[i])

    def left_copy(i):
        return pltpu.make_async_copy(left, left_hbm.at[0:18, i], left_sem)

    spans = ((0, 15), (15, 18), (18, 27))

    def right_copy(i, n):
        start, end = spans[n]
        return pltpu.make_async_copy(
            right.at[start:end], right_hbm.at[start:end, i], right_sem.at[n]
        )

    def right_push(i, n):
        start, end = spans[n]
        return remote(
            right.at[start:end], right_hbm.at[start:end, i], send_r.at[n], recv_r.at[i, n]
        )

    def save(i, slot, n):
        return pltpu.make_async_copy(
            kept_bufs[n].at[slot], own_hbm[n].at[rows_of(i)], load_sem.at[slot, n]
        )

    def push(i, slot, n):
        return remote(
            kept_bufs[n].at[slot], peer_hbm[n].at[rows_of(i)], send_k.at[i, n], recv_k.at[i, n]
        )

    def load(i, slot, n, source):
        return pltpu.make_async_copy(
            source[n].at[rows_of(i)], kept_bufs[n].at[slot], load_sem.at[slot, n]
        )

    def res_copy(i):
        return pltpu.make_async_copy(rows_out, res_hbm.at[rows_of(i)], res_sem)

    def own_gains():
        gains[0:1, :] = row(g1)
        gains[1:2, :] = row(g2)

    def gains_push():
        return remote(gains, gains_peer, send_g, recv_g)

    def vec_push():
        return remote(vec_sent, vec_peer, send_v, recv_v)

    @pl.when(first)
    def _():
        x_copy(0).start()

    for which in range(4):
        w_copy(which).start()

    @pl.when(first)
    def _():
        for i in range(1, chunks):
            x_copy(i).start()

    @pl.when(second)
    def _():
        for i in range(half, chunks):
            e_copy(i).start()

    barrier = pltpu.get_barrier_semaphore()
    pl.semaphore_signal(barrier, inc=1, device_id=partner, device_id_type=MESH)
    vec[...] = jnp.zeros_like(vec)
    gains[...] = jnp.zeros_like(gains)
    own_gains()
    pl.semaphore_wait(barrier, 1)

    @pl.when(second)
    def _():
        gains_push().start()
        for i in range(half):
            e_push(i).start()
        for which in (3, 2, 1, 0):
            w_push(which).start()

    def weights_ready(i, which):
        @pl.when(i == 0)
        def _():
            w_copy(which).wait()

    lanes = lax.broadcasted_iota(jnp.int32, (CHUNK, 128), 1)
    low = lanes < 64

    def forward_chunk(i, carry):
        slot = lax.rem(i, 2)

        @pl.when(i >= 2)
        def _():
            @pl.when(first)
            def _():
                for n in range(4):
                    save(i - 2, slot, n).wait()

            @pl.when(second)
            def _():
                for n in range(4):
                    push(i - 2, slot, n).wait_send()

        weights_ready(i, 0)

        @pl.when(first)
        def _():
            x_copy(i).wait()

        @pl.when(second)
        def _():
            hand_on(i).wait_recv()

        for copy in x_out_copies(i):
            copy.start()
        now_a, now_b, old_b = keep_a.at[slot], keep_b.at[slot], keep_b.at[1 - slot]

        def keep(ref, start, value):
            ref[:, start : start + value.shape[1]] = value.astype(jnp.bfloat16)

        def blocks(first_block, value):
            for n in range(value.shape[1] // UNIT):
                left[first_block + n] = value[:, n * UNIT : (n + 1) * UNIT]

        x = x_in[i]
        for part, (name, slope) in enumerate((("q", "sq"), ("k", "sk"))):
            cols = slice(part * width, (part + 1) * width)
            soft, sigma = softplus_pair(dot(x, wp[:, cols]) + row(bp)[:, cols])
            keep(now_b, KEEP_B[name], soft)
            keep(now_b, KEEP_B[slope], sigma)
        cols = slice(2 * width, 3 * width)
        keep(now_b, KEEP_B["v"], dot(x, wp[:, cols]) + row(bp)[:, cols])

        def mix_pair(pair, source, table, fresh):
            def cut(ref, name):
                return ref[:, KEEP_B[name] + pair * 128 : KEEP_B[name] + (pair + 1) * 128]

            queries, keys_in, values = cut(now_b, "q"), cut(source, "k"), cut(source, "v")
            zero, one = jnp.zeros_like(keys_in), jnp.ones_like(values)
            for half in range(2):
                own = low if half == 0 else jnp.logical_not(low)
                scores = back_product(queries, jnp.where(own, keys_in, zero)) * table
                num = dot(scores.astype(jnp.bfloat16), jnp.where(own, values, one))
                at = 2 * pair + half
                nums[at] = num if fresh else nums[at] + num

        for pair in range(pairs):
            mix_pair(pair, now_b, mix[0], True)

        @pl.when(slot == 1)
        def _():
            for pair in range(pairs):
                mix_pair(pair, old_b, mix[1], False)

        @pl.when(i >= 1)
        def _():
            left_copy(i - 1).wait()

        for pair in range(pairs):
            num_a, num_b = nums[2 * pair], nums[2 * pair + 1]
            inv = inverse(
                jnp.where(low, pltpu.roll(num_a, 64, 1), pltpu.roll(num_b, 64, 1))
            )
            span = slice(pair * 128, (pair + 1) * 128)
            stat_b[slot, :, span] = jnp.where(low, num_a, num_b) * inv
            stat_a[slot, :, span] = inv
        blocks(15, stat_b[slot].astype(jnp.bfloat16))
        weights_ready(i, 1)
        first_sum = x.astype(jnp.float32) + row(bo)
        for n in range(3):
            first_sum += dot(left[15 + n], wo[n * UNIT : (n + 1) * UNIT, :])
        unit_one, scale_one = centred(first_sum)
        keep(now_a, KEEP_A["u1"], unit_one)
        stat_a[slot, :, STAT_A["s1"] : STAT_A["s1"] + 128] = wide(scale_one)
        normed = unit_one * row(g1) + row(h1)
        resid = dn1
        resid[...] = normed + row(bd)
        up_in = normed.astype(jnp.bfloat16)
        blocks(12, up_in)
        weights_ready(i, 2)

        def hidden_of(n):
            cols = slice(n * width, (n + 1) * width)
            return dot(up_in, wu[:, cols]) + row(bu)[:, cols]

        hidden = hidden_of(0)
        for n in range(4):
            later = hidden_of(n + 1) if n < 3 else None
            active, slope = gelu_pair(hidden)
            active = active.astype(jnp.bfloat16)
            blocks(3 * n, active)
            keep(now_a, n * width, slope)
            if n == 0:
                weights_ready(i, 3)
            resid[...] += dot(active, wd[n * width : (n + 1) * width, :])
            hidden = later
        unit_two, scale_two = centred(resid[...])
        keep(now_a, KEEP_A["u2"], unit_two)
        stat_a[slot, :, STAT_A["s2"] : STAT_A["s2"] + 128] = wide(scale_two)
        result = unit_two * row(g2) + row(h2)

        @pl.when(first)
        def _():
            handed[i] = result.astype(jnp.bfloat16)
            hand_on(i).start()

        @pl.when(second)
        def _():
            @pl.when(i >= 1)
            def _():
                res_copy(i - 1).wait()

            rows_out[...] = result
            res_copy(i).start()

        left_copy(i).start()

        @pl.when(first)
        def _():
            for n in range(4):
                save(i, slot, n).start()

        @pl.when(jnp.logical_and(second, i < half))
        def _():
            for n in range(4):
                push(i, slot, n).start()

        return carry

    lax.fori_loop(0, chunks, forward_chunk, 0)
    left_copy(chunks - 1).wait()
    for i in range(chunks):
        for copy in x_out_copies(i):
            copy.wait()

    @pl.when(first)
    def _():
        for i in range(half, chunks):
            for n in range(4):
                save(i, i % 2, n).wait()
        for which in (3, 2, 1, 0):
            w_push(which).wait_recv()
            w_copy(which, peer_w_hbm).start()
        for i in (1, 0):
            for n in range(4):
                push(i, i, n).wait_recv()
                load(i, i, n, peer_hbm).start()
        for i in range(chunks):
            hand_on(i).wait_send()

    @pl.when(second)
    def _():
        res_copy(chunks - 1).wait()
        for i in range(half):
            e_push(i).wait_send()
        gains_push().wait_send()
        for which in range(4):
            w_push(which).wait_send()

    def tally(name, start, values):
        total = jnp.sum(values.astype(jnp.float32), axis=0, keepdims=True)
        at = VECTORS[name][0] + start // UNIT
        for n in range(values.shape[1] // UNIT):
            vec[at + n : at + n + 1, :] += total[:, n * UNIT : (n + 1) * UNIT]

    def right_blocks(first_block, value):
        for n in range(value.shape[1] // UNIT):
            right[first_block + n] = value[:, n * UNIT : (n + 1) * UNIT]

    turns = jnp.where(first, chunks + half, half)

    def chunk_of(turn):
        late = jnp.where(first, turn >= chunks, True)
        return 1 - lax.rem(turn, 2) + jnp.where(late, half, 0)

    def loads(turn, some, action):
        for peers in (True, False):
            @pl.when((turn < half) if peers else (turn >= half))
            def _():
                i = chunk_of(turn)
                for n in some:
                    action(load(i, lax.rem(i, 2), n, peer_hbm if peers else own_hbm))

    def right_done(turn, n):
        i = chunk_of(turn)

        @pl.when(jnp.logical_and(first, turn < half))
        def _():
            right_push(i, n).wait_send()

        @pl.when(jnp.logical_not(jnp.logical_and(first, turn < half)))
        def _():
            right_copy(i, n).wait()

    def right_go(turn, n):
        i = chunk_of(turn)

        @pl.when(jnp.logical_and(first, turn < half))
        def _():
            right_push(i, n).start()

        @pl.when(jnp.logical_not(jnp.logical_and(first, turn < half)))
        def _():
            right_copy(i, n).start()

    def tail_part(turn, i):
        slot = lax.rem(i, 2)

        @pl.when(first)
        def _():
            loads(turn, (0, 1), lambda copy: copy.wait())

            @pl.when(turn < half)
            def _():
                e_push(i).wait_recv()

            @pl.when(turn == 0)
            def _():
                gains_push().wait_recv()
                gains[...] = gains_peer[...]

            @pl.when(turn == half)
            def _():
                own_gains()

            @pl.when(turn >= chunks)
            def _():
                hand_back(i).wait_recv()

        @pl.when(second)
        def _():
            e_copy(i).wait()

        @pl.when(turn >= 1)
        def _():
            for n in range(2):
                right_done(turn - 1, n)

        def ready(which):
            @pl.when(jnp.logical_and(first, jnp.logical_or(turn == 0, turn == half)))
            def _():
                w_copy(which).wait()

        now_a, total = keep_a.at[slot], dn1

        def kept(name, start=0):
            at = KEEP_A[name] + start
            return now_a[:, at : at + width].astype(jnp.float32)

        e = e_in[i].astype(jnp.float32)
        unit_two = kept("u2")
        tally("g2", 0, e * unit_two)
        tally("h2", 0, e)
        second_full = norm_back(
            e * gains[1:2, :], unit_two, stat_a[slot, :, STAT_A["s2"] : STAT_A["s2"] + 1]
        )
        second_low = second_full.astype(jnp.bfloat16)
        right_blocks(0, second_low)
        tally("bd", 0, second_low)
        total[...] = second_full

        ready(3)

        def pulled(n):
            return back_product(second_low, wd[n * width : (n + 1) * width, :])

        grad = pulled(0)
        for n in range(4):
            later = pulled(n + 1) if n < 3 else None
            hidden_low = (grad * kept("slope", n * width)).astype(jnp.bfloat16)
            right_blocks(3 + 3 * n, hidden_low)
            tally("bu", n * width, hidden_low)
            if n == 0:
                ready(2)
            total[...] += back_product(hidden_low, wu[:, n * width : (n + 1) * width])
            grad = later
        right_go(turn, 0)
        grad_normed = total[...]
        unit_one = kept("u1")
        tally("g1", 0, grad_normed * unit_one)
        tally("h1", 0, grad_normed)
        grad_first = norm_back(
            grad_normed * gains[0:1, :], unit_one, stat_a[slot, :, STAT_A["s1"] : STAT_A["s1"] + 1]
        )
        total[...] = grad_first
        first_low = grad_first.astype(jnp.bfloat16)
        right_blocks(15, first_low)
        right_go(turn, 1)
        tally("bo", 0, first_low)
        ready(1)
        grad_mixed = back_product(first_low, wo[...]).astype(jnp.bfloat16).astype(jnp.float32)
        weighed[...] = (grad_mixed * stat_a[slot, :, 0:width]).astype(jnp.bfloat16)

        @pl.when(first)
        def _():
            @pl.when(turn + 2 < turns)
            def _():
                loads(turn + 2, (0, 1), lambda copy: copy.start())

            @pl.when(turn == half - 1)
            def _():
                for which in (3, 2, 1):
                    w_copy(which).start()

    def pair_part(i, pair):
        slot = lax.rem(i, 2)
        now_b, old_b = keep_b.at[slot], keep_b.at[1 - slot]
        span = pl.ds(pl.multiple_of(pair * 128, 128), 128)

        def cut(ref, name):
            return ref[:, pl.ds(pl.multiple_of(KEEP_B[name] + pair * 128, 128), 128)]

        def half_block(source, table):
            queries, keys_in, values = cut(now_b, "q"), cut(source, "k"), cut(source, "v")
            w = weighed[:, span]
            cross = w.astype(jnp.float32) * stat_b[slot, :, span]
            zero, one = jnp.zeros_like(keys_in), jnp.ones_like(values)
            total_q, total_k, total_v = 0.0, 0.0, 0.0
            for half in range(2):
                own = low if half == 0 else jnp.logical_not(low)
                spare = 64 * (1 - half)
                inner = jnp.sum(jnp.where(own, cross, 0.0), axis=-1, keepdims=True)
                rough = inner.astype(jnp.bfloat16).astype(jnp.float32)
                extra = jnp.where(
                    lanes == spare, -rough, jnp.where(lanes == spare + 1, rough - inner, 0.0)
                ).astype(jnp.bfloat16)
                own_keys = jnp.where(own, keys_in, zero)
                scores = (back_product(queries, own_keys) * table).astype(jnp.bfloat16)
                grads = (
                    back_product(
                        jnp.where(own, w, extra), jnp.where(own, values, one)
                    )
                    * table
                ).astype(jnp.bfloat16)
                total_q += dot(grads, own_keys)
                total_k += rows_product(grads, jnp.where(own, queries, zero))
                total_v += rows_product(scores, jnp.where(own, w, zero))
            return total_q, total_k, total_v

        total_q, total_k, total_v = half_block(now_b, mix[0])
        dq[:, span] = total_q
        dk[:, span] = total_k
        dv[:, span] = total_v

        @pl.when(slot == 0)
        def _():
            dk[:, span] += carry_k[:, span]
            dv[:, span] += carry_v[:, span]

        @pl.when(slot == 1)
        def _():
            far_q, far_k, far_v = half_block(old_b, mix[1])
            dq[:, span] += far_q
            carry_k[:, span] = far_k
            carry_v[:, span] = far_v

    def head_part(turn, i):
        slot = lax.rem(i, 2)

        @pl.when(turn >= 1)
        def _():
            right_done(turn - 1, 2)

        @pl.when(jnp.logical_and(first, jnp.logical_or(turn == 0, turn == half)))
        def _():
            w_copy(0).wait()

        now_b = keep_b.at[slot]
        grad_in = dn1[...]
        for n, (source, slope) in enumerate(((dq, "sq"), (dk, "sk"), (dv, None))):
            values = source[...]
            if slope:
                at = KEEP_B[slope]
                values = values * now_b[:, at : at + width].astype(jnp.float32)
            values = values.astype(jnp.bfloat16)
            right_blocks(18 + 3 * n, values)
            tally("bp", n * width, values)
            grad_in += back_product(values, wp[:, n * width : (n + 1) * width])
        right_go(turn, 2)

        @pl.when(first)
        def _():
            @pl.when(turn < half)
            def _():
                e_in[i] = grad_in.astype(jnp.bfloat16)

            @pl.when(turn >= half)
            def _():
                @pl.when(turn > half)
                def _():
                    res_copy(chunk_of(turn - 1)).wait()

                rows_out[...] = grad_in
                res_copy(i).start()

            @pl.when(turn + 2 < turns)
            def _():
                loads(turn + 2, (2, 3), lambda copy: copy.start())

            @pl.when(turn == half - 1)
            def _():
                w_copy(0).start()
                vec_sent[...] = vec[0:40, :]
                vec_push().start()
                vec[...] = jnp.zeros_like(vec)

        @pl.when(second)
        def _():
            handed[i] = grad_in.astype(jnp.bfloat16)
            hand_back(i).start()

    def one_turn(turn, carry):
        i = chunk_of(turn)
        tail_part(turn, i)

        @pl.when(jnp.logical_and(first, lax.rem(turn, 2) == 0))
        def _():
            loads(turn, (2, 3), lambda copy: copy.wait())
            loads(turn + 1, (2, 3), lambda copy: copy.wait())

        def one_pair(pair, inner):
            pair_part(i, pair)
            return inner

        lax.fori_loop(0, pairs, one_pair, 0)
        head_part(turn, i)
        return carry

    lax.fori_loop(0, turns, one_turn, 0)
    for n in range(3):
        right_copy(half, n).wait()

    @pl.when(first)
    def _():
        res_copy(half).wait()
        vec_push().wait_send()

    @pl.when(second)
    def _():
        for i in range(half, chunks):
            hand_back(i).wait_send()
        vec_push().wait_recv()
        vec[0:40, :] += vec_peer[...]
        for i in range(half):
            for n in range(3):
                right_push(i, n).wait_recv()

    vec_out[...] = vec[...]


def run_layers(ends, mats, rows_in, mix, dp_size):
    tokens, width = ends.shape
    chunks = tokens // CHUNK
    rows = sum_sizes(dp_size)[1]
    bf16, f32 = jnp.bfloat16, jnp.float32

    def kept(count):
        return [
            jax.ShapeDtypeStruct((count * CHUNK, columns), dtype)
            for columns, dtype in (
                (KEEP_A_WIDTH, bf16), (STAT_A_WIDTH, f32), (KEEP_B_WIDTH, bf16), (width, f32)
            )
        ]

    out_shape = (
        [
            jax.ShapeDtypeStruct((21, chunks, CHUNK, UNIT), bf16),
            jax.ShapeDtypeStruct((27, chunks, CHUNK, UNIT), bf16),
        ]
        + kept(chunks)
        + kept(chunks // 2)
        + [jax.ShapeDtypeStruct(mat.shape, mat.dtype) for mat in mats]
        + [
            jax.ShapeDtypeStruct((tokens, width), f32),
            jax.ShapeDtypeStruct((rows, UNIT), f32),
        ]
    )
    chunk_f32 = pltpu.VMEM((CHUNK, width), f32)
    all_rows = pltpu.VMEM((chunks, CHUNK, width), bf16)
    dma = pltpu.SemaphoreType.DMA
    outs = pl.pallas_call(
        partial(layers_kernel, chunks),
        out_shape=out_shape,
        in_specs=any_specs(5) + vmem_specs(9),
        out_specs=any_specs(15) + vmem_specs(1),
        scratch_shapes=[pltpu.VMEM(mat.shape, mat.dtype) for mat in mats]
        + [
            all_rows,
            all_rows,
            all_rows,
            pltpu.VMEM((18, CHUNK, UNIT), bf16),
            pltpu.VMEM((27, CHUNK, UNIT), bf16),
            pltpu.VMEM((2, CHUNK, KEEP_A_WIDTH), bf16),
            pltpu.VMEM((2, CHUNK, STAT_A_WIDTH), f32),
            pltpu.VMEM((2, CHUNK, KEEP_B_WIDTH), bf16),
            pltpu.VMEM((2, CHUNK, width), f32),
            chunk_f32,
            pltpu.VMEM((HEADS, CHUNK, 128), f32),
            chunk_f32,
            chunk_f32,
            chunk_f32,
            chunk_f32,
            chunk_f32,
            chunk_f32,
            pltpu.VMEM((CHUNK, width), bf16),
            pltpu.VMEM((rows, UNIT), f32),
            pltpu.VMEM((40, UNIT), f32),
            pltpu.VMEM((40, UNIT), f32),
            pltpu.VMEM((8, width), f32),
            pltpu.VMEM((8, width), f32),
            dma((4,)),
            dma((chunks,)),
            dma((chunks, 3)),
            dma((chunks,)),
            dma,
            dma((3,)),
            dma((2, 4)),
            dma,
            dma((chunks,)),
            dma((chunks,)),
            dma((chunks,)),
            dma((chunks,)),
            dma((4,)),
            dma((4,)),
            dma((chunks // 2,)),
            dma((chunks // 2,)),
            dma((chunks // 2, 4)),
            dma((chunks // 2, 4)),
            dma((3,)),
            dma((chunks // 2, 3)),
            dma,
            dma,
            dma,
            dma,
        ],
        compiler_params=pltpu.CompilerParams(
            collective_id=2, has_side_effects=True, vmem_limit_bytes=62 << 20
        ),
        name="layers",
    )(ends, *mats, *rows_in, mix)
    return outs[14], outs[0], outs[1], outs[15]


def widen_kernel(proj, out, up, down, small, *refs):
    sources = (proj, out, up, down)
    targets, vectors = refs[:4], refs[4:12]
    held, wide_held = refs[12:16], refs[16:20]
    in_sem, out_sem = refs[20:]
    blocks = []
    for which, source in enumerate(sources):
        step = 256 if source.shape[1] > 768 else 768
        for start in range(0, source.shape[0], step):
            blocks.append((which, pl.ds(start, step)))
    copies_in = [
        pltpu.make_async_copy(sources[which].at[span], held[which].at[span], in_sem.at[n])
        for n, (which, span) in enumerate(blocks)
    ]
    copies_out = [
        pltpu.make_async_copy(wide_held[which].at[span], targets[which].at[0, span], out_sem.at[n])
        for n, (which, span) in enumerate(blocks)
    ]
    for copy in copies_in:
        copy.start()
    for (start, count), vector in zip(VECTORS.values(), vectors):
        for n in range(count):
            vector[:, n * UNIT : (n + 1) * UNIT] = small[start + n : start + n + 1, :].astype(
                jnp.float32
            )
    for n, (which, span) in enumerate(blocks):
        copies_in[n].wait()
        wide_held[which][span, :] = held[which][span, :].astype(jnp.float32)
        copies_out[n].start()
    for copy in copies_out:
        copy.wait()


def widen(proj, out, up, down, small):
    mats = (proj, out, up, down)
    return pl.pallas_call(
        widen_kernel,
        out_shape=[jax.ShapeDtypeStruct((1,) + mat.shape, jnp.float32) for mat in mats]
        + [jax.ShapeDtypeStruct((1, count * UNIT), jnp.float32) for _, count in VECTORS.values()],
        in_specs=any_specs(4) + vmem_specs(1),
        out_specs=any_specs(4) + vmem_specs(8),
        scratch_shapes=[pltpu.VMEM(mat.shape, jnp.bfloat16) for mat in mats]
        + [pltpu.VMEM(mat.shape, jnp.float32) for mat in mats]
        + [pltpu.SemaphoreType.DMA((11,)), pltpu.SemaphoreType.DMA((11,))],
        compiler_params=pltpu.CompilerParams(vmem_limit_bytes=60 << 20),
        name="widen",
    )(proj, out, up, down, small)


def mix_tables(length):
    places = jnp.arange(2 * CHUNK, dtype=jnp.int32)
    angles = places.astype(jnp.float32) * ((0.5 * math.pi) / length.astype(jnp.float32))
    cosine, sine, document = lax.optimization_barrier(
        (jnp.cos(angles), jnp.sin(angles), places // length)
    )

    def table(start):
        later, earlier = slice(start, start + CHUNK), slice(0, CHUNK)
        seen = jnp.logical_and(
            document[later, None] == document[None, earlier],
            places[later, None] >= places[None, earlier],
        )
        near = cosine[later, None] * cosine[None, earlier] + sine[later, None] * sine[None, earlier]
        return jnp.where(seen, near, 0.0)

    return jnp.stack([table(0), table(CHUNK)])


def shards(
    endpoints,
    projection,
    projection_bias,
    output_weight,
    output_bias,
    first_gain,
    first_shift,
    up_weight,
    up_bias,
    down_weight,
    down_bias,
    second_gain,
    second_shift,
    segment_length,
):
    dp_size = lax.axis_size("dp")
    mats = (projection[0], output_weight[0], up_weight[0], down_weight[0])
    rows = (
        projection_bias, output_bias, first_gain, first_shift, up_bias, down_bias, second_gain,
        second_shift,
    )
    mix = mix_tables(segment_length[0])
    results, left, right, vec = run_layers(endpoints[0], mats, rows, mix, dp_size)
    sums = reduce_gradients(left, right, vec, dp_size)
    proj, out, up, down, bp, bo, g1, h1, bu, bd, g2, h2 = widen(*sums)
    return (results[None], proj, bp, out, bo, g1, h1, up, bu, down, bd, g2, h2)


def solution(mesh):
    in_specs = (
        P("section", "dp", None),
        P("section", None, None),
        P("section", None),
        P("section", None, None),
        P("section", None),
        P("section", None),
        P("section", None),
        P("section", None, None),
        P("section", None),
        P("section", None, None),
        P("section", None),
        P("section", None),
        P("section", None),
        P("dp"),
    )
    out_specs = (
        P("section", "dp", None),
        P("section", None, None),
        P("section", None),
        P("section", None, None),
        P("section", None),
        P("section", None),
        P("section", None),
        P("section", None, None),
        P("section", None),
        P("section", None, None),
        P("section", None),
        P("section", None),
        P("section", None),
    )
    return jax.shard_map(shards, mesh=mesh, in_specs=in_specs, out_specs=out_specs, check_vma=False)
```

time: 373 us -> 337 us (0.903)
  other arithmetic: 20.1 us -> 1.34 us
  Pallas kernels: 344 us -> 333 us
  local copies, waits for them, and re-layouts: 6.83 us -> 1.7 us
    broadcast_in_dim x4 -> x0, other arithmetic: 16.5 us -> none  [whole(): return mat.astype(jnp.float32)[None]]
    pallas_call x3, Pallas kernels: 344 us -> 333 us  [the longest x1 185 us: reduce_gradients(): pl.pallas_call(partial(reduce_kernel, dims, pieces, rows), out_shape=sum_...]
    unnamed x22 -> x3, local copies, waits for them, and re-layouts: 6.83 us -> 1.67 us
where the time goes in v3:
time: 337 us
  Pallas kernels  333 us (99%)
    pallas_call x1, Pallas kernels, reduce_gradients(): pl.pallas_call(partial(reduce_kernel, dims, pieces, rows), out_shape=sum_...  185 us
    pallas_call x1, Pallas kernels, run_layers(): pl.pallas_call(partial(layers_kernel, chunks), out_shape=out_shape, in_sp...  132 us
    pallas_call x1, Pallas kernels, widen(): pl.pallas_call(widen_kernel, out_shape=[jax.ShapeDtypeStruct((1,) + mat.s...  15.3 us

profile of v3, /device:TPU:0, one launch (start us, length us, event | category | flops | bytes accessed | tf_op | source)
XLA Modules:
  0.0 337.3 jit_solution(1021931011274435242)
XLA Ops:
  1.3 0.1 add_select_fusion.2
  1.6 0.3 add_select_fusion.1
  1.9 0.8 pad_maximum_fusion.refs_13_
  2.8 132.4 %layers.1 = (bf16[21,4,256,256]{3,2,1,0:T(8,128)(2,1)}, bf16[27,4,256,256]{3,2,1,0:T(8,128)(2,1)}, bf16[1024,4608]{1,0:T(8,128)(2,1)}, f32[1024,1024]{1,0:T(8,12...) custom-call(bf16[1024,768]{1,0:T(8,128)(2,1)} %bitcast.14, ...), custom_call_target="tpu_custom_call" | custom-call | tf_op jit(solution)/shard_map/layers/pallas_call | solution.py:1124
  135.2 185.1 %reduce.1 = (bf16[768,2304]{1,0:T(8,128)(2,1)}, bf16[768,768]{1,0:T(8,128)(2,1)}, bf16[768,3072]{1,0:T(8,128)(2,1)}, bf16[3072,768]{1,0:T(8,128)(2,1)}, bf16[512,256]{1,0:T(8,128)(2,1)}) custom-call(bf16[21,4,256,256]{3,2,1,0:T(8,128)(2,1)} %get-tuple-element.41.left_hbm, bf16[27,4,256,256]{3,2,1,0:T(8,128)(2,1)} %get-tuple-element.42.right_hbm, ...), custom_call_target="tpu_custom_call" | custom-call | tf_op jit(solution)/shard_map/reduce/pallas_call | solution.py:382
  320.3 0.0 copy-start
  320.3 15.3 %widen.1 = (f32[1,768,2304]{2,1,0:T(8,128)}, f32[1,768,768]{2,1,0:T(8,128)}, f32[1,768,3072]{2,1,0:T(8,128)}, f32[1,3072,768]{2,1,0:T(8,128)}, f32[1,2304]{1,0:T...) custom-call(bf16[768,2304]{1,0:T(8,128)(2,1)} %get-tuple-element.44., ...), custom_call_target="tpu_custom_call" | custom-call | tf_op jit(solution)/shard_map/widen/pallas_call | solution.py:1222
  335.6 0.0 copy-done
  335.6 1.7 copy.29
  (8 shorter events, 0.1 us)
Async XLA Ops:
  320.3 15.3 %copy-start = (f32[1024,768]{1,0:T(8,128)S(1)}, f32[1024,768]{1,0:T(8,128)}, u32[]{:S(2)}) copy-start(f32[1024,768]{1,0:T(8,128)} %get-tuple-element.40) | copy-start | bytes 9437188

commit v4 on v3

--- a/solution.py
+++ b/solution.py
@@ -33,6 +33,7 @@
 ORDERS = {"a": (0, 1, 2), "b": (1, 2, 0), "c": (2, 0, 1)}
 PATTERN = "abacabc"
 LAG = 3
+END_LAG = 4
 OUT_LAG = 4
 UNIT = 256
 UNITS = 108
@@ -297,38 +298,40 @@
                     ).wait(),
                 )
 
-    def tick(now):
-        oldest = now - n_stages * LAG - OUT_LAG
-
-        @pl.when(jnp.logical_and(oldest >= 0, oldest < pieces))
-        def _():
-            out_copies(jnp.clip(oldest, 0, pieces - 1), lambda copy: copy.wait())
-
-        for stage in reversed(range(n_stages + 1)):
-            piece = now - stage * LAG
-            alive = jnp.logical_and(piece >= 0, piece < pieces)
-            piece = jnp.clip(piece, 0, pieces - 1)
-            spot_in = piece % period
-
-            def on(name):
-                found = False
-                for n in range(period):
-                    if PATTERN[n] == name:
-                        found = jnp.logical_or(found, spot_in == n)
-                return found
-
-            if stage == 0:
-                @pl.when(alive)
+    starts = [0]
+    for stage in range(n_stages):
+        starts.append(starts[-1] + (END_LAG if stage in (0, n_stages - 1) else LAG))
+    total_ticks = pieces + starts[-1] + OUT_LAG
+
+    def run():
+        prime()
+
+        def some_ticks(turn, carry):
+            for spot_in in range(period):
+                now = turn * period + spot_in
+                oldest = now - starts[-1] - OUT_LAG
+
+                @pl.when(jnp.logical_and(oldest >= 0, oldest < pieces))
                 def _():
-                    for sub in range(per_piece):
-                        form(piece, sub)
-
-            for name in ORDERS:
-                @pl.when(jnp.logical_and(alive, on(name)))
-                def _():
-                    work(name, stage, piece)
-
-    return prime, tick, pieces + n_stages * LAG + OUT_LAG
+                    out_copies(jnp.clip(oldest, 0, pieces - 1), lambda copy: copy.wait())
+
+                for stage in reversed(range(n_stages + 1)):
+                    piece = now - starts[stage]
+                    name = PATTERN[(spot_in - starts[stage]) % period]
+
+                    @pl.when(jnp.logical_and(piece >= 0, piece < pieces))
+                    def _():
+                        at = jnp.clip(piece, 0, pieces - 1)
+                        if stage == 0:
+                            for sub in range(per_piece):
+                                form(at, sub)
+                        work(name, stage, at)
+
+            return carry
+
+        lax.fori_loop(0, -(-total_ticks // period), some_ticks, 0)
+
+    return run
 
 
 def sum_sizes(dp_size):
@@ -361,18 +364,11 @@
     around = greet_axes(dims, barrier)
     pl.semaphore_wait(barrier, around)
     slots = acc.shape[0] // rows
-    prime, tick, ticks = summing(
-        dims, pieces, rows, acc, slots, full, pieces, landing, slots, left_hbm, right_hbm,
-        vec, (proj_hbm, out_hbm, up_hbm, down_hbm, small_hbm), left_ring, right_ring, load_sem,
-        out_sem, send_sem, recv_sem,
-    )
-    prime()
-
-    def body(now, carry):
-        tick(now)
-        return carry
-
-    lax.fori_loop(0, ticks, body, 0)
+    summing(
+        dims, pieces, rows, acc, slots, full, pieces, landing, slots, left_hbm, right_hbm, vec,
+        (proj_hbm, out_hbm, up_hbm, down_hbm, small_hbm), left_ring, right_ring, load_sem, out_sem,
+        send_sem, recv_sem,
+    )()
 
 
 def reduce_gradients(left, right, vec, dp_size):

time: 337 us -> 328 us (0.973)
  Pallas kernels: 333 us -> 324 us
    pallas_call x1, Pallas kernels: 185 us -> 176 us  [reduce_gradients(): pl.pallas_call(partial(reduce_kernel, dims, pieces, rows), out_shape=sum_...]
where the time goes in v4:
time: 328 us
  Pallas kernels  324 us (99%)
    pallas_call x1, Pallas kernels, reduce_gradients(): pl.pallas_call(partial(reduce_kernel, dims, pieces, rows), out_shape=sum_...  176 us
    pallas_call x1, Pallas kernels, run_layers(): pl.pallas_call(partial(layers_kernel, chunks), out_shape=out_shape, in_sp...  132 us
    pallas_call x1, Pallas kernels, widen(): pl.pallas_call(widen_kernel, out_shape=[jax.ShapeDtypeStruct((1,) + mat.s...  15.3 us

profile of v4, /device:TPU:0, one launch (start us, length us, event | category | flops | bytes accessed | tf_op | source)
XLA Modules:
  0.0 328.1 jit_solution(13607344037868846197)
XLA Ops:
  1.3 0.1 add_select_fusion.2
  1.6 0.3 add_select_fusion.1
  1.9 0.8 pad_maximum_fusion.refs_13_
  2.8 132.4 %layers.1 = (bf16[21,4,256,256]{3,2,1,0:T(8,128)(2,1)}, bf16[27,4,256,256]{3,2,1,0:T(8,128)(2,1)}, bf16[1024,4608]{1,0:T(8,128)(2,1)}, f32[1024,1024]{1,0:T(8,12...) custom-call(bf16[1024,768]{1,0:T(8,128)(2,1)} %bitcast.14, ...), custom_call_target="tpu_custom_call" | custom-call | tf_op jit(solution)/shard_map/layers/pallas_call | solution.py:1120
  135.2 175.9 %reduce.1 = (bf16[768,2304]{1,0:T(8,128)(2,1)}, bf16[768,768]{1,0:T(8,128)(2,1)}, bf16[768,3072]{1,0:T(8,128)(2,1)}, bf16[3072,768]{1,0:T(8,128)(2,1)}, bf16[512,256]{1,0:T(8,128)(2,1)}) custom-call(bf16[21,4,256,256]{3,2,1,0:T(8,128)(2,1)} %get-tuple-element.41.left_hbm, bf16[27,4,256,256]{3,2,1,0:T(8,128)(2,1)} %get-tuple-element.42.right_hbm, ...), custom_call_target="tpu_custom_call" | custom-call | tf_op jit(solution)/shard_map/reduce/pallas_call | solution.py:378
  311.1 0.0 copy-start
  311.1 15.3 %widen.1 = (f32[1,768,2304]{2,1,0:T(8,128)}, f32[1,768,768]{2,1,0:T(8,128)}, f32[1,768,3072]{2,1,0:T(8,128)}, f32[1,3072,768]{2,1,0:T(8,128)}, f32[1,2304]{1,0:T...) custom-call(bf16[768,2304]{1,0:T(8,128)(2,1)} %get-tuple-element.44., ...), custom_call_target="tpu_custom_call" | custom-call | tf_op jit(solution)/shard_map/widen/pallas_call | solution.py:1218
  326.4 0.0 copy-done
  326.4 1.7 copy.29
  (8 shorter events, 0.1 us)
Async XLA Ops:
  311.1 15.3 %copy-start = (f32[1024,768]{1,0:T(8,128)S(1)}, f32[1024,768]{1,0:T(8,128)}, u32[]{:S(2)}) copy-start(f32[1024,768]{1,0:T(8,128)} %get-tuple-element.40) | copy-start | bytes 9437188

commit v5 on v4

--- a/solution.py
+++ b/solution.py
@@ -34,7 +34,6 @@
 PATTERN = "abacabc"
 LAG = 3
 END_LAG = 4
-OUT_LAG = 4
 UNIT = 256
 UNITS = 108
 PIECE_ROWS = 512
@@ -114,10 +113,9 @@
         pl.when(can)(action)
 
 
-def summing(dims, pieces, rows, acc, acc_slots, full, full_slots, landing, land_slots, left_hbm,
-            right_hbm, vec, outs, left_ring, right_ring, load_sem, out_sem, send_sem, recv_sem):
+def summing(dims, pieces, rows, acc, acc_slots, full, landing, land_slots, left_hbm,
+            right_hbm, vec, left_ring, right_ring, load_sem, send_sem, recv_sem):
     here, strides, place = axis_places(dims)
-    proj_hbm, out_hbm, up_hbm, down_hbm, small_hbm = outs
     ring, chunks = left_ring.shape[0], left_ring.shape[1]
     per_piece = rows // UNIT
     land_rows = landing.shape[0] // land_slots
@@ -196,7 +194,7 @@
         kind, level, ax, step, part, land = plans[name][stage]
         count, spot = dims[ax], place[ax]
         slot = piece % SEM_SLOTS
-        held, index = (acc, piece % acc_slots) if kind == "reduce" else (full, piece % full_slots)
+        held, index = (acc, piece % acc_slots) if kind == "reduce" else (full, piece)
         land_start = piece % land_slots * land_rows + land
 
         def chunk(q):
@@ -252,23 +250,6 @@
                 receives.append((can, remote(chunk(q), chunk(q), way, sign), q, None))
         return sends, receives, chunk
 
-    def out_copies(piece, action):
-        for sub in range(per_piece):
-            unit = piece * per_piece + sub
-            source = view(full, piece % full_slots, sub * UNIT, UNIT)
-            for begin, end, across, target in (
-                (0, 36, 3, down_hbm), (36, 72, 12, up_hbm), (72, 81, 3, out_hbm),
-                (81, 108, 9, proj_hbm), (108, 108 + per_piece, 1, small_hbm),
-            ):
-                @pl.when(jnp.logical_and(unit >= begin, unit < end))
-                def _():
-                    local = jnp.clip(unit - begin, 0, end - begin - 1)
-                    place_in = target.at[
-                        pl.ds(pl.multiple_of(local // across * UNIT, UNIT), UNIT),
-                        pl.ds(pl.multiple_of(local % across * UNIT, UNIT), UNIT),
-                    ]
-                    action(pltpu.make_async_copy(source, place_in, out_sem.at[unit]))
-
     def work(name, stage, piece):
         if stage > 0:
             sends, receives, chunk = copies(name, stage - 1, piece)
@@ -281,13 +262,11 @@
                 guarded(can, finish)
         if stage == n_stages // 2:
             mine = bases[name][3]
-            own = view(full, piece % full_slots, mine, shard)
+            own = view(full, piece, mine, shard)
             own[...] = view(acc, piece % acc_slots, mine, shard)[...]
         if stage < n_stages:
             for can, copy in copies(name, stage, piece)[0]:
                 guarded(can, lambda: copy().start())
-        else:
-            out_copies(piece, lambda copy: copy.start())
         if stage == n_stages:
             for can, amount in sent_rows[name]:
                 sent = landing.at[pl.ds(0, amount)]
@@ -301,7 +280,7 @@
     starts = [0]
     for stage in range(n_stages):
         starts.append(starts[-1] + (END_LAG if stage in (0, n_stages - 1) else LAG))
-    total_ticks = pieces + starts[-1] + OUT_LAG
+    total_ticks = pieces + starts[-1]
 
     def run():
         prime()
@@ -309,12 +288,6 @@
         def some_ticks(turn, carry):
             for spot_in in range(period):
                 now = turn * period + spot_in
-                oldest = now - starts[-1] - OUT_LAG
-
-                @pl.when(jnp.logical_and(oldest >= 0, oldest < pieces))
-                def _():
-                    out_copies(jnp.clip(oldest, 0, pieces - 1), lambda copy: copy.wait())
-
                 for stage in reversed(range(n_stages + 1)):
                     piece = now - starts[stage]
                     name = PATTERN[(spot_in - starts[stage]) % period]
@@ -341,33 +314,23 @@
     return dims, rows, -(-(UNITS + 1) * UNIT // rows), land, 2 * (sum(dims) - 3)
 
 
-def sum_out_shapes(rows):
-    return [
-        jax.ShapeDtypeStruct(shape, jnp.bfloat16)
-        for shape in ((768, 2304), (768, 768), (768, 3072), (3072, 768), (rows, UNIT))
-    ]
-
-
-def sum_semaphores(ring, rows, pieces, stages):
+def sum_semaphores(ring, stages):
     return [
         pltpu.SemaphoreType.DMA((ring, 2)),
-        pltpu.SemaphoreType.DMA((pieces * rows // UNIT,)),
         pltpu.SemaphoreType.DMA((SEM_SLOTS,)),
         pltpu.SemaphoreType.DMA((SEM_SLOTS, stages, 2)),
     ]
 
 
-def reduce_kernel(dims, pieces, rows, left_hbm, right_hbm, vec, proj_hbm, out_hbm, up_hbm, down_hbm,
-                  small_hbm, acc, full, landing, left_ring, right_ring, load_sem, out_sem, send_sem,
-                  recv_sem):
+def reduce_kernel(dims, pieces, rows, left_hbm, right_hbm, vec, full, acc, landing, left_ring, right_ring,
+                  load_sem, send_sem, recv_sem):
     barrier = pltpu.get_barrier_semaphore()
     around = greet_axes(dims, barrier)
     pl.semaphore_wait(barrier, around)
     slots = acc.shape[0] // rows
     summing(
-        dims, pieces, rows, acc, slots, full, pieces, landing, slots, left_hbm, right_hbm, vec,
-        (proj_hbm, out_hbm, up_hbm, down_hbm, small_hbm), left_ring, right_ring, load_sem, out_sem,
-        send_sem, recv_sem,
+        dims, pieces, rows, acc, slots, full, landing, slots, left_hbm, right_hbm, vec, left_ring,
+        right_ring, load_sem, send_sem, recv_sem,
     )()
 
 
@@ -377,19 +340,18 @@
     slots = min(SEM_SLOTS, pieces)
     return pl.pallas_call(
         partial(reduce_kernel, dims, pieces, rows),
-        out_shape=sum_out_shapes(rows),
+        out_shape=pltpu.VMEM((pieces * rows, UNIT), jnp.bfloat16),
         in_specs=any_specs(2) + vmem_specs(1),
-        out_specs=any_specs(5),
+        out_specs=pl.BlockSpec(memory_space=pltpu.VMEM),
         scratch_shapes=[
             pltpu.VMEM((slots * rows, UNIT), jnp.bfloat16),
-            pltpu.VMEM((pieces * rows, UNIT), jnp.bfloat16),
             pltpu.VMEM((slots * land, UNIT), jnp.bfloat16),
             pltpu.VMEM((ring,) + left.shape[1:], jnp.bfloat16),
             pltpu.VMEM((ring,) + left.shape[1:], jnp.bfloat16),
         ]
-        + sum_semaphores(ring, rows, pieces, stages),
+        + sum_semaphores(ring, stages),
         compiler_params=pltpu.CompilerParams(
-            collective_id=1, has_side_effects=True, vmem_limit_bytes=62 << 20
+            collective_id=1, has_side_effects=True, vmem_limit_bytes=47 << 20
         ),
         name="reduce",
     )(left, right, vec)
@@ -1180,53 +1142,51 @@
     return outs[14], outs[0], outs[1], outs[15]
 
 
-def widen_kernel(proj, out, up, down, small, *refs):
-    sources = (proj, out, up, down)
-    targets, vectors = refs[:4], refs[4:12]
-    held, wide_held = refs[12:16], refs[16:20]
-    in_sem, out_sem = refs[20:]
-    blocks = []
-    for which, source in enumerate(sources):
-        step = 256 if source.shape[1] > 768 else 768
-        for start in range(0, source.shape[0], step):
-            blocks.append((which, pl.ds(start, step)))
-    copies_in = [
-        pltpu.make_async_copy(sources[which].at[span], held[which].at[span], in_sem.at[n])
-        for n, (which, span) in enumerate(blocks)
-    ]
-    copies_out = [
-        pltpu.make_async_copy(wide_held[which].at[span], targets[which].at[0, span], out_sem.at[n])
-        for n, (which, span) in enumerate(blocks)
-    ]
-    for copy in copies_in:
-        copy.start()
+MATRICES = ((81, 9, 3), (72, 3, 3), (36, 12, 3), (0, 3, 12))
+
+
+def widen_kernel(full, *refs):
+    targets, vectors, held, out_sem = refs[:4], refs[4:12], refs[12:16], refs[16]
+    copies, turn = [], 0
+    for which, (begin, across, down) in enumerate(MATRICES):
+        for block in range(down):
+            span = pl.ds(block * UNIT, UNIT)
+            copy = pltpu.make_async_copy(
+                held[which].at[span], targets[which].at[0, span], out_sem.at[turn]
+            )
+
+            def one(n, carry):
+                start = pl.multiple_of((begin + block * across + n) * UNIT, UNIT)
+                held[which][span, pl.ds(pl.multiple_of(n * UNIT, UNIT), UNIT)] = full[
+                    pl.ds(start, UNIT), :
+                ].astype(jnp.float32)
+                return carry
+
+            lax.fori_loop(0, across, one, 0)
+            copy.start()
+            copies.append(copy)
+            turn += 1
     for (start, count), vector in zip(VECTORS.values(), vectors):
         for n in range(count):
-            vector[:, n * UNIT : (n + 1) * UNIT] = small[start + n : start + n + 1, :].astype(
-                jnp.float32
-            )
-    for n, (which, span) in enumerate(blocks):
-        copies_in[n].wait()
-        wide_held[which][span, :] = held[which][span, :].astype(jnp.float32)
-        copies_out[n].start()
-    for copy in copies_out:
+            at = UNITS * UNIT + start + n
+            vector[:, n * UNIT : (n + 1) * UNIT] = full[at : at + 1, :].astype(jnp.float32)
+    for copy in copies:
         copy.wait()
 
 
-def widen(proj, out, up, down, small):
-    mats = (proj, out, up, down)
+def widen(full):
+    shapes = [(down * UNIT, across * UNIT) for _, across, down in MATRICES]
     return pl.pallas_call(
         widen_kernel,
-        out_shape=[jax.ShapeDtypeStruct((1,) + mat.shape, jnp.float32) for mat in mats]
+        out_shape=[jax.ShapeDtypeStruct((1,) + shape, jnp.float32) for shape in shapes]
         + [jax.ShapeDtypeStruct((1, count * UNIT), jnp.float32) for _, count in VECTORS.values()],
-        in_specs=any_specs(4) + vmem_specs(1),
+        in_specs=[pl.BlockSpec(memory_space=pltpu.VMEM)],
         out_specs=any_specs(4) + vmem_specs(8),
-        scratch_shapes=[pltpu.VMEM(mat.shape, jnp.bfloat16) for mat in mats]
-        + [pltpu.VMEM(mat.shape, jnp.float32) for mat in mats]
-        + [pltpu.SemaphoreType.DMA((11,)), pltpu.SemaphoreType.DMA((11,))],
-        compiler_params=pltpu.CompilerParams(vmem_limit_bytes=60 << 20),
+        scratch_shapes=[pltpu.VMEM(shape, jnp.float32) for shape in shapes]
+        + [pltpu.SemaphoreType.DMA((sum(down for _, _, down in MATRICES),))],
+        compiler_params=pltpu.CompilerParams(vmem_limit_bytes=36 << 20),
         name="widen",
-    )(proj, out, up, down, small)
+    )(full)
 
 
 def mix_tables(length):
@@ -1272,8 +1232,8 @@
     )
     mix = mix_tables(segment_length[0])
     results, left, right, vec = run_layers(endpoints[0], mats, rows, mix, dp_size)
-    sums = reduce_gradients(left, right, vec, dp_size)
-    proj, out, up, down, bp, bo, g1, h1, bu, bd, g2, h2 = widen(*sums)
+    full = reduce_gradients(left, right, vec, dp_size)
+    proj, out, up, down, bp, bo, g1, h1, bu, bd, g2, h2 = widen(full)
     return (results[None], proj, bp, out, bo, g1, h1, up, bu, down, bd, g2, h2)
 
 

time: 328 us -> 321 us (0.979)
  Pallas kernels: 324 us -> 317 us
    pallas_call x2, Pallas kernels: 191 us -> 185 us  [the longest x1 174 us: reduce_gradients(): pl.pallas_call(partial(reduce_kernel, dims, pieces, rows), out_shape=pltp...]
where the time goes in v5:
time: 321 us
  Pallas kernels  317 us (99%)
    pallas_call x1, Pallas kernels, reduce_gradients(): pl.pallas_call(partial(reduce_kernel, dims, pieces, rows), out_shape=pltp...  174 us
    pallas_call x1, Pallas kernels, run_layers(): pl.pallas_call(partial(layers_kernel, chunks), out_shape=out_shape, in_sp...  132 us
    pallas_call x1, Pallas kernels, widen(): pl.pallas_call(widen_kernel, out_shape=[jax.ShapeDtypeStruct((1,) + shape...  10.6 us

profile of v5, /device:TPU:0, one launch (start us, length us, event | category | flops | bytes accessed | tf_op | source)
XLA Modules:
  0.0 321.3 jit_solution(10088921252395991754)
XLA Ops:
  1.3 0.1 add_select_fusion.2
  1.6 0.3 add_select_fusion.1
  1.9 0.8 pad_maximum_fusion.refs_13_
  2.8 132.3 %layers.1 = (bf16[21,4,256,256]{3,2,1,0:T(8,128)(2,1)}, bf16[27,4,256,256]{3,2,1,0:T(8,128)(2,1)}, bf16[1024,4608]{1,0:T(8,128)(2,1)}, f32[1024,1024]{1,0:T(8,12...) custom-call(bf16[1024,768]{1,0:T(8,128)(2,1)} %bitcast.14, ...), custom_call_target="tpu_custom_call" | custom-call | tf_op jit(solution)/shard_map/layers/pallas_call | solution.py:1082
  135.0 174.0 %reduce.1.full = bf16[28160,256]{1,0:T(8,128)(2,1)S(1)} custom-call(bf16[21,4,256,256]{3,2,1,0:T(8,128)(2,1)} %get-tuple-element.36.left_hbm, bf16[27,4,256,256]{3,2,1,0:T(8,128)(2,1)} %get-tuple-element.37.right_hbm, f32[512,256]{1,0:T(8,128)} %get-tuple-element.38.vec), custom_call_target="tpu_custom_call" | custom-call | tf_op jit(solution)/shard_map/reduce/pallas_call | solution.py:341
  309.0 0.0 copy-start
  309.0 10.6 %widen.1 = (f32[1,768,2304]{2,1,0:T(8,128)}, f32[1,768,768]{2,1,0:T(8,128)}, f32[1,768,3072]{2,1,0:T(8,128)}, f32[1,3072,768]{2,1,0:T(8,128)}, f32[1,2304]{1,0:T...) custom-call(bf16[28160,256]{1,0:T(8,128)(2,1)S(1)} %reduce.1.full), custom_call_target="tpu_custom_call" | custom-call | tf_op jit(solution)/shard_map/widen/pallas_call | solution.py:1179
  319.6 0.0 copy-done
  319.6 1.7 copy.29
  (8 shorter events, 0.1 us)
Async XLA Ops:
  309.0 10.6 %copy-start = (f32[1024,768]{1,0:T(8,128)S(1)}, f32[1024,768]{1,0:T(8,128)}, u32[]{:S(2)}) copy-start(f32[1024,768]{1,0:T(8,128)} %get-tuple-element.35) | copy-start | bytes 9437188

commit v6 on v5

--- a/solution.py
+++ b/solution.py
@@ -114,7 +114,7 @@
 
 
 def summing(dims, pieces, rows, acc, acc_slots, full, landing, land_slots, left_hbm,
-            right_hbm, vec, left_ring, right_ring, load_sem, send_sem, recv_sem):
+            right_hbm, vec_hbm, vec, left_ring, right_ring, load_sem, vec_sem, send_sem, recv_sem):
     here, strides, place = axis_places(dims)
     ring, chunks = left_ring.shape[0], left_ring.shape[1]
     per_piece = rows // UNIT
@@ -167,6 +167,8 @@
             for copy in loads(jnp.int32(unit)):
                 copy.start()
 
+    vec_copy = pltpu.make_async_copy(vec_hbm, vec.at[pl.ds(0, vec_hbm.shape[0])], vec_sem)
+
     def form(piece, sub):
         unit = piece * per_piece + sub
         target = view(acc, piece % acc_slots, sub * UNIT, UNIT)
@@ -188,6 +190,8 @@
 
         @pl.when(unit >= UNITS)
         def _():
+            if sub == 0:
+                vec_copy.wait()
             target[...] = vec[sub * UNIT : (sub + 1) * UNIT, :].astype(jnp.bfloat16)
 
     def copies(name, stage, piece):
@@ -282,13 +286,16 @@
         starts.append(starts[-1] + (END_LAG if stage in (0, n_stages - 1) else LAG))
     total_ticks = pieces + starts[-1]
 
-    def run():
+    def run(meet):
         prime()
+        vec[...] = jnp.zeros_like(vec)
+        vec_copy.start()
+        meet()
 
         def some_ticks(turn, carry):
             for spot_in in range(period):
                 now = turn * period + spot_in
-                for stage in reversed(range(n_stages + 1)):
+                for stage in range(n_stages + 1):
                     piece = now - starts[stage]
                     name = PATTERN[(spot_in - starts[stage]) % period]
 
@@ -317,21 +324,22 @@
 def sum_semaphores(ring, stages):
     return [
         pltpu.SemaphoreType.DMA((ring, 2)),
+        pltpu.SemaphoreType.DMA,
         pltpu.SemaphoreType.DMA((SEM_SLOTS,)),
         pltpu.SemaphoreType.DMA((SEM_SLOTS, stages, 2)),
     ]
 
 
-def reduce_kernel(dims, pieces, rows, left_hbm, right_hbm, vec, full, acc, landing, left_ring, right_ring,
-                  load_sem, send_sem, recv_sem):
+def reduce_kernel(dims, pieces, rows, left_hbm, right_hbm, vec_hbm, full, acc, landing, vec, left_ring,
+                  right_ring, load_sem, vec_sem, send_sem, recv_sem):
     barrier = pltpu.get_barrier_semaphore()
     around = greet_axes(dims, barrier)
-    pl.semaphore_wait(barrier, around)
     slots = acc.shape[0] // rows
-    summing(
-        dims, pieces, rows, acc, slots, full, landing, slots, left_hbm, right_hbm, vec, left_ring,
-        right_ring, load_sem, send_sem, recv_sem,
-    )()
+    run = summing(
+        dims, pieces, rows, acc, slots, full, landing, slots, left_hbm, right_hbm, vec_hbm, vec,
+        left_ring, right_ring, load_sem, vec_sem, send_sem, recv_sem,
+    )
+    run(lambda: pl.semaphore_wait(barrier, around))
 
 
 def reduce_gradients(left, right, vec, dp_size):
@@ -341,11 +349,12 @@
     return pl.pallas_call(
         partial(reduce_kernel, dims, pieces, rows),
         out_shape=pltpu.VMEM((pieces * rows, UNIT), jnp.bfloat16),
-        in_specs=any_specs(2) + vmem_specs(1),
+        in_specs=any_specs(3),
         out_specs=pl.BlockSpec(memory_space=pltpu.VMEM),
         scratch_shapes=[
             pltpu.VMEM((slots * rows, UNIT), jnp.bfloat16),
             pltpu.VMEM((slots * land, UNIT), jnp.bfloat16),
+            pltpu.VMEM((rows, UNIT), jnp.float32),
             pltpu.VMEM((ring,) + left.shape[1:], jnp.bfloat16),
             pltpu.VMEM((ring,) + left.shape[1:], jnp.bfloat16),
         ]
@@ -368,15 +377,14 @@
     "bp": (0, 9), "bo": (9, 3), "g1": (12, 3), "h1": (15, 3), "bu": (18, 12), "bd": (30, 3), "g2": (33, 3),
     "h2": (36, 3),
 }
-TAIL_SCALE = 0.375
+TAIL_SCALE = 0.45
 TAIL_POLY = (
-    0.21141059805705423,
-    0.21471795439954675,
-    0.17184958530833144,
-    0.26915459919947066,
-    -0.10973686091480542,
-    0.37354383408912983,
-    -0.13093832475477368,
+    0.25396798653159114,
+    0.25170428274474826,
+    0.24846812412232888,
+    0.08947906819608953,
+    0.2922223682202733,
+    -0.13585125317877522,
 )
 
 
@@ -390,7 +398,7 @@
 
 
 def gelu_pair(hidden):
-    bell = jnp.exp(hidden * hidden * -0.5)
+    bell = jnp.exp2(hidden * hidden * (-0.5 * math.log2(math.e)))
     t = inverse(1.0 + (TAIL_SCALE * math.sqrt(0.5)) * jnp.abs(hidden))
     poly = jnp.full_like(t, 0.5 * TAIL_POLY[-1])
     for coefficient in TAIL_POLY[-2::-1]:
@@ -665,11 +673,17 @@
             span = slice(pair * 128, (pair + 1) * 128)
             stat_b[slot, :, span] = jnp.where(low, num_a, num_b) * inv
             stat_a[slot, :, span] = inv
-        blocks(15, stat_b[slot].astype(jnp.bfloat16))
+        mixed_low = stat_b[slot].astype(jnp.bfloat16)
+        blocks(15, mixed_low)
         weights_ready(i, 1)
-        first_sum = x.astype(jnp.float32) + row(bo)
-        for n in range(3):
-            first_sum += dot(left[15 + n], wo[n * UNIT : (n + 1) * UNIT, :])
+        first_sum = x.astype(jnp.float32) + row(bo) + dot(mixed_low, wo[...])
+
+        @pl.when(jnp.logical_and(first, i == chunks - 1))
+        def _():
+            for which in (1, 0):
+                w_push(which).wait_recv()
+                w_copy(which, peer_w_hbm).start()
+
         unit_one, scale_one = centred(first_sum)
         keep(now_a, KEEP_A["u1"], unit_one)
         stat_a[slot, :, STAT_A["s1"] : STAT_A["s1"] + 128] = wide(scale_one)
@@ -729,25 +743,27 @@
         return carry
 
     lax.fori_loop(0, chunks, forward_chunk, 0)
+    @pl.when(first)
+    def _():
+        def fetch(i, some):
+            for n in some:
+                save(i + half, i, n).wait()
+                push(i, i, n).wait_recv()
+                load(i, i, n, peer_hbm).start()
+
+        fetch(1, (0, 1))
+        for which in (3, 2):
+            w_push(which).wait_recv()
+            w_copy(which, peer_w_hbm).start()
+        fetch(1, (2, 3))
+        fetch(0, (2, 3, 0, 1))
+        for i in range(chunks):
+            hand_on(i).wait_send()
+
     left_copy(chunks - 1).wait()
     for i in range(chunks):
         for copy in x_out_copies(i):
             copy.wait()
-
-    @pl.when(first)
-    def _():
-        for i in range(half, chunks):
-            for n in range(4):
-                save(i, i % 2, n).wait()
-        for which in (3, 2, 1, 0):
-            w_push(which).wait_recv()
-            w_copy(which, peer_w_hbm).start()
-        for i in (1, 0):
-            for n in range(4):
-                push(i, i, n).wait_recv()
-                load(i, i, n, peer_hbm).start()
-        for i in range(chunks):
-            hand_on(i).wait_send()
 
     @pl.when(second)
     def _():
@@ -1001,7 +1017,7 @@
             @pl.when(turn == half - 1)
             def _():
                 w_copy(0).start()
-                vec_sent[...] = vec[0:40, :]
+                vec_sent[...] = vec[...]
                 vec_push().start()
                 vec[...] = jnp.zeros_like(vec)
 
@@ -1041,18 +1057,19 @@
         for i in range(half, chunks):
             hand_back(i).wait_send()
         vec_push().wait_recv()
-        vec[0:40, :] += vec_peer[...]
+        vec[...] += vec_peer[...]
         for i in range(half):
             for n in range(3):
                 right_push(i, n).wait_recv()
 
-    vec_out[...] = vec[...]
-
-
-def run_layers(ends, mats, rows_in, mix, dp_size):
+    out_copy = pltpu.make_async_copy(vec, vec_out, w_sem.at[0])
+    out_copy.start()
+    out_copy.wait()
+
+
+def run_layers(ends, mats, rows_in, mix):
     tokens, width = ends.shape
     chunks = tokens // CHUNK
-    rows = sum_sizes(dp_size)[1]
     bf16, f32 = jnp.bfloat16, jnp.float32
 
     def kept(count):
@@ -1073,7 +1090,7 @@
         + [jax.ShapeDtypeStruct(mat.shape, mat.dtype) for mat in mats]
         + [
             jax.ShapeDtypeStruct((tokens, width), f32),
-            jax.ShapeDtypeStruct((rows, UNIT), f32),
+            jax.ShapeDtypeStruct((40, UNIT), f32),
         ]
     )
     chunk_f32 = pltpu.VMEM((CHUNK, width), f32)
@@ -1083,7 +1100,7 @@
         partial(layers_kernel, chunks),
         out_shape=out_shape,
         in_specs=any_specs(5) + vmem_specs(9),
-        out_specs=any_specs(15) + vmem_specs(1),
+        out_specs=any_specs(16),
         scratch_shapes=[pltpu.VMEM(mat.shape, mat.dtype) for mat in mats]
         + [
             all_rows,
@@ -1104,7 +1121,7 @@
             chunk_f32,
             chunk_f32,
             pltpu.VMEM((CHUNK, width), bf16),
-            pltpu.VMEM((rows, UNIT), f32),
+            pltpu.VMEM((40, UNIT), f32),
             pltpu.VMEM((40, UNIT), f32),
             pltpu.VMEM((40, UNIT), f32),
             pltpu.VMEM((8, width), f32),
@@ -1231,7 +1248,7 @@
         second_shift,
     )
     mix = mix_tables(segment_length[0])
-    results, left, right, vec = run_layers(endpoints[0], mats, rows, mix, dp_size)
+    results, left, right, vec = run_layers(endpoints[0], mats, rows, mix)
     full = reduce_gradients(left, right, vec, dp_size)
     proj, out, up, down, bp, bo, g1, h1, bu, bd, g2, h2 = widen(full)
     return (results[None], proj, bp, out, bo, g1, h1, up, bu, down, bd, g2, h2)

time: 321 us -> 317 us (0.988)
  Pallas kernels: 317 us -> 312 us
    pallas_call x1, Pallas kernels: 132 us -> 128 us  [run_layers(): pl.pallas_call(partial(layers_kernel, chunks), out_shape=out_shape, in_sp...]
where the time goes in v6:
time: 317 us
  Pallas kernels  312 us (98%)
    pallas_call x1, Pallas kernels, reduce_gradients(): pl.pallas_call(partial(reduce_kernel, dims, pieces, rows), out_shape=pltp...  173 us
    pallas_call x1, Pallas kernels, run_layers(): pl.pallas_call(partial(layers_kernel, chunks), out_shape=out_shape, in_sp...  128 us
    pallas_call x1, Pallas kernels, widen(): pl.pallas_call(widen_kernel, out_shape=[jax.ShapeDtypeStruct((1,) + shape...  10.6 us

profile of v6, /device:TPU:0, one launch (start us, length us, event | category | flops | bytes accessed | tf_op | source)
XLA Modules:
  0.0 316.6 jit_solution(18388228628769044566)
XLA Ops:
  1.3 0.1 add_select_fusion.2
  1.6 0.3 add_select_fusion.1
  1.9 0.8 pad_maximum_fusion.refs_13_
  2.8 128.2 %layers.1 = (bf16[21,4,256,256]{3,2,1,0:T(8,128)(2,1)}, bf16[27,4,256,256]{3,2,1,0:T(8,128)(2,1)}, bf16[1024,4608]{1,0:T(8,128)(2,1)}, f32[1024,1024]{1,0:T(8,12...) custom-call(bf16[1024,768]{1,0:T(8,128)(2,1)} %bitcast.14, ...), custom_call_target="tpu_custom_call" | custom-call | tf_op jit(solution)/shard_map/layers/pallas_call | solution.py:1099
  131.0 173.4 %reduce.1.full = bf16[28160,256]{1,0:T(8,128)(2,1)S(1)} custom-call(bf16[21,4,256,256]{3,2,1,0:T(8,128)(2,1)} %get-tuple-element.36.left_hbm, bf16[27,4,256,256]{3,2,1,0:T(8,128)(2,1)} %get-tuple-element.37.right_hbm, f32[40,256]{1,0:T(8,128)} %get-tuple-element.38.vec_hbm), custom_call_target="tpu_custom_call" | custom-call | tf_op jit(solution)/shard_map/reduce/pallas_call | solution.py:349
  304.4 0.0 copy-start
  304.4 10.6 %widen.1 = (f32[1,768,2304]{2,1,0:T(8,128)}, f32[1,768,768]{2,1,0:T(8,128)}, f32[1,768,3072]{2,1,0:T(8,128)}, f32[1,3072,768]{2,1,0:T(8,128)}, f32[1,2304]{1,0:T...) custom-call(bf16[28160,256]{1,0:T(8,128)(2,1)S(1)} %reduce.1.full), custom_call_target="tpu_custom_call" | custom-call | tf_op jit(solution)/shard_map/widen/pallas_call | solution.py:1196
  314.9 0.0 copy-done
  314.9 1.7 copy.29
  (8 shorter events, 0.1 us)
Async XLA Ops:
  304.4 10.6 %copy-start = (f32[1024,768]{1,0:T(8,128)S(1)}, f32[1024,768]{1,0:T(8,128)}, u32[]{:S(2)}) copy-start(f32[1024,768]{1,0:T(8,128)} %get-tuple-element.35) | copy-start | bytes 9437188

commit v7 on v6

--- a/solution.py
+++ b/solution.py
@@ -393,8 +393,7 @@
 
 
 def inverse(value):
-    rough = pl.reciprocal(value, approx=True)
-    return rough * (2.0 - value * rough)
+    return pl.reciprocal(value, approx=True)
 
 
 def gelu_pair(hidden):
@@ -409,11 +408,9 @@
 
 
 def softplus_pair(value):
-    small = jnp.exp(-jnp.abs(value))
+    small = jnp.exp2(jnp.abs(value) * -math.log2(math.e))
     whole = 1.0 + small
-    log_whole = jnp.where(
-        small < 1e-2, small * (1.0 - small * (0.5 - small * (1.0 / 3.0))), jnp.log(whole)
-    )
+    log_whole = jnp.where(small < 2e-3, small * (1.0 - 0.5 * small), jnp.log(whole))
     return (
         jnp.maximum(value, 0.0) + log_whole,
         jnp.where(value >= 0, 1.0, small) * inverse(whole),
@@ -458,7 +455,7 @@
     own_hbm, peer_hbm, peer_w_hbm = refs[16:20], refs[20:24], refs[24:28]
     res_hbm, vec_out = refs[28:30]
     (wp, wo, wu, wd, x_in, e_in, handed, left, right, keep_a, stat_a, keep_b, stat_b, rows_out, nums, dq,
-     dk, dv, carry_k, carry_v, dn1, weighed, vec, vec_sent, vec_peer, gains, gains_peer, w_sem, x_sem, xo_sem, e_sem, left_sem,
+     dk, dv, carry_k, carry_v, dn1, weighed, vec, vec_sent, vec_peer, gains, gains_peer, cut_in, rest_in, rest, w_sem, x_sem, xo_sem, e_sem, left_sem,
      right_sem, load_sem, res_sem, send_f, recv_f, send_b, recv_b, send_w, recv_w, send_e, recv_e,
      send_k, recv_k, send_r, recv_r, send_v, recv_v, send_g, recv_g) = refs[30:]
 
@@ -508,7 +505,14 @@
         return remote(handed.at[i], x_in.at[i], send_f.at[i], recv_f.at[i])
 
     def hand_back(i):
-        return remote(handed.at[i], e_in.at[i], send_b.at[i], recv_b.at[i])
+        at = i - half
+        return [
+            remote(
+                right.at[18 + 3 * n : 21 + 3 * n], cut_in.at[at, 3 * n : 3 * n + 3],
+                send_b.at[at, n], recv_b.at[at, n],
+            )
+            for n in range(3)
+        ] + [remote(rest.at[at], rest_in.at[at], send_b.at[at, 3], recv_b.at[at, 3])]
 
     def left_copy(i):
         return pltpu.make_async_copy(left, left_hbm.at[0:18, i], left_sem)
@@ -709,6 +713,19 @@
                 weights_ready(i, 3)
             resid[...] += dot(active, wd[n * width : (n + 1) * width, :])
             hidden = later
+
+            @pl.when(jnp.logical_and(first, i == chunks - 1))
+            def _():
+                if n == 0:
+                    w_push(3).wait_recv()
+                    w_push(2).wait_recv()
+                quarter = pl.ds(n * width, width)
+                pltpu.make_async_copy(
+                    peer_w_hbm[3].at[quarter], wd.at[quarter], w_sem.at[3]
+                ).start()
+                pltpu.make_async_copy(
+                    peer_w_hbm[2].at[:, quarter], wu.at[:, quarter], w_sem.at[2]
+                ).start()
         unit_two, scale_two = centred(resid[...])
         keep(now_a, KEEP_A["u2"], unit_two)
         stat_a[slot, :, STAT_A["s2"] : STAT_A["s2"] + 128] = wide(scale_two)
@@ -752,9 +769,6 @@
                 load(i, i, n, peer_hbm).start()
 
         fetch(1, (0, 1))
-        for which in (3, 2):
-            w_push(which).wait_recv()
-            w_copy(which, peer_w_hbm).start()
         fetch(1, (2, 3))
         fetch(0, (2, 3, 0, 1))
         for i in range(chunks):
@@ -839,10 +853,6 @@
             @pl.when(turn == half)
             def _():
                 own_gains()
-
-            @pl.when(turn >= chunks)
-            def _():
-                hand_back(i).wait_recv()
 
         @pl.when(second)
         def _():
@@ -908,6 +918,11 @@
         grad_mixed = back_product(first_low, wo[...]).astype(jnp.bfloat16).astype(jnp.float32)
         weighed[...] = (grad_mixed * stat_a[slot, :, 0:width]).astype(jnp.bfloat16)
 
+        @pl.when(second)
+        def _():
+            rest[i - half] = total[...]
+            hand_back(i)[3].start()
+
         @pl.when(first)
         def _():
             @pl.when(turn + 2 < turns)
@@ -927,31 +942,35 @@
         def cut(ref, name):
             return ref[:, pl.ds(pl.multiple_of(KEEP_B[name] + pair * 128, 128), 128)]
 
+        queries = cut(now_b, "q")
+        w = weighed[:, span]
+        cross = w.astype(jnp.float32) * stat_b[slot, :, span]
+        zero, one = jnp.zeros_like(w), jnp.ones_like(w)
+        halves = []
+        for part in range(2):
+            own = low if part == 0 else jnp.logical_not(low)
+            spare = 64 * (1 - part)
+            inner = jnp.sum(jnp.where(own, cross, 0.0), axis=-1, keepdims=True)
+            rough = inner.astype(jnp.bfloat16).astype(jnp.float32)
+            extra = jnp.where(
+                lanes == spare, -rough, jnp.where(lanes == spare + 1, rough - inner, 0.0)
+            ).astype(jnp.bfloat16)
+            halves.append(
+                (own, jnp.where(own, w, extra), jnp.where(own, queries, zero), jnp.where(own, w, zero))
+            )
+
         def half_block(source, table):
-            queries, keys_in, values = cut(now_b, "q"), cut(source, "k"), cut(source, "v")
-            w = weighed[:, span]
-            cross = w.astype(jnp.float32) * stat_b[slot, :, span]
-            zero, one = jnp.zeros_like(keys_in), jnp.ones_like(values)
+            keys_in, values = cut(source, "k"), cut(source, "v")
             total_q, total_k, total_v = 0.0, 0.0, 0.0
-            for half in range(2):
-                own = low if half == 0 else jnp.logical_not(low)
-                spare = 64 * (1 - half)
-                inner = jnp.sum(jnp.where(own, cross, 0.0), axis=-1, keepdims=True)
-                rough = inner.astype(jnp.bfloat16).astype(jnp.float32)
-                extra = jnp.where(
-                    lanes == spare, -rough, jnp.where(lanes == spare + 1, rough - inner, 0.0)
-                ).astype(jnp.bfloat16)
+            for own, w_extra, own_queries, own_w in halves:
                 own_keys = jnp.where(own, keys_in, zero)
                 scores = (back_product(queries, own_keys) * table).astype(jnp.bfloat16)
-                grads = (
-                    back_product(
-                        jnp.where(own, w, extra), jnp.where(own, values, one)
-                    )
-                    * table
-                ).astype(jnp.bfloat16)
+                grads = (back_product(w_extra, jnp.where(own, values, one)) * table).astype(
+                    jnp.bfloat16
+                )
                 total_q += dot(grads, own_keys)
-                total_k += rows_product(grads, jnp.where(own, queries, zero))
-                total_v += rows_product(scores, jnp.where(own, w, zero))
+                total_k += rows_product(grads, own_queries)
+                total_v += rows_product(scores, own_w)
             return total_q, total_k, total_v
 
         total_q, total_k, total_v = half_block(now_b, mix[0])
@@ -978,12 +997,16 @@
         def _():
             right_done(turn - 1, 2)
 
+            @pl.when(second)
+            def _():
+                for copy in hand_back(chunk_of(turn - 1))[:3]:
+                    copy.wait_send()
+
         @pl.when(jnp.logical_and(first, jnp.logical_or(turn == 0, turn == half)))
         def _():
             w_copy(0).wait()
 
         now_b = keep_b.at[slot]
-        grad_in = dn1[...]
         for n, (source, slope) in enumerate(((dq, "sq"), (dk, "sk"), (dv, None))):
             values = source[...]
             if slope:
@@ -991,12 +1014,24 @@
                 values = values * now_b[:, at : at + width].astype(jnp.float32)
             values = values.astype(jnp.bfloat16)
             right_blocks(18 + 3 * n, values)
+
+            @pl.when(second)
+            def _():
+                hand_back(i)[n].start()
+
             tally("bp", n * width, values)
-            grad_in += back_product(values, wp[:, n * width : (n + 1) * width])
         right_go(turn, 2)
 
+        def through(blocks_of, start):
+            for n in range(3):
+                values = jnp.concatenate([blocks_of[3 * n + m] for m in range(3)], axis=1)
+                start += back_product(values, wp[:, n * width : (n + 1) * width])
+            return start
+
         @pl.when(first)
         def _():
+            grad_in = through(right.at[18:27], dn1[...])
+
             @pl.when(turn < half)
             def _():
                 e_in[i] = grad_in.astype(jnp.bfloat16)
@@ -1016,15 +1051,16 @@
 
             @pl.when(turn == half - 1)
             def _():
-                w_copy(0).start()
                 vec_sent[...] = vec[...]
                 vec_push().start()
                 vec[...] = jnp.zeros_like(vec)
-
-        @pl.when(second)
-        def _():
-            handed[i] = grad_in.astype(jnp.bfloat16)
-            hand_back(i).start()
+                for late in (chunks - 1, chunks - 2):
+                    for copy in hand_back(late):
+                        copy.wait_recv()
+                    e_in[late] = through(cut_in.at[late - half], rest_in[late - half]).astype(
+                        jnp.bfloat16
+                    )
+                w_copy(0).start()
 
     def one_turn(turn, carry):
         i = chunk_of(turn)
@@ -1054,8 +1090,10 @@
 
     @pl.when(second)
     def _():
+        for copy in hand_back(half)[:3]:
+            copy.wait_send()
         for i in range(half, chunks):
-            hand_back(i).wait_send()
+            hand_back(i)[3].wait_send()
         vec_push().wait_recv()
         vec[...] += vec_peer[...]
         for i in range(half):
@@ -1126,6 +1164,9 @@
             pltpu.VMEM((40, UNIT), f32),
             pltpu.VMEM((8, width), f32),
             pltpu.VMEM((8, width), f32),
+            pltpu.VMEM((chunks // 2, 9, CHUNK, UNIT), bf16),
+            pltpu.VMEM((chunks // 2, CHUNK, width), f32),
+            pltpu.VMEM((chunks // 2, CHUNK, width), f32),
             dma((4,)),
             dma((chunks,)),
             dma((chunks, 3)),
@@ -1136,8 +1177,8 @@
             dma,
             dma((chunks,)),
             dma((chunks,)),
-            dma((chunks,)),
-            dma((chunks,)),
+            dma((chunks // 2, 4)),
+            dma((chunks // 2, 4)),
             dma((4,)),
             dma((4,)),
             dma((chunks // 2,)),

time: 317 us -> 311 us (0.981)
  Pallas kernels: 312 us -> 306 us
    pallas_call x1, Pallas kernels: 173 us -> 159 us  [reduce_gradients(): pl.pallas_call(partial(reduce_kernel, dims, pieces, rows), out_shape=pltp...]
    pallas_call x1, Pallas kernels: 128 us -> 136 us  [run_layers(): pl.pallas_call(partial(layers_kernel, chunks), out_shape=out_shape, in_sp...]
where the time goes in v7:
time: 311 us; the launch traced here: 310 us
  Pallas kernels  306 us (98%)
    pallas_call x1, Pallas kernels, reduce_gradients(): pl.pallas_call(partial(reduce_kernel, dims, pieces, rows), out_shape=pltp...  159 us
    pallas_call x1, Pallas kernels, run_layers(): pl.pallas_call(partial(layers_kernel, chunks), out_shape=out_shape, in_sp...  136 us
    pallas_call x1, Pallas kernels, widen(): pl.pallas_call(widen_kernel, out_shape=[jax.ShapeDtypeStruct((1,) + shape...  10.6 us

profile of v7, /device:TPU:0, one launch (start us, length us, event | category | flops | bytes accessed | tf_op | source)
XLA Modules:
  0.0 310.4 jit_solution(14428791471813551827)
XLA Ops:
  1.3 0.1 add_select_fusion.2
  1.6 0.3 add_select_fusion.1
  1.9 0.8 pad_maximum_fusion.refs_13_
  2.8 136.1 %layers.1 = (bf16[21,4,256,256]{3,2,1,0:T(8,128)(2,1)}, bf16[27,4,256,256]{3,2,1,0:T(8,128)(2,1)}, bf16[1024,4608]{1,0:T(8,128)(2,1)}, f32[1024,1024]{1,0:T(8,12...) custom-call(bf16[1024,768]{1,0:T(8,128)(2,1)} %bitcast.14, ...), custom_call_target="tpu_custom_call" | custom-call | tf_op jit(solution)/shard_map/layers/pallas_call | solution.py:1137
  138.8 159.3 %reduce.1.full = bf16[28160,256]{1,0:T(8,128)(2,1)S(1)} custom-call(bf16[21,4,256,256]{3,2,1,0:T(8,128)(2,1)} %get-tuple-element.36.left_hbm, bf16[27,4,256,256]{3,2,1,0:T(8,128)(2,1)} %get-tuple-element.37.right_hbm, f32[40,256]{1,0:T(8,128)} %get-tuple-element.38.vec_hbm), custom_call_target="tpu_custom_call" | custom-call | tf_op jit(solution)/shard_map/reduce/pallas_call | solution.py:349
  298.2 0.0 copy-start
  298.2 10.6 %widen.1 = (f32[1,768,2304]{2,1,0:T(8,128)}, f32[1,768,768]{2,1,0:T(8,128)}, f32[1,768,3072]{2,1,0:T(8,128)}, f32[1,3072,768]{2,1,0:T(8,128)}, f32[1,2304]{1,0:T...) custom-call(bf16[28160,256]{1,0:T(8,128)(2,1)S(1)} %reduce.1.full), custom_call_target="tpu_custom_call" | custom-call | tf_op jit(solution)/shard_map/widen/pallas_call | solution.py:1237
  308.7 0.0 copy-done
  308.7 1.7 copy.29
  (8 shorter events, 0.1 us)
Async XLA Ops:
  298.2 10.6 %copy-start = (f32[1024,768]{1,0:T(8,128)S(1)}, f32[1024,768]{1,0:T(8,128)}, u32[]{:S(2)}) copy-start(f32[1024,768]{1,0:T(8,128)} %get-tuple-element.35) | copy-start | bytes 9437188

commit v8 on v7

--- a/solution.py
+++ b/solution.py
@@ -119,14 +119,17 @@
     ring, chunks = left_ring.shape[0], left_ring.shape[1]
     per_piece = rows // UNIT
     land_rows = landing.shape[0] // land_slots
-    plans = {name: stage_list(order, dims, rows)[0] for name, order in ORDERS.items()}
+    period = len(PATTERN)
+    n_shards = dims[0] * dims[1] * dims[2]
+    orders = {**ORDERS, "last": ORDERS[PATTERN[(pieces - 1) % period]]}
+    sizes = {name: min(rows, 16 * n_shards) if name == "last" else rows for name in orders}
+    plans = {name: stage_list(order, dims, sizes[name])[0] for name, order in orders.items()}
     n_stages = len(plans["a"])
     shard = rows // (dims[0] * dims[1] * dims[2])
-    period = len(PATTERN)
 
     bases = {}
-    for name, order in ORDERS.items():
-        base, size, found = 0, rows, []
+    for name, order in orders.items():
+        base, size, found = 0, sizes[name], []
         for ax in order:
             found.append(base)
             size = size // dims[ax]
@@ -266,6 +269,7 @@
                 guarded(can, finish)
         if stage == n_stages // 2:
             mine = bases[name][3]
+            shard = sizes[name] // n_shards
             own = view(full, piece, mine, shard)
             own[...] = view(acc, piece % acc_slots, mine, shard)[...]
         if stage < n_stages:
@@ -299,13 +303,21 @@
                     piece = now - starts[stage]
                     name = PATTERN[(spot_in - starts[stage]) % period]
 
-                    @pl.when(jnp.logical_and(piece >= 0, piece < pieces))
+                    @pl.when(jnp.logical_and(piece >= 0, piece < pieces - 1))
                     def _():
-                        at = jnp.clip(piece, 0, pieces - 1)
+                        at = jnp.clip(piece, 0, pieces - 2)
                         if stage == 0:
                             for sub in range(per_piece):
                                 form(at, sub)
                         work(name, stage, at)
+
+                    if (spot_in - starts[stage] - pieces + 1) % period == 0:
+                        @pl.when(piece == pieces - 1)
+                        def _():
+                            if stage == 0:
+                                for sub in range(sizes["last"] // UNIT):
+                                    form(jnp.int32(pieces - 1), sub)
+                            work("last", stage, jnp.int32(pieces - 1))
 
             return carry
 

time: 311 us -> 309 us (level)
  no operation moved by 1% of the time
where the time goes in v8:
time: 309 us
  Pallas kernels  304 us (98%)
    pallas_call x1, Pallas kernels, reduce_gradients(): pl.pallas_call(partial(reduce_kernel, dims, pieces, rows), out_shape=pltp...  158 us
    pallas_call x1, Pallas kernels, run_layers(): pl.pallas_call(partial(layers_kernel, chunks), out_shape=out_shape, in_sp...  136 us
    pallas_call x1, Pallas kernels, widen(): pl.pallas_call(widen_kernel, out_shape=[jax.ShapeDtypeStruct((1,) + shape...  10.6 us

profile of v8, /device:TPU:0, one launch (start us, length us, event | category | flops | bytes accessed | tf_op | source)
XLA Modules:
  0.0 308.7 jit_solution(10031663747952966988)
XLA Ops:
  1.3 0.1 add_select_fusion.2
  1.6 0.3 add_select_fusion.1
  1.9 0.8 pad_maximum_fusion.refs_13_
  2.8 136.1 %layers.1 = (bf16[21,4,256,256]{3,2,1,0:T(8,128)(2,1)}, bf16[27,4,256,256]{3,2,1,0:T(8,128)(2,1)}, bf16[1024,4608]{1,0:T(8,128)(2,1)}, f32[1024,1024]{1,0:T(8,12...) custom-call(bf16[1024,768]{1,0:T(8,128)(2,1)} %bitcast.14, ...), custom_call_target="tpu_custom_call" | custom-call | tf_op jit(solution)/shard_map/layers/pallas_call | solution.py:1149
  138.8 157.6 %reduce.1.full = bf16[28160,256]{1,0:T(8,128)(2,1)S(1)} custom-call(bf16[21,4,256,256]{3,2,1,0:T(8,128)(2,1)} %get-tuple-element.36.left_hbm, bf16[27,4,256,256]{3,2,1,0:T(8,128)(2,1)} %get-tuple-element.37.right_hbm, f32[40,256]{1,0:T(8,128)} %get-tuple-element.38.vec_hbm), custom_call_target="tpu_custom_call" | custom-call | tf_op jit(solution)/shard_map/reduce/pallas_call | solution.py:361
  296.4 0.0 copy-start
  296.4 10.6 %widen.1 = (f32[1,768,2304]{2,1,0:T(8,128)}, f32[1,768,768]{2,1,0:T(8,128)}, f32[1,768,3072]{2,1,0:T(8,128)}, f32[1,3072,768]{2,1,0:T(8,128)}, f32[1,2304]{1,0:T...) custom-call(bf16[28160,256]{1,0:T(8,128)(2,1)S(1)} %reduce.1.full), custom_call_target="tpu_custom_call" | custom-call | tf_op jit(solution)/shard_map/widen/pallas_call | solution.py:1249
  307.0 0.0 copy-done
  307.0 1.7 copy.29
  (8 shorter events, 0.1 us)
Async XLA Ops:
  296.4 10.6 %copy-start = (f32[1024,768]{1,0:T(8,128)S(1)}, f32[1024,768]{1,0:T(8,128)}, u32[]{:S(2)}) copy-start(f32[1024,768]{1,0:T(8,128)} %get-tuple-element.35) | copy-start | bytes 9437188
